TPU v7x, 256 devices: a whole 4x4x8 slice. The times are simulated.
256 devices in a mesh: src: 64 (over x, y, z_lo, core), tgt: 4 (over z_hi).
Axes of the slice: x: 4, y: 4, z: 8 (z_hi: 4, z_lo: 2; z = z_hi * 2 + z_lo), core: 2. Of those that a mesh axis runs over, the one named last changes fastest.
Arguments:
- src_emb: bfloat16 [64, 65536], P(None, 'src'), may hold values from -6 to 6
- src_pos: float32 [2, 65536], P(None, 'src'), may hold values from 0 to 12
- src_logw: float32 [65536], P('src'), may hold values from -1 to 1
- tgt_emb: bfloat16 [64, 16384], P(None, ('src', 'tgt')), may hold values from -6 to 6
- tgt_pos: bfloat16 [2, 16384], P(None, ('src', 'tgt')), may hold values from 0 to 12
- tgt_logw: bfloat16 [16384], P(('src', 'tgt')), may hold values from -1 to 1
Outputs:
- src_potential: float32 [65536], P('src')
- tgt_potential: float32 [16384], P(('src', 'tgt'))
- feature_grad: float32 [64, 65536], P(None, 'src')
All inputs are finite; a program needn't handle non-finite values.
Results may differ from a plain program's by a relative error of at most 0.0053.
Values may be sent and summed in bfloat16 or wider, within the bound.
No kernel may reach another device: no remote copies, remote signals or barrier semaphores. Data moves between devices by JAX's collectives and lax.ppermute only.
A program may use at most 64 MiB of HBM per device.

v0:
```python
import math

import jax
import jax.numpy as jnp
from jax import lax
from jax.sharding import PartitionSpec as P

ITERS = 3


eps_reg = 0.25
rho_reg = 2.0
damping = rho_reg / (rho_reg + eps_reg)
block_width = 256


def merged(value, axis, join):
    pieces = jax.tree.map(lambda part: lax.all_gather(part, axis), value)
    head = jax.tree.map(lambda part: part[0], pieces)
    tail = jax.tree.map(lambda part: part[1:], pieces)
    so_far, _ = lax.scan(lambda so_far, piece: (join(so_far, piece), None), head, tail)
    return so_far


def pair_combine(first, second):
    top = jnp.maximum(first[0], second[0])
    total = first[1] * jnp.exp(first[0] - top) + second[1] * jnp.exp(second[0] - top)
    return (top, total)


def cost_tile(source, cols_emb, cols_geo):
    src_emb, src_sq, src_pos, src_logw = source
    inner = lax.dot_general(
        src_emb, cols_emb, (((0,), (0,)), ((), ())), preferred_element_type=jnp.float32
    )
    cols_sq = jnp.sum(jnp.square(cols_emb.astype(jnp.float32)), axis=0)
    geo_f = cols_geo.astype(jnp.float32)
    delta_x = src_pos[0][:, None] - geo_f[0][None, :]
    delta_y = src_pos[1][:, None] - geo_f[1][None, :]
    return (
        (src_sq[:, None] + cols_sq[None, :] - 2.0 * inner) / cols_emb.shape[0]
        + delta_x * delta_x
        + delta_y * delta_y
    )


def column_slab(array, begin, width):
    return lax.dynamic_slice_in_dim(array, begin, width, array.ndim - 1)


def row_fold(state, source, cols_emb, cols_geo, g_cols):
    count = cols_emb.shape[1]
    width = math.gcd(count, block_width)

    def row_advance(carry, index):
        begin = index * width
        geo_part = column_slab(cols_geo, begin, width)
        cost = cost_tile(source, column_slab(cols_emb, begin, width), geo_part)
        score = (
            geo_part[2].astype(jnp.float32)[None, :]
            + (column_slab(g_cols, begin, width)[None, :] - cost) / eps_reg
        )
        block_max = jnp.max(score, axis=1)
        block_sum = jnp.sum(jnp.exp(score - block_max[:, None]), axis=1)
        return (pair_combine(carry, (block_max, block_sum)), None)

    result, unused = lax.scan(row_advance, state, jnp.arange(count // width, dtype=jnp.int32))
    return result


def column_parts(source, potential_f, cols_emb, cols_geo):
    count = cols_emb.shape[1]
    width = math.gcd(count, block_width)
    src_logw = source[3]

    def one_block(index):
        begin = index * width
        cost = cost_tile(
            source, column_slab(cols_emb, begin, width), column_slab(cols_geo, begin, width)
        )
        score = src_logw[:, None] + (potential_f[:, None] - cost) / eps_reg
        block_max = jnp.max(score, axis=0)
        return (block_max, jnp.sum(jnp.exp(score - block_max[None, :]), axis=0))

    maxima, totals = lax.map(one_block, jnp.arange(count // width, dtype=jnp.int32))
    return (maxima.reshape(count), totals.reshape(count))


def plan_fold(state, source, potential_f, cols_emb, cols_geo, g_cols):
    count = cols_emb.shape[1]
    width = math.gcd(count, block_width)
    src_logw = source[3]

    def plan_advance(carry, index):
        begin = index * width
        emb_part = column_slab(cols_emb, begin, width)
        geo_part = column_slab(cols_geo, begin, width)
        cost = cost_tile(source, emb_part, geo_part)
        exponent = src_logw[:, None] + geo_part[2].astype(jnp.float32)[None, :]
        plan = jnp.exp(
            exponent
            + (potential_f[:, None] + column_slab(g_cols, begin, width)[None, :] - cost) / eps_reg
        )
        mass = carry[0] + jnp.sum(plan, axis=1)
        pull = carry[1] + lax.dot_general(
            emb_part,
            plan.astype(jnp.bfloat16),
            (((1,), (1,)), ((), ())),
            preferred_element_type=jnp.float32,
        )
        return ((mass, pull), None)

    result, unused = lax.scan(plan_advance, state, jnp.arange(count // width, dtype=jnp.int32))
    return result


def per_device(src_emb, src_pos, src_logw, tgt_emb, tgt_pos, tgt_logw):
    src_sq = jnp.sum(jnp.square(src_emb.astype(jnp.float32)), axis=0)
    source = (src_emb, src_sq, src_pos, src_logw)
    tgt_geo = jnp.concatenate([tgt_pos, tgt_logw[None, :]], 0)
    piece = tgt_emb.shape[1]
    groups = lax.axis_size("src")
    block = piece * groups
    rows = src_emb.shape[1]
    potential_g = jnp.zeros((block,), jnp.float32)
    potential_f = jnp.zeros((rows,), jnp.float32)
    all_emb, all_geo = (
        lax.all_gather(tgt_emb, "src", axis=1, tiled=True),
        lax.all_gather(tgt_geo, "src", axis=1, tiled=True),
    )
    for step in range(ITERS):
        start_state = (jnp.full((rows,), -jnp.inf, jnp.float32), jnp.zeros((rows,), jnp.float32))
        row_state = row_fold(start_state, source, all_emb, all_geo, potential_g)
        row_max, row_sum = merged(row_state, "tgt", pair_combine)
        potential_f = -damping * eps_reg * (row_max + jnp.log(row_sum))
        col_max, col_sum = column_parts(source, potential_f, all_emb, all_geo)
        col_max, col_sum = merged((col_max, col_sum), "src", pair_combine)
        potential_g = -damping * eps_reg * (col_max + jnp.log(col_sum))
    plan_start = (jnp.zeros((rows,), jnp.float32), jnp.zeros((src_emb.shape[0], rows), jnp.float32))
    plan_state = plan_fold(plan_start, source, potential_f, all_emb, all_geo, potential_g)
    mass, pull = lax.psum((plan_state[0], plan_state[1]), "tgt")
    feature_grad = mass[None, :] * src_emb.astype(jnp.float32) - pull
    tgt_potential = lax.dynamic_slice_in_dim(potential_g, lax.axis_index("src") * piece, piece, 0)
    return (potential_f, tgt_potential, feature_grad)


def solution(mesh):
    placed = (
        P(None, "src"),
        P(None, "src"),
        P("src"),
        P(None, ("src", "tgt")),
        P(None, ("src", "tgt")),
        P(("src", "tgt")),
    )
    return jax.shard_map(
        per_device,
        mesh=mesh,
        in_specs=placed,
        out_specs=(P("src"), P(("src", "tgt")), P(None, "src")),
        check_vma=False,
    )
```

profile of v0, /device:TPU:1, one launch (start us, length us, event | category | flops | bytes accessed | tf_op | source)
XLA Modules:
  0.0 1414.4 jit_solution(15772326837270009191)
XLA Ops:
  7.9 84.3 %all-gather.6 = bf16[64,64,3]{1,2,0:T(4,128)(2,1)S(1)} all-gather(bf16[1,64,3]{1,2,0:T(4,128)(2,1)S(1)} %maximum_bitcast_fusion), channel_id=1, replica_groups=mesh['src'=64,'tgt'=4] {'src'}, dimensions={0}, use_global_device_ids=true | all-gather | bytes 24960 | tf_op jit(solution)/shard_map/all_gather | solution.py:129
  93.2 80.7 %all_gather.61 = bf16[64,4096]{0,1:T(8,128)(2,1)S(1)} all-gather(bf16[64,64]{0,1:T(8,128)(2,1)S(1)} %copy.19), channel_id=1, replica_groups=mesh['src'=64,'tgt'=4] {'src'}, dimensions={1}, use_global_device_ids=true | all-gather | bytes 532480 | tf_op jit(solution)/shard_map/all_gather | solution.py:128
  174.5 34.6 %while.169 = (s32[]{:T(128)}, f32[1024]{0:T(1024)S(1)}, f32[1024]{0:T(1024)S(1)}, s32[16]{0:T(128)S(1)}, bf16[3,4096]{1,0:T(4,128)(2,1)S(1)}, /*index=5*/f32[102...) while((s32[]{:T(128)}, f32[1024]{0:T(1024)S(1)}, ...), condition=%wide.region_5.6_spmd.clone, body=%wide.region_1.5_spmd.clone.sunk | while | flops 37804808 | bytes 2374897 | solution.py:67
  209.2 13.6 all-gather
  223.4 10.8 all-gather.1
  236.5 39.9 %while.161 = (s32[]{:T(128)}, f32[16,256]{1,0:T(8,128)S(1)}, f32[16,256]{1,0:T(8,128)S(1)}, f32[1024]{0:T(1024)S(1)}, f32[1024]{0:T(1024)S(1)}, /*index=5*/f32[1...) while((s32[]{:T(128)}, f32[16,256]{1,0:T(8,128)S(1)}, ...), condition=%wide.region_12.13_spmd, body=%wide.region_8.12_spmd.sunk | while | flops 37797892 | bytes 2350819 | solution.py:85
  277.8 103.4 %all-gather.20.cloned.1.call-done = f32[64,1,4096]{2,1,0:T(1,128)} async-done(((f32[1,1,4096]{2,1,0:T(1,128)}), f32[64,1,4096]{2,1,0:T(1,128)}) %all-gather.20.cloned.1.call-update) | async-done | bytes 1048592 | tf_op jit(solution)/shard_map/all_gather | solution.py:18
  381.2 1.2 slice-done
  383.0 102.7 %all-gather.22.cloned.1.call-done = f32[64,1,4096]{2,1,0:T(1,128)} async-done(((f32[1,1,4096]{2,1,0:T(1,128)}), f32[64,1,4096]{2,1,0:T(1,128)}) %all-gather.22.cloned.1.call-update) | async-done | bytes 1048592 | tf_op jit(solution)/shard_map/all_gather | solution.py:18
  485.7 1.2 slice-done.2
  487.0 1.6 copy.43
  489.3 61.6 %while.162 = (s32[]{:T(128)}, f32[4096]{0:T(1024)S(1)}, f32[4096]{0:T(1024)S(1)}, f32[63,4096]{1,0:T(8,128)S(1)}, f32[63,4096]{1,0:T(8,128)}, /*index=5*/s32[]{:T(128)}) while((s32[]{:T(128)}, f32[4096]{0:T(1024)S(1)}, f32[4096]{0:T(1024)S(1)}, f32[63,4096]{1,0:T(8,128)S(1)}, f32[63,4096]{1,0:T(8,128)}, /*index=5*/s32[]{:T(128)}) %tuple.392), condition=%wide.region_14.15_spmd, body=%wide.region_13.14_spmd.sunk | while | flops 24578 | bytes 163921 | solution.py:21
  550.9 37.9 %while.170 = (s32[]{:T(128)}, f32[1024]{0:T(1024)S(1)}, f32[1024]{0:T(1024)S(1)}, s32[16]{0:T(128)S(1)}, bf16[3,4096]{1,0:T(4,128)(2,1)S(1)}, /*index=5*/f32[409...) while((s32[]{:T(128)}, f32[1024]{0:T(1024)S(1)}, ...), condition=%wide.region_19.20_spmd.clone, body=%wide.region_15.19_spmd.clone.sunk | while | flops 37804808 | bytes 2377981 | solution.py:67
  588.8 12.3 all-gather.2
  601.7 10.8 all-gather.3
  614.2 39.9 %while.164 = (s32[]{:T(128)}, f32[16,256]{1,0:T(8,128)S(1)}, f32[16,256]{1,0:T(8,128)S(1)}, f32[1024]{0:T(1024)S(1)}, f32[1024]{0:T(1024)S(1)}, /*index=5*/f32[1...) while((s32[]{:T(128)}, f32[16,256]{1,0:T(8,128)S(1)}, ...), condition=%wide.region_26.27_spmd, body=%wide.region_22.26_spmd.sunk | while | flops 37797892 | bytes 2350819 | solution.py:85
  655.5 106.3 %all-gather.24.cloned.1.call-done = f32[64,1,4096]{2,1,0:T(1,128)} async-done(((f32[1,1,4096]{2,1,0:T(1,128)}), f32[64,1,4096]{2,1,0:T(1,128)}) %all-gather.24.cloned.1.call-update) | async-done | bytes 1048592 | tf_op jit(solution)/shard_map/all_gather | solution.py:18
  761.8 1.2 slice-done.4
  763.6 102.6 %all-gather.26.cloned.1.call-done = f32[64,1,4096]{2,1,0:T(1,128)} async-done(((f32[1,1,4096]{2,1,0:T(1,128)}), f32[64,1,4096]{2,1,0:T(1,128)}) %all-gather.26.cloned.1.call-update) | async-done | bytes 1048592 | tf_op jit(solution)/shard_map/all_gather | solution.py:18
  866.2 1.2 slice-done.6
  867.4 1.6 copy.41
  869.8 61.6 %while.165 = (s32[]{:T(128)}, f32[4096]{0:T(1024)S(1)}, f32[4096]{0:T(1024)S(1)}, f32[63,4096]{1,0:T(8,128)S(1)}, f32[63,4096]{1,0:T(8,128)}, /*index=5*/s32[]{:T(128)}) while((s32[]{:T(128)}, f32[4096]{0:T(1024)S(1)}, f32[4096]{0:T(1024)S(1)}, f32[63,4096]{1,0:T(8,128)S(1)}, f32[63,4096]{1,0:T(8,128)}, /*index=5*/s32[]{:T(128)}) %tuple.393), condition=%wide.region_28.29_spmd, body=%wide.region_27.28_spmd.sunk | while | flops 24578 | bytes 163921 | solution.py:21
  931.4 37.9 %while.171 = (s32[]{:T(128)}, f32[1024]{0:T(1024)S(1)}, f32[1024]{0:T(1024)S(1)}, s32[16]{0:T(128)S(1)}, bf16[3,4096]{1,0:T(4,128)(2,1)S(1)}, /*index=5*/f32[409...) while((s32[]{:T(128)}, f32[1024]{0:T(1024)S(1)}, ...), condition=%wide.region_33.34_spmd.clone, body=%wide.region_29.33_spmd.clone.sunk | while | flops 37804808 | bytes 2377981 | solution.py:67
  969.3 12.3 all-gather.4
  982.2 11.0 all-gather.5
  994.8 39.9 %while.167 = (s32[]{:T(128)}, f32[16,256]{1,0:T(8,128)S(1)}, f32[16,256]{1,0:T(8,128)S(1)}, f32[1024]{0:T(1024)S(1)}, f32[1024]{0:T(1024)S(1)}, /*index=5*/f32[1...) while((s32[]{:T(128)}, f32[16,256]{1,0:T(8,128)S(1)}, ...), condition=%wide.region_40.41_spmd, body=%wide.region_36.40_spmd.sunk | while | flops 37797892 | bytes 2350819 | solution.py:85
  1036.1 106.4 %all-gather.28.cloned.1.call-done = f32[64,1,4096]{2,1,0:T(1,128)} async-done(((f32[1,1,4096]{2,1,0:T(1,128)}), f32[64,1,4096]{2,1,0:T(1,128)}) %all-gather.28.cloned.1.call-update) | async-done | bytes 1048592 | tf_op jit(solution)/shard_map/all_gather | solution.py:18
  1142.5 1.2 slice-done.8
  1143.7 1.6 copy.40
  1145.3 101.6 %all-gather.30.cloned.1.call-done = f32[64,1,4096]{2,1,0:T(1,128)} async-done(((f32[1,1,4096]{2,1,0:T(1,128)}), f32[64,1,4096]{2,1,0:T(1,128)}) %all-gather.30.cloned.1.call-update) | async-done | bytes 1048592 | tf_op jit(solution)/shard_map/all_gather | solution.py:18
  1246.9 1.2 slice-done.10
  1248.1 1.6 copy.39
  1250.4 65.6 %while.168 = (s32[]{:T(128)}, f32[4096]{0:T(1024)S(1)}, f32[4096]{0:T(1024)S(1)}, f32[63,4096]{1,0:T(8,128)}, f32[63,4096]{1,0:T(8,128)}, /*index=5*/s32[]{:T(128)}) while((s32[]{:T(128)}, f32[4096]{0:T(1024)S(1)}, f32[4096]{0:T(1024)S(1)}, f32[63,4096]{1,0:T(8,128)}, f32[63,4096]{1,0:T(8,128)}, /*index=5*/s32[]{:T(128)}) %tuple.394), condition=%wide.region_42.43_spmd, body=%wide.region_41.42_spmd.sunk | while | flops 24578 | bytes 163921 | solution.py:21
  1252.5 1.0 constant_dynamic-slice_fusion.23
  1254.5 1.0 constant_dynamic-slice_fusion.23
  1255.6 1.0 constant_dynamic-slice_fusion.23
  1257.7 1.0 constant_dynamic-slice_fusion.23
  1260.8 1.0 constant_dynamic-slice_fusion.23
  1263.9 1.0 constant_dynamic-slice_fusion.23
  1266.0 1.0 constant_dynamic-slice_fusion.23
  1269.1 1.0 constant_dynamic-slice_fusion.23
  1272.2 1.0 constant_dynamic-slice_fusion.23
  1274.3 1.0 constant_dynamic-slice_fusion.23
  1275.4 1.0 constant_dynamic-slice_fusion.23
  1277.4 1.0 constant_dynamic-slice_fusion.23
  1280.6 1.0 constant_dynamic-slice_fusion.23
  1283.7 1.0 constant_dynamic-slice_fusion.23
  1285.8 1.0 constant_dynamic-slice_fusion.23
  1288.9 1.0 constant_dynamic-slice_fusion.23
  1292.0 1.0 constant_dynamic-slice_fusion.23
  1294.1 1.0 constant_dynamic-slice_fusion.23
  1295.1 1.0 constant_dynamic-slice_fusion.23
  1297.2 1.0 constant_dynamic-slice_fusion.23
  1300.3 1.0 constant_dynamic-slice_fusion.23
  1303.5 1.0 constant_dynamic-slice_fusion.23
  1305.5 1.0 constant_dynamic-slice_fusion.23
  1308.7 1.0 constant_dynamic-slice_fusion.23
  1311.8 1.0 constant_dynamic-slice_fusion.23
  1313.9 1.0 constant_dynamic-slice_fusion.23
  1314.9 1.0 constant_dynamic-slice_fusion.23
  1316.0 41.6 %while.172 = (s32[]{:T(128)}, f32[1024]{0:T(1024)S(1)}, f32[64,1024]{1,0:T(8,128)S(1)}, f32[1024]{0:T(1024)S(1)}, s32[16]{0:T(128)S(1)}, /*index=5*/bf16[3,4096]...) while((s32[]{:T(128)}, f32[1024]{0:T(1024)S(1)}, ...), condition=%wide.region_46.47_spmd.clone, body=%wide.region_43.46_spmd.clone.sunk | while | flops 71747336 | bytes 1874194 | solution.py:113
  1358.9 10.0 psum.14
  1368.9 37.0 %all-reduce.2.cloned.1.call-done = f32[64,1024]{1,0:T(8,128)} async-done(((f32[64,1024]{1,0:T(8,128)}), f32[64,1024]{1,0:T(8,128)}) %all-reduce.2.cloned.1.call-update) | async-done | bytes 262160 | tf_op jit(solution)/shard_map/psum | solution.py:141
  1405.9 1.7 fusion.78
  (1548 shorter events, 369.6 us)
Async XLA Ops:
  7.2 374.0 %all-gather.20.cloned.1.call-start = ((), (), s32[]{:S(2)}) async-start(), calls=%async_computation.1 | async-start | bytes 1064960 | tf_op jit(solution)/shard_map/all_gather | solution.py:18
  7.2 0.7 copy-start.8
  7.2 0.7 copy-start.9
  7.9 84.4 %copy-start.2 = (bf16[64,1024]{1,0:T(8,128)(2,1)S(1)}, bf16[64,1024]{1,0:T(8,128)(2,1)}, u32[]{:S(2)}) copy-start(bf16[64,1024]{1,0:T(8,128)(2,1)} %param.32) | copy-start | bytes 393220
  92.3 0.7 copy-start.6
  173.8 0.7 copy-start
  222.8 0.6 copy-start.3
  234.2 0.7 slice-start.13
  234.9 0.7 slice-start.12
  235.8 0.7 copy-start.10
  277.0 208.7 %all-gather.22.cloned.1.call-start = ((), (), s32[]{:S(2)}) async-start(), calls=%async_computation.2 | async-start | bytes 1064960 | tf_op jit(solution)/shard_map/all_gather | solution.py:18
  277.7 484.1 %all-gather.24.cloned.1.call-start = ((), (), s32[]{:S(2)}) async-start(), calls=%async_computation.3 | async-start | bytes 1064960 | tf_op jit(solution)/shard_map/all_gather | solution.py:18
  381.2 1.2 slice-start
  485.7 1.2 slice-start.2
  488.6 0.7 slice-start.1
  488.6 0.7 slice-start.3
  601.1 0.6 copy-start.4
  612.6 0.7 slice-start.15
  613.3 0.7 slice-start.14
  654.7 211.5 %all-gather.26.cloned.1.call-start = ((), (), s32[]{:S(2)}) async-start(), calls=%async_computation.4 | async-start | bytes 1064960 | tf_op jit(solution)/shard_map/all_gather | solution.py:18
  655.4 487.0 %all-gather.28.cloned.1.call-start = ((), (), s32[]{:S(2)}) async-start(), calls=%async_computation.5 | async-start | bytes 1064960 | tf_op jit(solution)/shard_map/all_gather | solution.py:18
  761.8 1.2 slice-start.4
  866.2 1.2 slice-start.6
  869.0 0.7 slice-start.5
  869.0 0.7 slice-start.7
  981.6 0.6 copy-start.5
  993.2 0.7 slice-start.17
  993.9 0.7 slice-start.16
  1035.4 211.5 %all-gather.30.cloned.1.call-start = ((), (), s32[]{:S(2)}) async-start(), calls=%async_computation.6 | async-start | bytes 1064960 | tf_op jit(solution)/shard_map/all_gather | solution.py:18
  1036.0 369.9 %all-reduce.2.cloned.1.call-start = ((), (), s32[]{:S(2)}) async-start(), calls=%async_computation | async-start | bytes 524288 | tf_op jit(solution)/shard_map/psum | solution.py:141
  1142.5 1.2 slice-start.8
  1246.8 1.2 slice-start.10
  1249.6 0.7 slice-start.9
  1249.6 0.7 slice-start.11
  1357.6 0.7 copy-start.1
  1357.6 0.7 copy-start.7
Sparse Core Ops, SparseCore 0:
  277.1 104.0 all-gather.19
  383.1 102.6 all-gather.21
  654.9 106.9 all-gather.23
  763.5 102.6 all-gather.25
  1035.5 106.9 all-gather.27
  1144.2 102.6 all-gather.29
  1358.4 47.4 all-reduce.1
where the time goes:
time: 1420 us; the launch traced here: 1410 us
  waiting for transfers between devices  660 us (46%)
  local copies, waits for them, and re-layouts  286 us (20%)
  blocking collectives  246 us (17%)
  matrix products  85.9 us (6%)
  loops' own time  82.6 us (6%)
  other arithmetic  39.2 us (3%)
  between operations  14.6 us (1%)
    all_gather x6, waiting for transfers between devices, merged(): pieces = jax.tree.map(lambda part: lax.all_gather(part, axis), value)  623 us
    dynamic_slice x198, local copies, waits for them, and re-layouts, merged(): lax.scan(lambda so_far, piece: (join(so_far, piece), None), head, tail)  181 us
    all_gather x1, blocking collectives, per_device(): lax.all_gather(tgt_geo, 'src', axis=1, tiled=True)  84.3 us
    dot_general x112, matrix products, cost_tile(): lax.dot_general(src_emb, cols_emb, (((0,), (0,)), ((), ())), preferred_el...  82.1 us
    all_gather x1, blocking collectives, per_device(): lax.all_gather(tgt_emb, 'src', axis=1, tiled=True)  80.7 us
    all_gather x6, blocking collectives, merged(): pieces = jax.tree.map(lambda part: lax.all_gather(part, axis), value)  70.8 us
    dynamic_slice x112, local copies, waits for them, and re-layouts, row_fold(): lax.scan(row_advance, state, jnp.arange(count // width, dtype=jnp.int32))  65.2 us
    psum x1, waiting for transfers between devices, per_device(): mass, pull = lax.psum((plan_state[0], plan_state[1]), 'tgt')  37 us
  transfers between devices with their start and end apart: 7, of which 7 were waited for; matrix products, arithmetic and copies ran while one was open for 0% of the time, Pallas kernels for 0%

commit v1 on v0

v1 whole, which is shorter than its diff:
```python
import functools

import jax
import jax.numpy as jnp
from jax import lax
from jax.experimental import pallas as pl
from jax.experimental.pallas import tpu as pltpu
from jax.sharding import PartitionSpec as P

ITERS = 3
EPS = 0.25
RHO = 2.0
LAM = RHO / (RHO + EPS)
EMB = 64
DEPTH = 128
PACK = 80
MIB = 1 << 20
LOW, HIGH = 1e-25, 1e30


def pieces(value):
    high = value.astype(jnp.bfloat16).astype(jnp.float32)
    rest = value - high
    mid = rest.astype(jnp.bfloat16).astype(jnp.float32)
    low = (rest - mid).astype(jnp.bfloat16).astype(jnp.float32)
    return high, mid, low


def stacked(rows, height, width):
    index = lax.broadcasted_iota(jnp.int32, (height, width), 0)
    block = jnp.zeros((height, width), jnp.float32)
    for at, row in enumerate(rows):
        if row is not None:
            block = jnp.where(index == at, row, block)
    return block


def source_static(emb_ref, pos_ref, out_ref):
    width = emb_ref.shape[1]
    pos = pos_ref[...]
    emb = emb_ref[...].astype(jnp.float32)
    sq = jnp.sum(emb * emb, axis=0, keepdims=True)
    shift = -(sq * (1.0 / EMB) + pos[0:1] * pos[0:1] + pos[1:2] * pos[1:2]) * (1.0 / EPS)
    pos = pos * (2.0 / EPS)
    zero, one = jnp.zeros((1, width), jnp.float32), jnp.ones((1, width), jnp.float32)
    rows = [*pieces(pos[0:1]), *pieces(pos[1:2]), zero, zero, zero, one, one, one]
    extra = stacked(rows, 16, width)
    emb = emb * (2.0 / (EMB * EPS))
    pad = jnp.zeros((DEPTH - PACK, 128), jnp.float32)
    for at in range(0, width, 128):
        block = jnp.concatenate([emb[:, at : at + 128], extra[:, at : at + 128], pad], axis=0)
        out_ref[at : at + 128, :] = block.T.astype(jnp.bfloat16)
    return shift


def target_static(pack_ref, at, out_ref):
    width = pack_ref.shape[1]
    pack = pack_ref[...].astype(jnp.float32)
    emb, geo = pack[0:EMB], pack[EMB : EMB + 4]
    sq = jnp.sum(emb * emb, axis=0, keepdims=True)
    x, y = geo[0:1], geo[1:2]
    shift = -(sq * (1.0 / EMB) + x * x + y * y) * (1.0 / EPS)
    one = jnp.ones((1, width), jnp.float32)
    cut = slice(at, at + width)
    out_ref[0:EMB, cut] = pack_ref[0:EMB, :]
    out_ref[EMB:PACK, cut] = stacked([x, x, x, y, y, y, one, one, one], 16, width).astype(jnp.bfloat16)
    out_ref[PACK:DEPTH, cut] = jnp.zeros((DEPTH - PACK, width), jnp.bfloat16)
    return shift, geo[2:3]


def set_source(a_ref, shift, a_s):
    block = stacked([None] * 6 + [*pieces(shift)], 16, a_ref.shape[0])
    above = jnp.zeros((EMB, 128), jnp.float32)
    below = jnp.zeros((DEPTH - PACK, 128), jnp.float32)
    for at in range(0, a_ref.shape[0], 128):
        part = jnp.concatenate([above, block[:, at : at + 128], below], axis=0).T
        a_s[at : at + 128, :] = a_ref[at : at + 128, :] + part.astype(jnp.bfloat16)


def set_target(b_ref, shift, b_s):
    block = stacked([None] * 9 + [*pieces(shift)], 16, b_ref.shape[1])
    b_s[EMB:PACK, :] = (b_ref[EMB:PACK, :].astype(jnp.float32) + block).astype(jnp.bfloat16)


def copy_target(b_ref, b_s):
    b_s[0:EMB, :] = b_ref[0:EMB, :]
    b_s[PACK:DEPTH, :] = b_ref[PACK:DEPTH, :]


def score(a, b):
    return lax.dot_general(a, b, (((1,), (0,)), ((), ())), preferred_element_type=jnp.float32)


def row_sums(a_s, b_s, acc_s, tile):
    acc_s[...] = jnp.zeros_like(acc_s)

    def step(index, carry):
        cut = pl.ds(pl.multiple_of(index * tile, tile), tile)
        value = jnp.exp(score(a_s[...], b_s[:, cut]))
        part = value[:, 0:128]
        for col in range(128, tile, 128):
            part += value[:, col : col + 128]
        acc_s[...] += part
        return carry

    lax.fori_loop(0, b_s.shape[1] // tile, step, 0)


def row_tops(a_s, b_s, acc_s, tile, count):
    acc_s[...] = jnp.full(acc_s.shape, -jnp.inf, jnp.float32)

    def step(index, carry):
        cut = pl.ds(pl.multiple_of(index * tile, tile), tile)
        value = score(a_s[...], b_s[:, cut])
        part = value[:, 0:128]
        for col in range(128, tile, 128):
            part = jnp.maximum(part, value[:, col : col + 128])
        acc_s[...] = jnp.maximum(acc_s[...], part)
        return carry

    lax.fori_loop(0, count, step, 0)


def over_lanes(acc_s, out_s, join):
    for at in range(0, acc_s.shape[0], 128):
        out_s[:, at : at + 128] = join(acc_s[at : at + 128, :].T, axis=0, keepdims=True)


def in_range(total):
    return jnp.logical_and(jnp.min(total) > LOW, jnp.max(total) < HIGH)


def row_pass(a_ref, b_ref, r_ref, c, guess_ref, out_ref, a_s, b_s, acc_s, guess_s, total_s, tile):
    cols = b_ref.shape[1]
    copy_target(b_ref, b_s)
    set_target(b_ref, c, b_s)

    def about_tops(count):
        set_source(a_ref, r_ref[...], a_s)
        row_tops(a_s, b_s, acc_s, tile, count)
        over_lanes(acc_s, guess_s, jnp.max)

    def sums():
        set_source(a_ref, r_ref[...] - guess_s[...], a_s)
        row_sums(a_s, b_s, acc_s, tile)
        over_lanes(acc_s, total_s, jnp.sum)

    if guess_ref is None:
        about_tops(1)
    else:
        guess_s[...] = guess_ref[...]
    sums()

    @pl.when(jnp.logical_not(in_range(total_s[...])))
    def _():
        about_tops(cols // tile)
        sums()

    out_ref[...] = guess_s[...] + jnp.log(total_s[...])


def first_kernel(emb_ref, pos_ref, own_ref, other_ref, out_ref, a_ref, b_ref, r_ref, c_ref, w_ref, a_s, b_s, acc_s, guess_s, total_s, *, tile):
    half = own_ref.shape[1]
    r_ref[...] = source_static(emb_ref, pos_ref, a_ref)
    c_ref[:, 0:half], w_ref[:, 0:half] = target_static(own_ref, 0, b_ref)
    c_ref[:, half:], w_ref[:, half:] = target_static(other_ref, half, b_ref)
    row_pass(a_ref, b_ref, r_ref, c_ref[...] + w_ref[...], None, out_ref, a_s, b_s, acc_s, guess_s, total_s, tile)


def target_shift(c_ref, w_ref, own_ref, other_ref):
    lse = jnp.concatenate([own_ref[...], other_ref[...]], axis=1)
    return c_ref[...] + w_ref[...] - LAM * lse


def row_kernel(a_ref, b_ref, r_ref, c_ref, w_ref, own_ref, other_ref, guess_ref, out_ref, a_s, b_s, acc_s, guess_s, total_s, *, tile):
    c = target_shift(c_ref, w_ref, own_ref, other_ref)
    row_pass(a_ref, b_ref, r_ref, c, guess_ref, out_ref, a_s, b_s, acc_s, guess_s, total_s, tile)


def joined(first, second):
    top = jnp.maximum(first, second)
    return top + jnp.log(jnp.exp(first - top) + jnp.exp(second - top))


def col_kernel(a_ref, b_ref, r_ref, c_ref, logw_ref, one_ref, two_ref, *refs, tile, first):
    if first:
        own_ref, other_ref, f_ref, a_s, b_s, guess_s, total_s = refs
    else:
        last_own_ref, last_other_ref, own_ref, other_ref, f_ref, a_s, b_s, guess_s, total_s = refs
    cols = b_ref.shape[1]
    lse = joined(one_ref[...], two_ref[...])
    f_ref[...] = -LAM * EPS * lse
    set_source(a_ref, r_ref[...] + logw_ref[...] - LAM * lse, a_s)
    copy_target(b_ref, b_s)

    def over_tiles(work):
        def step(index, carry):
            cut = pl.ds(pl.multiple_of(index * tile, tile), tile)
            work(cut, score(a_s[...], b_s[:, cut]))
            return carry

        lax.fori_loop(0, cols // tile, step, 0)

    def about_tops():
        def top(cut, value):
            guess_s[:, cut] = jnp.max(value, axis=0, keepdims=True)

        set_target(b_ref, c_ref[...], b_s)
        over_tiles(top)

    def sums():
        def total(cut, value):
            total_s[:, cut] = jnp.sum(jnp.exp(value), axis=0, keepdims=True)

        set_target(b_ref, c_ref[...] - guess_s[...], b_s)
        over_tiles(total)

    if first:
        about_tops()
        sums()
    else:
        guess_s[...] = jnp.concatenate([last_own_ref[...], last_other_ref[...]], axis=1)
        sums()

        @pl.when(jnp.logical_not(in_range(total_s[...])))
        def _():
            about_tops()
            sums()

    result = guess_s[...] + jnp.log(total_s[...])
    own_ref[...] = result[:, 0 : cols // 2]
    other_ref[...] = result[:, cols // 2 :]


def plan_kernel(emb_ref, a_ref, b_ref, r_ref, c_ref, w_ref, logw_ref, f_ref, own_ref, other_ref, out_ref, a_s, b_s, mass_s, pull_s, *, tile):
    rows, cols = emb_ref.shape[1], b_ref.shape[1]
    set_source(a_ref, r_ref[...] + logw_ref[...] + f_ref[...] * (1.0 / EPS), a_s)
    copy_target(b_ref, b_s)
    set_target(b_ref, target_shift(c_ref, w_ref, own_ref, other_ref), b_s)
    mass_s[...] = jnp.zeros_like(mass_s)
    pull_s[...] = jnp.zeros_like(pull_s)

    def step(index, carry):
        cut = pl.ds(pl.multiple_of(index * tile, tile), tile)
        plan = jnp.exp(score(a_s[...], b_s[:, cut]))
        mass = plan[:, 0:128]
        for col in range(128, tile, 128):
            mass += plan[:, col : col + 128]
        mass_s[...] += mass
        pull_s[...] += lax.dot_general(
            plan.astype(jnp.bfloat16),
            b_ref[0:EMB, cut],
            (((1,), (1,)), ((), ())),
            preferred_element_type=jnp.float32,
        )
        return carry

    lax.fori_loop(0, cols // tile, step, 0)
    for at in range(0, rows, 128):
        mass = jnp.sum(mass_s[at : at + 128, :].T, axis=0, keepdims=True)
        pull = jnp.concatenate([pull_s[at : at + 128, :], jnp.zeros((128, 128 - EMB), jnp.float32)], axis=1).T
        grad = mass * emb_ref[:, at : at + 128].astype(jnp.float32) - pull[0:EMB, :]
        out_ref[:, at : at + 128] = grad.astype(out_ref.dtype)


def params(mib):
    return pltpu.CompilerParams(vmem_limit_bytes=mib * MIB)


TILE = 1024


def line(width):
    return jax.ShapeDtypeStruct((1, width), jnp.float32)


def operands(rows, cols):
    return [pltpu.VMEM((rows, DEPTH), jnp.bfloat16), pltpu.VMEM((DEPTH, cols), jnp.bfloat16)]


def row_scratch(rows, cols):
    return operands(rows, cols) + [
        pltpu.VMEM((rows, 128), jnp.float32),
        pltpu.VMEM((1, rows), jnp.float32),
        pltpu.VMEM((1, rows), jnp.float32),
    ]


def first_call(src_emb, src_pos, own, other):
    rows, cols = src_emb.shape[1], 2 * own.shape[1]
    return pl.pallas_call(
        functools.partial(first_kernel, tile=min(TILE, cols)),
        out_shape=(
            line(rows),
            jax.ShapeDtypeStruct((rows, DEPTH), jnp.bfloat16),
            jax.ShapeDtypeStruct((DEPTH, cols), jnp.bfloat16),
            line(rows),
            line(cols),
            line(cols),
        ),
        scratch_shapes=row_scratch(rows, cols),
        compiler_params=params(32),
        name="first_row_lse",
    )(src_emb, src_pos, own, other)


def row_call(a, b, r, c, w, parts, guess):
    rows, cols = a.shape[0], b.shape[1]
    return pl.pallas_call(
        functools.partial(row_kernel, tile=min(TILE, cols)),
        out_shape=line(rows),
        scratch_shapes=row_scratch(rows, cols),
        compiler_params=params(32),
        name="row_lse",
    )(a, b, r, c, w, *parts, guess)


def col_call(a, b, r, c, logw, parts, last):
    rows, cols = a.shape[0], b.shape[1]
    return pl.pallas_call(
        functools.partial(col_kernel, tile=min(TILE, cols), first=not last),
        out_shape=(line(cols // 2), line(cols // 2), line(rows)),
        scratch_shapes=operands(rows, cols) + [pltpu.VMEM((1, cols), jnp.float32), pltpu.VMEM((1, cols), jnp.float32)],
        compiler_params=params(32),
        name="col_lse",
    )(a, b, r, c, logw, *parts, *last)


def plan_call(src_emb, a, b, r, c, w, logw, f, parts):
    rows, cols = a.shape[0], b.shape[1]
    return pl.pallas_call(
        functools.partial(plan_kernel, tile=min(TILE, cols)),
        out_shape=jax.ShapeDtypeStruct((EMB, rows), jnp.bfloat16),
        scratch_shapes=operands(rows, cols) + [pltpu.VMEM((rows, 128), jnp.float32), pltpu.VMEM((rows, EMB), jnp.float32)],
        compiler_params=params(32),
        name="plan_grad",
    )(src_emb, a, b, r, c, w, logw, f, *parts)


def rounded_sum(first, second):
    total = first.astype(jnp.float32) + second.astype(jnp.float32)
    return lax.reduce_precision(total, 8, 7).astype(jnp.bfloat16)


def swapped(value, axis, mask):
    return lax.ppermute(value, axis, [(k, k ^ mask) for k in range(lax.axis_size(axis))])


def exchanged(value, join):
    value = join(value, swapped(value, "tgt", 1))
    return value, swapped(value, "tgt", 3)


def spread(block):
    size = lax.axis_size("src")
    groups = [list(range(core, size, 2)) for core in range(2)]
    block = jnp.broadcast_to(block, (size // 2,) + block.shape)
    return lax.all_to_all(block, "src", 0, 0, axis_index_groups=groups, tiled=True)


def per_device(src_emb, src_pos, src_logw, tgt_emb, tgt_pos, tgt_logw):
    piece = tgt_emb.shape[1]
    half = piece * (lax.axis_size("src") // 2)
    logw = src_logw[None, :]

    count = EMB + 4
    own = jnp.concatenate([tgt_emb, tgt_pos, tgt_logw[None, :], tgt_logw[None, :]], 0).reshape(count * piece // 128, 128)
    own = spread(own).reshape(-1, count, piece).transpose(1, 0, 2).reshape(count, half)
    lse, a, b, r, c, w = first_call(src_emb, src_pos, own, swapped(own, "src", 1))

    last = ()
    for step in range(ITERS):
        if step:
            lse = row_call(a, b, r, c, w, parts, lse)
        mine, theirs, f = col_call(a, b, r, c, logw, exchanged(lse, joined), last)
        last = (mine, theirs)
        col = spread(joined(mine, swapped(theirs, "src", 1)).reshape(half // 128, 128))
        top = jnp.max(col, axis=0)
        col = (top + jnp.log(jnp.sum(jnp.exp(col - top), axis=0))).reshape(1, half)
        parts = (col, swapped(col, "src", 1))
    begin = lax.axis_index("src") // 2 * piece
    g_own = -LAM * EPS * lax.dynamic_slice_in_dim(col[0], begin, piece, 0)
    grad = plan_call(src_emb, a, b, r, c, w, logw, f, parts)
    first, second = exchanged(grad, rounded_sum)
    return f[0], g_own, first.astype(jnp.float32) + second.astype(jnp.float32)


def solution(mesh):
    placed = (
        P(None, "src"),
        P(None, "src"),
        P("src"),
        P(None, ("src", "tgt")),
        P(None, ("src", "tgt")),
        P(("src", "tgt")),
    )
    return jax.shard_map(
        per_device,
        mesh=mesh,
        in_specs=placed,
        out_specs=(P("src"), P(("src", "tgt")), P(None, "src")),
        check_vma=False,
    )
```

time: 1420 us -> 154 us (0.11)
  waiting for transfers between devices: 660 us -> 25.1 us
  local copies, waits for them, and re-layouts: 286 us -> 2.44 us
  blocking collectives: 246 us -> 54.1 us
  matrix products: 85.9 us -> 0 us
  loops' own time: 82.6 us -> 0 us
  starting transfers between devices: 0.29 us -> 37 us
  other arithmetic: 39.2 us -> 2.6 us
  Pallas kernels: 0 us -> 31 us
    all_gather x6 -> x0, waiting for transfers between devices: 623 us -> none  [merged(): pieces = jax.tree.map(lambda part: lax.all_gather(part, axis), value)]
    dynamic_slice x359 -> x0, local copies, waits for them, and re-layouts: 250 us -> none  [the longest x198 181 us: merged(): lax.scan(lambda so_far, piece: (join(so_far, piece), None), head, tail)]
    all_gather x8 -> x0, blocking collectives: 236 us -> none  [the longest x1 84.3 us: per_device(): lax.all_gather(tgt_geo, 'src', axis=1, tiled=True)]
    dot_general x128 -> x0, matrix products: 85.9 us -> none  [the longest x112 82.1 us: cost_tile(): lax.dot_general(src_emb, cols_emb, (((0,), (0,)), ((), ())), preferred_el...]
    another operation x13 -> x0, loops' own time: 82.6 us -> none  [the longest x3 34 us: column_parts(): lax.map(one_block, jnp.arange(count // width, dtype=jnp.int32))]
    all_to_all x0 -> x4, blocking collectives: none -> 54.1 us  [spread(): lax.all_to_all(block, 'src', 0, 0, axis_index_groups=groups, tiled=True)]
    ppermute x0 -> x15, starting transfers between devices: none -> 37 us  [swapped(): lax.ppermute(value, axis, [(k, k ^ mask) for k in range(lax.axis_size(axi...]
    psum x1 -> x0, waiting for transfers between devices: 37 us -> none  [per_device(): mass, pull = lax.psum((plan_state[0], plan_state[1]), 'tgt')]
  transfers between devices with their start and end apart: 7 -> 15, of which waited for: 7 -> 15; matrix products, arithmetic and copies ran while one was open for 0% -> 0% of each run, Pallas kernels for 0% -> 0%
where the time goes in v1:
time: 154 us; the launch traced here: 153 us
  blocking collectives  54.1 us (35%)
  starting transfers between devices  37 us (24%)
  Pallas kernels  31 us (20%)
  waiting for transfers between devices  25.1 us (16%)
  other arithmetic  2.6 us (2%)
  local copies, waits for them, and re-layouts  2.44 us (2%)
    all_to_all x4, blocking collectives, spread(): lax.all_to_all(block, 'src', 0, 0, axis_index_groups=groups, tiled=True)  54.1 us
    ppermute x15, starting transfers between devices, swapped(): lax.ppermute(value, axis, [(k, k ^ mask) for k in range(lax.axis_size(axi...  37 us
    ppermute x15, waiting for transfers between devices, swapped(): lax.ppermute(value, axis, [(k, k ^ mask) for k in range(lax.axis_size(axi...  25.1 us
    pallas_call x3, Pallas kernels, col_call(): pl.pallas_call(functools.partial(col_kernel, tile=min(TILE, cols), first=...  14 us
    pallas_call x2, Pallas kernels, row_call(): pl.pallas_call(functools.partial(row_kernel, tile=min(TILE, cols)), out_s...  7.02 us
    pallas_call x1, Pallas kernels, plan_call(): pl.pallas_call(functools.partial(plan_kernel, tile=min(TILE, cols)), out_...  5.59 us
    pallas_call x1, Pallas kernels, first_call(): pl.pallas_call(functools.partial(first_kernel, tile=min(TILE, cols)), out...  4.48 us
  transfers between devices with their start and end apart: 15, of which 15 were waited for; matrix products, arithmetic and copies ran while one was open for 0% of the time, Pallas kernels for 0%

profile of v1, /device:TPU:1, one launch (start us, length us, event | category | flops | bytes accessed | tf_op | source)
XLA Modules:
  0.0 153.2 jit_solution(16193386325130866411)
XLA Ops:
  0.6 0.0 copy-start.4
  0.6 0.0 copy-start.5
  0.7 0.6 copy-done.4
  1.3 0.0 copy-done.5
  1.3 0.7 pad_maximum_fusion
  2.0 0.1 reshape.100
  2.2 18.2 %all_to_all.20 = bf16[32,34,128]{2,1,0:T(8,128)(2,1)S(1)} all-to-all(bf16[32,34,128]{2,1,0:T(8,128)(2,1)S(1)} %broadcast_in_dim.23), channel_id=1, replica_groups={{0,8,16,24,32,40,48,56,64,72,80,88,96,104,112,120,128,136,144,152,160,1..., dimensions={0} | all-to-all | bytes 557056 | tf_op jit(solution)/shard_map/all_to_all | solution.py:358
  20.4 0.4 reshape.101
  20.8 0.1 copy.10
  20.9 0.0 copy-start
  20.9 0.0 copy-start.2
  20.9 0.4 reshape.102.own_ref
  21.3 2.0 %collective-permute-start = (bf16[68,2048]{1,0:T(8,128)(2,1)S(1)}, bf16[68,2048]{1,0:T(8,128)(2,1)S(1)}, u32[]{:S(2)}, u32[]{:S(2)}) collective-permute-start(bf16[68,2048]{1,0:T(8,128)(2,1)S(1)} %reshape.102.own_ref), channel_id=1, source_target_pairs={{0,4},{4,0},{8,12},{12,8},{16,20},{20,16},{24,28},{28,24},{32,36},... | collective-permute-start | bytes 835592 | tf_op jit(solution)/shard_map/ppermute | solution.py:346
  23.4 1.2 collective-permute-done.other_ref
  24.6 0.0 copy-done
  24.6 0.0 copy-done.2
  24.6 4.5 %first_row_lse.1 = (f32[1,1024]{1,0:T(1,128)S(1)}, bf16[1024,128]{1,0:T(8,128)(2,1)S(1)}, bf16[128,4096]{1,0:T(8,128)(2,1)S(1)}, f32[1,1024]{1,0:T(1,128)S(1)}, ...) custom-call(bf16[64,1024]{1,0:T(8,128)(2,1)S(1)} %copy-done, f32[2,1024]{1,0:T(2,128)S(1)} %copy-done.2, ...), custom_call_target="tpu_custom_call" | custom-call | tf_op jit(solution)/shard_map/first_row_lse/pallas_call | solution.py:291
  29.1 3.1 %collective-permute-start.1 = (f32[1,1024]{1,0:T(1,128)S(1)}, f32[1,1024]{1,0:T(1,128)S(1)}, u32[]{:S(2)}, u32[]{:S(2)}) collective-permute-start(f32[1,1024]{1,0:T(1,128)S(1)} %get-tuple-element.21.guess_ref), channel_id=1, source_target_pairs={{0,1},{1,0},{2,3},{3,2},{4,5},{5,4},{6,7},{7,6},{8,9},{9,8},{10,11... | collective-permute-start | bytes 12296 | tf_op jit(solution)/shard_map/ppermute | solution.py:346
  32.1 1.0 collective-permute-done.1
  33.2 4.6 %collective-permute-start.2 = (f32[1,1024]{1,0:T(1,128)S(1)}, f32[1,1024]{1,0:T(1,128)S(1)}, u32[]{:S(2)}, u32[]{:S(2)}) collective-permute-start(f32[1,1024]{1,0:T(1,128)S(1)} %log_add_fusion.8.one_ref), channel_id=1, source_target_pairs={{0,3},{1,2},{2,1},{3,0},{4,7},{5,6},{6,5},{7,4},{8,11},{9,10},{10,... | collective-permute-start | bytes 12296 | tf_op jit(solution)/shard_map/ppermute | solution.py:346
  37.7 1.0 collective-permute-done.2.two_ref
  38.7 0.0 copy-start.1
  38.7 0.7 copy-done.1
  39.4 6.1 %col_lse.3 = (f32[1,2048]{1,0:T(1,128)S(1)}, f32[1,2048]{1,0:T(1,128)S(1)}, f32[1,1024]{1,0:T(1,128)}) custom-call(bf16[1024,128]{1,0:T(8,128)(2,1)S(1)} %get-tuple-element.16.a_ref, bf16[128,4096]{1,0:T(8,128)(2,1)S(1)} %get-tuple-element.17.b_ref, f32[1,1024]{1,0:T(1,128)S(1)} %get-tuple-element.18.r_ref, f32[1,4096]{1,0:T(1,128)S(1)} %get-tuple-element.19.c_ref, ...), custom_call_target="tpu_custom_call" | custom-call | tf_op jit(solution)/shard_map/col_lse/pallas_call | solution.py:320
  45.5 2.5 %collective-permute-start.3 = (f32[1,2048]{1,0:T(1,128)S(1)}, f32[1,2048]{1,0:T(1,128)S(1)}, u32[]{:S(2)}, u32[]{:S(2)}) collective-permute-start(f32[1,2048]{1,0:T(1,128)S(1)} %get-tuple-element.23.refs_1_), channel_id=1, source_target_pairs={{0,4},{4,0},{8,12},{12,8},{16,20},{20,16},{24,28},{28,24},{32,36},... | collective-permute-start | bytes 24584 | tf_op jit(solution)/shard_map/ppermute | solution.py:346
  48.0 0.8 collective-permute-done.3
  48.9 11.9 %all_to_all.21 = f32[32,16,128]{2,1,0:T(8,128)S(1)} all-to-all(f32[32,16,128]{2,1,0:T(8,128)S(1)} %broadcast_in_dim.25), channel_id=1, replica_groups={{0,8,16,24,32,40,48,56,64,72,80,88,96,104,112,120,128,136,144,152,160,1..., dimensions={0} | all-to-all | bytes 524288 | tf_op jit(solution)/shard_map/all_to_all | solution.py:358
  60.8 0.1 exponential_reduce_fusion.2
  60.9 1.6 %collective-permute-start.4 = (f32[1,2048]{1,0:T(1,128)S(1)}, f32[1,2048]{1,0:T(1,128)S(1)}, u32[]{:S(2)}, u32[]{:S(2)}) collective-permute-start(f32[1,2048]{1,0:T(1,128)S(1)} %bitcast.18), channel_id=1, source_target_pairs={{0,4},{4,0},{8,12},{12,8},{16,20},{20,16},{24,28},{28,24},{32,36},... | collective-permute-start | bytes 24584 | tf_op jit(solution)/shard_map/ppermute | solution.py:346
  62.5 0.8 collective-permute-done.4.other_ref
  63.4 3.6 %row_lse.2.guess_ref = f32[1,1024]{1,0:T(1,128)S(1)} custom-call(bf16[1024,128]{1,0:T(8,128)(2,1)S(1)} %get-tuple-element.16.a_ref, bf16[128,4096]{1,0:T(8,128)(2,1)S(1)} %get-tuple-element.17.b_ref, f32[1,1024]{1,0:T(1,128)S(1)} %get-tuple-element.18.r_ref, f32[1,4096]{1,0:T(1,128)S(1)} %get-tuple-element.19.c_ref, f32[1,4096]{1,0:T(1,128)S(1)} %get-tuple-element.20.w_ref, ...), custom_call_target="tpu_custom_call" | custom-call | tf_op jit(solution)/shard_map/row_lse/pallas_call | solution.py:309
  67.0 1.8 %collective-permute-start.5 = (f32[1,1024]{1,0:T(1,128)S(1)}, f32[1,1024]{1,0:T(1,128)S(1)}, u32[]{:S(2)}, u32[]{:S(2)}) collective-permute-start(f32[1,1024]{1,0:T(1,128)S(1)} %row_lse.2.guess_ref), channel_id=1, source_target_pairs={{0,1},{1,0},{2,3},{3,2},{4,5},{5,4},{6,7},{7,6},{8,9},{9,8},{10,11... | collective-permute-start | bytes 12296 | tf_op jit(solution)/shard_map/ppermute | solution.py:346
  68.8 1.7 %collective-permute-done.5 = f32[1,1024]{1,0:T(1,128)S(1)} collective-permute-done((f32[1,1024]{1,0:T(1,128)S(1)}, f32[1,1024]{1,0:T(1,128)S(1)}, u32[]{:S(2)}, u32[]{:S(2)}) %collective-permute-start.5) | collective-permute-done | bytes 4128 | tf_op jit(solution)/shard_map/ppermute | solution.py:346
  70.5 3.9 %collective-permute-start.6 = (f32[1,1024]{1,0:T(1,128)S(1)}, f32[1,1024]{1,0:T(1,128)S(1)}, u32[]{:S(2)}, u32[]{:S(2)}) collective-permute-start(f32[1,1024]{1,0:T(1,128)S(1)} %log_add_fusion.7.one_ref), channel_id=1, source_target_pairs={{0,3},{1,2},{2,1},{3,0},{4,7},{5,6},{6,5},{7,4},{8,11},{9,10},{10,... | collective-permute-start | bytes 12296 | tf_op jit(solution)/shard_map/ppermute | solution.py:346
  74.4 1.0 collective-permute-done.6.two_ref
  75.4 3.8 %col_lse.4 = (f32[1,2048]{1,0:T(1,128)S(1)}, f32[1,2048]{1,0:T(1,128)S(1)}, f32[1,1024]{1,0:T(1,128)}) custom-call(bf16[1024,128]{1,0:T(8,128)(2,1)S(1)} %get-tuple-element.16.a_ref, bf16[128,4096]{1,0:T(8,128)(2,1)S(1)} %get-tuple-element.17.b_ref, f32[1,1024]{1,0:T(1,128)S(1)} %get-tuple-element.18.r_ref, f32[1,4096]{1,0:T(1,128)S(1)} %get-tuple-element.19.c_ref, ...), custom_call_target="tpu_custom_call" | custom-call | tf_op jit(solution)/shard_map/col_lse/pallas_call | solution.py:320
  79.2 2.4 %collective-permute-start.7 = (f32[1,2048]{1,0:T(1,128)S(1)}, f32[1,2048]{1,0:T(1,128)S(1)}, u32[]{:S(2)}, u32[]{:S(2)}) collective-permute-start(f32[1,2048]{1,0:T(1,128)S(1)} %get-tuple-element.25.refs_1_), channel_id=1, source_target_pairs={{0,4},{4,0},{8,12},{12,8},{16,20},{20,16},{24,28},{28,24},{32,36},... | collective-permute-start | bytes 24584 | tf_op jit(solution)/shard_map/ppermute | solution.py:346
  81.6 0.8 collective-permute-done.7
  82.5 12.0 %all_to_all.22 = f32[32,16,128]{2,1,0:T(8,128)S(1)} all-to-all(f32[32,16,128]{2,1,0:T(8,128)S(1)} %broadcast_in_dim.26), channel_id=1, replica_groups={{0,8,16,24,32,40,48,56,64,72,80,88,96,104,112,120,128,136,144,152,160,1..., dimensions={0} | all-to-all | bytes 524288 | tf_op jit(solution)/shard_map/all_to_all | solution.py:358
  94.5 0.1 exponential_reduce_fusion.1
  94.6 1.6 %collective-permute-start.8 = (f32[1,2048]{1,0:T(1,128)S(1)}, f32[1,2048]{1,0:T(1,128)S(1)}, u32[]{:S(2)}, u32[]{:S(2)}) collective-permute-start(f32[1,2048]{1,0:T(1,128)S(1)} %bitcast.20), channel_id=1, source_target_pairs={{0,4},{4,0},{8,12},{12,8},{16,20},{20,16},{24,28},{28,24},{32,36},... | collective-permute-start | bytes 24584 | tf_op jit(solution)/shard_map/ppermute | solution.py:346
  96.2 0.8 collective-permute-done.8.other_ref
  97.1 3.4 %row_lse.3 = f32[1,1024]{1,0:T(1,128)S(1)} custom-call(bf16[1024,128]{1,0:T(8,128)(2,1)S(1)} %get-tuple-element.16.a_ref, bf16[128,4096]{1,0:T(8,128)(2,1)S(1)} %get-tuple-element.17.b_ref, f32[1,1024]{1,0:T(1,128)S(1)} %get-tuple-element.18.r_ref, f32[1,4096]{1,0:T(1,128)S(1)} %get-tuple-element.19.c_ref, f32[1,4096]{1,0:T(1,128)S(1)} %get-tuple-element.20.w_ref, ...), custom_call_target="tpu_custom_call" | custom-call | tf_op jit(solution)/shard_map/row_lse/pallas_call | solution.py:309
  100.5 1.8 %collective-permute-start.9 = (f32[1,1024]{1,0:T(1,128)S(1)}, f32[1,1024]{1,0:T(1,128)S(1)}, u32[]{:S(2)}, u32[]{:S(2)}) collective-permute-start(f32[1,1024]{1,0:T(1,128)S(1)} %row_lse.3), channel_id=1, source_target_pairs={{0,1},{1,0},{2,3},{3,2},{4,5},{5,4},{6,7},{7,6},{8,9},{9,8},{10,11... | collective-permute-start | bytes 12296 | tf_op jit(solution)/shard_map/ppermute | solution.py:346
  102.3 1.7 %collective-permute-done.9 = f32[1,1024]{1,0:T(1,128)S(1)} collective-permute-done((f32[1,1024]{1,0:T(1,128)S(1)}, f32[1,1024]{1,0:T(1,128)S(1)}, u32[]{:S(2)}, u32[]{:S(2)}) %collective-permute-start.9) | collective-permute-done | bytes 4128 | tf_op jit(solution)/shard_map/ppermute | solution.py:346
  104.0 3.9 %collective-permute-start.10 = (f32[1,1024]{1,0:T(1,128)S(1)}, f32[1,1024]{1,0:T(1,128)S(1)}, u32[]{:S(2)}, u32[]{:S(2)}) collective-permute-start(f32[1,1024]{1,0:T(1,128)S(1)} %log_add_fusion.6.one_ref), channel_id=1, source_target_pairs={{0,3},{1,2},{2,1},{3,0},{4,7},{5,6},{6,5},{7,4},{8,11},{9,10},{10,... | collective-permute-start | bytes 12296 | tf_op jit(solution)/shard_map/ppermute | solution.py:346
  107.9 1.0 collective-permute-done.10.two_ref
  108.9 4.1 %col_lse.5 = (f32[1,2048]{1,0:T(1,128)S(1)}, f32[1,2048]{1,0:T(1,128)S(1)}, f32[1,1024]{1,0:T(1,128)}) custom-call(bf16[1024,128]{1,0:T(8,128)(2,1)S(1)} %get-tuple-element.16.a_ref, bf16[128,4096]{1,0:T(8,128)(2,1)S(1)} %get-tuple-element.17.b_ref, f32[1,1024]{1,0:T(1,128)S(1)} %get-tuple-element.18.r_ref, f32[1,4096]{1,0:T(1,128)S(1)} %get-tuple-element.19.c_ref, ...), custom_call_target="tpu_custom_call" | custom-call | tf_op jit(solution)/shard_map/col_lse/pallas_call | solution.py:320
  113.0 2.4 %collective-permute-start.11 = (f32[1,2048]{1,0:T(1,128)S(1)}, f32[1,2048]{1,0:T(1,128)S(1)}, u32[]{:S(2)}, u32[]{:S(2)}) collective-permute-start(f32[1,2048]{1,0:T(1,128)S(1)} %get-tuple-element.28), channel_id=1, source_target_pairs={{0,4},{4,0},{8,12},{12,8},{16,20},{20,16},{24,28},{28,24},{32,36},... | collective-permute-start | bytes 24584 | tf_op jit(solution)/shard_map/ppermute | solution.py:346
  115.4 0.8 collective-permute-done.11
  116.3 12.0 %all_to_all.23 = f32[32,16,128]{2,1,0:T(8,128)S(1)} all-to-all(f32[32,16,128]{2,1,0:T(8,128)S(1)} %broadcast_in_dim.27), channel_id=1, replica_groups={{0,8,16,24,32,40,48,56,64,72,80,88,96,104,112,120,128,136,144,152,160,1..., dimensions={0} | all-to-all | bytes 524288 | tf_op jit(solution)/shard_map/all_to_all | solution.py:358
  128.3 0.1 exponential_reduce_fusion
  128.3 0.0 copy-start.3
  128.4 1.6 %collective-permute-start.12 = (f32[1,2048]{1,0:T(1,128)S(1)}, f32[1,2048]{1,0:T(1,128)S(1)}, u32[]{:S(2)}, u32[]{:S(2)}) collective-permute-start(f32[1,2048]{1,0:T(1,128)S(1)} %bitcast.15), channel_id=1, source_target_pairs={{0,4},{4,0},{8,12},{12,8},{16,20},{20,16},{24,28},{28,24},{32,36},... | collective-permute-start | bytes 24584 | tf_op jit(solution)/shard_map/ppermute | solution.py:346
  130.0 0.8 collective-permute-done.12.other_ref
  130.8 0.0 copy-done.3
  130.8 5.6 %plan_grad.1 = bf16[64,1024]{1,0:T(8,128)(2,1)S(1)} custom-call(bf16[64,1024]{1,0:T(8,128)(2,1)S(1)} %copy-done, bf16[1024,128]{1,0:T(8,128)(2,1)S(1)} %get-tuple-element.16.a_ref, bf16[128,4096]{1,0:T(8,128)(2,1)S(1)} %get-tuple-element.17.b_ref, f32[1,1024]{1,0:T(1,128)S(1)} %get-tuple-element.18.r_ref, f32[1,4096]{1,0:T(1,128)S(1)} %get-tuple-element.19.c_ref, ...), custom_call_target="tpu_custom_call" | custom-call | tf_op jit(solution)/shard_map/plan_grad/pallas_call | solution.py:331
  136.4 1.8 %collective-permute-start.13 = (bf16[64,1024]{1,0:T(8,128)(2,1)S(1)}, bf16[64,1024]{1,0:T(8,128)(2,1)S(1)}, u32[]{:S(2)}, u32[]{:S(2)}) collective-permute-start(bf16[64,1024]{1,0:T(8,128)(2,1)S(1)} %plan_grad.1), channel_id=1, source_target_pairs={{0,1},{1,0},{2,3},{3,2},{4,5},{5,4},{6,7},{7,6},{8,9},{9,8},{10,11... | collective-permute-start | bytes 393224 | tf_op jit(solution)/shard_map/ppermute | solution.py:346
  138.2 7.4 %collective-permute-done.13 = bf16[64,1024]{1,0:T(8,128)(2,1)S(1)} collective-permute-done((bf16[64,1024]{1,0:T(8,128)(2,1)S(1)}, bf16[64,1024]{1,0:T(8,128)(2,1)S(1)}, u32[]{:S(2)}, u32[]{:S(2)}) %collective-permute-start.13) | collective-permute-done | bytes 131104 | tf_op jit(solution)/shard_map/ppermute | solution.py:346
  145.6 2.0 %collective-permute-start.14 = (bf16[64,1024]{1,0:T(8,128)(2,1)S(1)}, bf16[64,1024]{1,0:T(8,128)(2,1)S(1)}, u32[]{:S(2)}, u32[]{:S(2)}) collective-permute-start(bf16[64,1024]{1,0:T(8,128)(2,1)S(1)} %reduce-precision_convert_fusion), channel_id=1, source_target_pairs={{0,3},{1,2},{2,1},{3,0},{4,7},{5,6},{6,5},{7,4},{8,11},{9,10},{10,... | collective-permute-start | bytes 393224 | tf_op jit(solution)/shard_map/ppermute | solution.py:346
  147.6 0.6 dynamic-slice_multiply_fusion
  148.2 4.2 %collective-permute-done.14 = bf16[64,1024]{1,0:T(8,128)(2,1)S(1)} collective-permute-done((bf16[64,1024]{1,0:T(8,128)(2,1)S(1)}, bf16[64,1024]{1,0:T(8,128)(2,1)S(1)}, u32[]{:S(2)}, u32[]{:S(2)}) %collective-permute-start.14) | collective-permute-done | bytes 131104 | tf_op jit(solution)/shard_map/ppermute | solution.py:346
  152.4 0.7 convert_add_fusion
  (17 shorter events, 0.5 us)
Async XLA Ops:
  0.6 0.7 copy-start.4
  0.6 0.7 copy-start.5
  20.9 3.7 %copy-start = (bf16[64,1024]{1,0:T(8,128)(2,1)S(1)}, bf16[64,1024]{1,0:T(8,128)(2,1)}, u32[]{:S(2)}) copy-start(bf16[64,1024]{1,0:T(8,128)(2,1)} %emb_ref.3) | copy-start | bytes 393220
  20.9 3.7 %copy-start.2 = (f32[2,1024]{1,0:T(2,128)S(1)}, f32[2,1024]{1,0:T(2,128)}, u32[]{:S(2)}) copy-start(f32[2,1024]{1,0:T(2,128)} %pos_ref.1) | copy-start | bytes 24580
  21.3 3.2 %collective-permute-start = (bf16[68,2048]{1,0:T(8,128)(2,1)S(1)}, bf16[68,2048]{1,0:T(8,128)(2,1)S(1)}, u32[]{:S(2)}, u32[]{:S(2)}) collective-permute-start(bf16[68,2048]{1,0:T(8,128)(2,1)S(1)} %reshape.102.own_ref), channel_id=1, source_target_pairs={{0,4},{4,0},{8,12},{12,8},{16,20},{20,16},{24,28},{28,24},{32,36},... | collective-permute-start | bytes 835592 | tf_op jit(solution)/shard_map/ppermute | solution.py:346
  29.1 4.1 %collective-permute-start.1 = (f32[1,1024]{1,0:T(1,128)S(1)}, f32[1,1024]{1,0:T(1,128)S(1)}, u32[]{:S(2)}, u32[]{:S(2)}) collective-permute-start(f32[1,1024]{1,0:T(1,128)S(1)} %get-tuple-element.21.guess_ref), channel_id=1, source_target_pairs={{0,1},{1,0},{2,3},{3,2},{4,5},{5,4},{6,7},{7,6},{8,9},{9,8},{10,11... | collective-permute-start | bytes 12296 | tf_op jit(solution)/shard_map/ppermute | solution.py:346
  33.2 5.6 %collective-permute-start.2 = (f32[1,1024]{1,0:T(1,128)S(1)}, f32[1,1024]{1,0:T(1,128)S(1)}, u32[]{:S(2)}, u32[]{:S(2)}) collective-permute-start(f32[1,1024]{1,0:T(1,128)S(1)} %log_add_fusion.8.one_ref), channel_id=1, source_target_pairs={{0,3},{1,2},{2,1},{3,0},{4,7},{5,6},{6,5},{7,4},{8,11},{9,10},{10,... | collective-permute-start | bytes 12296 | tf_op jit(solution)/shard_map/ppermute | solution.py:346
  38.7 0.7 copy-start.1
  45.5 3.3 %collective-permute-start.3 = (f32[1,2048]{1,0:T(1,128)S(1)}, f32[1,2048]{1,0:T(1,128)S(1)}, u32[]{:S(2)}, u32[]{:S(2)}) collective-permute-start(f32[1,2048]{1,0:T(1,128)S(1)} %get-tuple-element.23.refs_1_), channel_id=1, source_target_pairs={{0,4},{4,0},{8,12},{12,8},{16,20},{20,16},{24,28},{28,24},{32,36},... | collective-permute-start | bytes 24584 | tf_op jit(solution)/shard_map/ppermute | solution.py:346
  60.9 2.5 %collective-permute-start.4 = (f32[1,2048]{1,0:T(1,128)S(1)}, f32[1,2048]{1,0:T(1,128)S(1)}, u32[]{:S(2)}, u32[]{:S(2)}) collective-permute-start(f32[1,2048]{1,0:T(1,128)S(1)} %bitcast.18), channel_id=1, source_target_pairs={{0,4},{4,0},{8,12},{12,8},{16,20},{20,16},{24,28},{28,24},{32,36},... | collective-permute-start | bytes 24584 | tf_op jit(solution)/shard_map/ppermute | solution.py:346
  67.0 3.5 %collective-permute-start.5 = (f32[1,1024]{1,0:T(1,128)S(1)}, f32[1,1024]{1,0:T(1,128)S(1)}, u32[]{:S(2)}, u32[]{:S(2)}) collective-permute-start(f32[1,1024]{1,0:T(1,128)S(1)} %row_lse.2.guess_ref), channel_id=1, source_target_pairs={{0,1},{1,0},{2,3},{3,2},{4,5},{5,4},{6,7},{7,6},{8,9},{9,8},{10,11... | collective-permute-start | bytes 12296 | tf_op jit(solution)/shard_map/ppermute | solution.py:346
  70.5 4.9 %collective-permute-start.6 = (f32[1,1024]{1,0:T(1,128)S(1)}, f32[1,1024]{1,0:T(1,128)S(1)}, u32[]{:S(2)}, u32[]{:S(2)}) collective-permute-start(f32[1,1024]{1,0:T(1,128)S(1)} %log_add_fusion.7.one_ref), channel_id=1, source_target_pairs={{0,3},{1,2},{2,1},{3,0},{4,7},{5,6},{6,5},{7,4},{8,11},{9,10},{10,... | collective-permute-start | bytes 12296 | tf_op jit(solution)/shard_map/ppermute | solution.py:346
  79.2 3.2 %collective-permute-start.7 = (f32[1,2048]{1,0:T(1,128)S(1)}, f32[1,2048]{1,0:T(1,128)S(1)}, u32[]{:S(2)}, u32[]{:S(2)}) collective-permute-start(f32[1,2048]{1,0:T(1,128)S(1)} %get-tuple-element.25.refs_1_), channel_id=1, source_target_pairs={{0,4},{4,0},{8,12},{12,8},{16,20},{20,16},{24,28},{28,24},{32,36},... | collective-permute-start | bytes 24584 | tf_op jit(solution)/shard_map/ppermute | solution.py:346
  94.6 2.5 %collective-permute-start.8 = (f32[1,2048]{1,0:T(1,128)S(1)}, f32[1,2048]{1,0:T(1,128)S(1)}, u32[]{:S(2)}, u32[]{:S(2)}) collective-permute-start(f32[1,2048]{1,0:T(1,128)S(1)} %bitcast.20), channel_id=1, source_target_pairs={{0,4},{4,0},{8,12},{12,8},{16,20},{20,16},{24,28},{28,24},{32,36},... | collective-permute-start | bytes 24584 | tf_op jit(solution)/shard_map/ppermute | solution.py:346
  100.5 3.5 %collective-permute-start.9 = (f32[1,1024]{1,0:T(1,128)S(1)}, f32[1,1024]{1,0:T(1,128)S(1)}, u32[]{:S(2)}, u32[]{:S(2)}) collective-permute-start(f32[1,1024]{1,0:T(1,128)S(1)} %row_lse.3), channel_id=1, source_target_pairs={{0,1},{1,0},{2,3},{3,2},{4,5},{5,4},{6,7},{7,6},{8,9},{9,8},{10,11... | collective-permute-start | bytes 12296 | tf_op jit(solution)/shard_map/ppermute | solution.py:346
  104.0 4.9 %collective-permute-start.10 = (f32[1,1024]{1,0:T(1,128)S(1)}, f32[1,1024]{1,0:T(1,128)S(1)}, u32[]{:S(2)}, u32[]{:S(2)}) collective-permute-start(f32[1,1024]{1,0:T(1,128)S(1)} %log_add_fusion.6.one_ref), channel_id=1, source_target_pairs={{0,3},{1,2},{2,1},{3,0},{4,7},{5,6},{6,5},{7,4},{8,11},{9,10},{10,... | collective-permute-start | bytes 12296 | tf_op jit(solution)/shard_map/ppermute | solution.py:346
  113.0 3.2 %collective-permute-start.11 = (f32[1,2048]{1,0:T(1,128)S(1)}, f32[1,2048]{1,0:T(1,128)S(1)}, u32[]{:S(2)}, u32[]{:S(2)}) collective-permute-start(f32[1,2048]{1,0:T(1,128)S(1)} %get-tuple-element.28), channel_id=1, source_target_pairs={{0,4},{4,0},{8,12},{12,8},{16,20},{20,16},{24,28},{28,24},{32,36},... | collective-permute-start | bytes 24584 | tf_op jit(solution)/shard_map/ppermute | solution.py:346
  128.3 2.5 %copy-start.3 = (f32[1,1024]{1,0:T(1,128)S(1)}, f32[1,1024]{1,0:T(1,128)}, u32[]{:S(2)}) copy-start(f32[1,1024]{1,0:T(1,128)} %get-tuple-element.26.f_ref) | copy-start | bytes 12292
  128.4 2.5 %collective-permute-start.12 = (f32[1,2048]{1,0:T(1,128)S(1)}, f32[1,2048]{1,0:T(1,128)S(1)}, u32[]{:S(2)}, u32[]{:S(2)}) collective-permute-start(f32[1,2048]{1,0:T(1,128)S(1)} %bitcast.15), channel_id=1, source_target_pairs={{0,4},{4,0},{8,12},{12,8},{16,20},{20,16},{24,28},{28,24},{32,36},... | collective-permute-start | bytes 24584 | tf_op jit(solution)/shard_map/ppermute | solution.py:346
  136.4 9.2 %collective-permute-start.13 = (bf16[64,1024]{1,0:T(8,128)(2,1)S(1)}, bf16[64,1024]{1,0:T(8,128)(2,1)S(1)}, u32[]{:S(2)}, u32[]{:S(2)}) collective-permute-start(bf16[64,1024]{1,0:T(8,128)(2,1)S(1)} %plan_grad.1), channel_id=1, source_target_pairs={{0,1},{1,0},{2,3},{3,2},{4,5},{5,4},{6,7},{7,6},{8,9},{9,8},{10,11... | collective-permute-start | bytes 393224 | tf_op jit(solution)/shard_map/ppermute | solution.py:346
  145.6 6.8 %collective-permute-start.14 = (bf16[64,1024]{1,0:T(8,128)(2,1)S(1)}, bf16[64,1024]{1,0:T(8,128)(2,1)S(1)}, u32[]{:S(2)}, u32[]{:S(2)}) collective-permute-start(bf16[64,1024]{1,0:T(8,128)(2,1)S(1)} %reduce-precision_convert_fusion), channel_id=1, source_target_pairs={{0,3},{1,2},{2,1},{3,0},{4,7},{5,6},{6,5},{7,4},{8,11},{9,10},{10,... | collective-permute-start | bytes 393224 | tf_op jit(solution)/shard_map/ppermute | solution.py:346

commit v2 on v1

v2 whole, which is shorter than its diff:
```python
import functools

import jax
import jax.numpy as jnp
from jax import lax
from jax.experimental import pallas as pl
from jax.experimental.pallas import tpu as pltpu
from jax.sharding import PartitionSpec as P

ITERS = 3
EPS = 0.25
RHO = 2.0
LAM = RHO / (RHO + EPS)
EMB = 64
DEPTH = 128
PACK = 80
MIB = 1 << 20
LOW, HIGH = 1e-25, 1e30


def pieces(value):
    high = value.astype(jnp.bfloat16).astype(jnp.float32)
    rest = value - high
    mid = rest.astype(jnp.bfloat16).astype(jnp.float32)
    low = (rest - mid).astype(jnp.bfloat16).astype(jnp.float32)
    return high, mid, low


def stacked(rows, height, width):
    index = lax.broadcasted_iota(jnp.int32, (height, width), 0)
    block = jnp.zeros((height, width), jnp.float32)
    for at, row in enumerate(rows):
        if row is not None:
            block = jnp.where(index == at, row, block)
    return block


def source_static(emb_ref, pos_ref, out_ref):
    width = emb_ref.shape[1]
    pos = pos_ref[...]
    emb = emb_ref[...].astype(jnp.float32)
    sq = jnp.sum(emb * emb, axis=0, keepdims=True)
    shift = -(sq * (1.0 / EMB) + pos[0:1] * pos[0:1] + pos[1:2] * pos[1:2]) * (1.0 / EPS)
    pos = pos * (2.0 / EPS)
    zero, one = jnp.zeros((1, width), jnp.float32), jnp.ones((1, width), jnp.float32)
    rows = [*pieces(pos[0:1]), *pieces(pos[1:2]), zero, zero, zero, one, one, one]
    extra = stacked(rows, 16, width)
    emb = emb * (2.0 / (EMB * EPS))
    pad = jnp.zeros((DEPTH - PACK, 128), jnp.float32)
    for at in range(0, width, 128):
        block = jnp.concatenate([emb[:, at : at + 128], extra[:, at : at + 128], pad], axis=0)
        out_ref[at : at + 128, :] = block.T.astype(jnp.bfloat16)
    return shift


def target_static(pack_ref, at, out_ref):
    width = pack_ref.shape[1]
    pack = pack_ref[...].astype(jnp.float32)
    emb, geo = pack[0:EMB], pack[EMB : EMB + 4]
    sq = jnp.sum(emb * emb, axis=0, keepdims=True)
    x, y = geo[0:1], geo[1:2]
    shift = -(sq * (1.0 / EMB) + x * x + y * y) * (1.0 / EPS)
    one = jnp.ones((1, width), jnp.float32)
    cut = slice(at, at + width)
    out_ref[0:EMB, cut] = pack_ref[0:EMB, :]
    out_ref[EMB:PACK, cut] = stacked([x, x, x, y, y, y, one, one, one], 16, width).astype(jnp.bfloat16)
    out_ref[PACK:DEPTH, cut] = jnp.zeros((DEPTH - PACK, width), jnp.bfloat16)
    return shift, geo[2:3]


def source_parts(shift):
    block = stacked([None] * 6 + [*pieces(shift)], 16, shift.shape[1]).astype(jnp.bfloat16)
    above = jnp.zeros((EMB, 128), jnp.bfloat16)
    below = jnp.zeros((DEPTH - PACK, 128), jnp.bfloat16)
    return [
        jnp.concatenate([above, block[:, at : at + 128], below], axis=0).T
        for at in range(0, shift.shape[1], 128)
    ]


def set_source(a_ref, shift, a_s):
    for index, part in enumerate(source_parts(shift)):
        cut = slice(index * 128, index * 128 + 128)
        a_s[cut, :] = a_ref[cut, :] + part


def target_parts(rows, shift):
    block = stacked([None] * 9 + [*pieces(shift)], 16, shift.shape[1])
    return (rows.astype(jnp.float32) + block).astype(jnp.bfloat16)


def set_target(b_ref, shift, b_s):
    b_s[0:EMB, :] = b_ref[0:EMB, :]
    b_s[EMB:PACK, :] = target_parts(b_ref[EMB:PACK, :], shift)
    b_s[PACK:DEPTH, :] = b_ref[PACK:DEPTH, :]


def loop_lanes(width, work):
    def step(index, carry):
        work(pl.ds(pl.multiple_of(index * 128, 128), 128))
        return carry

    lax.fori_loop(0, width // 128, step, 0)


def loop_source(a_ref, shift_of, a_s):
    def work(cut):
        a_s[cut, :] = a_ref[cut, :] + source_parts(shift_of(cut))[0]

    loop_lanes(a_ref.shape[0], work)


def loop_target(b_ref, shift_of, b_s):
    def work(cut):
        b_s[0:EMB, cut] = b_ref[0:EMB, cut]
        b_s[EMB:PACK, cut] = target_parts(b_ref[EMB:PACK, cut], shift_of(cut))
        b_s[PACK:DEPTH, cut] = b_ref[PACK:DEPTH, cut]

    loop_lanes(b_ref.shape[1], work)


def over_lanes(acc_s, out_s, join):
    for at in range(0, acc_s.shape[0], 128):
        out_s[:, at : at + 128] = join(acc_s[at : at + 128, :].T, axis=0, keepdims=True)


def loop_over_lanes(acc_s, out_s, join):
    def work(cut):
        out_s[:, cut] = join(acc_s[cut, :].T, axis=0, keepdims=True)

    loop_lanes(acc_s.shape[0], work)


def score(a, b):
    return lax.dot_general(a, b, (((1,), (0,)), ((), ())), preferred_element_type=jnp.float32)


def over_tiles(left, right, tile, work, width=None):
    width = right.shape[1] if width is None else width
    tile = min(tile, width)

    def step(index, carry):
        cut = pl.ds(pl.multiple_of(index * tile, tile), tile)
        work(cut, score(left[...], right[:, cut]))
        return carry

    lax.fori_loop(0, width // tile, step, 0)


def folded(value, join):
    part = value[:, 0:128]
    for col in range(128, value.shape[1], 128):
        part = join(part, value[:, col : col + 128])
    return part


def row_sums(left, right, acc_s, tile):
    def work(cut, value):
        acc_s[...] += folded(jnp.exp(value), jnp.add)

    over_tiles(left, right, tile, work)


def row_tops(left, right, acc_s, tile, width=None):
    def work(cut, value):
        acc_s[...] = jnp.maximum(acc_s[...], folded(value, jnp.maximum))

    over_tiles(left, right, tile, work, width)


def col_sums(left, right, out, tile):
    def work(cut, value):
        out[:, cut] = jnp.sum(jnp.exp(value), axis=0, keepdims=True)

    over_tiles(left, right, tile, work)


def col_tops(left, right, out, tile):
    def work(cut, value):
        out[:, cut] = jnp.max(value, axis=0, keepdims=True)

    over_tiles(left, right, tile, work)


def in_range(total):
    return jnp.logical_and(jnp.min(total) > LOW, jnp.max(total) < HIGH)


def static_kernel(emb_ref, pos_ref, pack_ref, a_ref, r_ref, b_ref, c_ref, w_ref, ready_ref, guess_ref, acc_ref, b_s):
    r_ref[...] = source_static(emb_ref, pos_ref, a_ref)
    c_ref[...], w_ref[...] = target_static(pack_ref, 0, b_ref)
    set_target(b_ref, c_ref[...] + w_ref[...], b_s)
    set_source(a_ref, r_ref[...], ready_ref)
    acc_ref[...] = jnp.full(acc_ref.shape, -jnp.inf, jnp.float32)
    row_tops(ready_ref, b_s, acc_ref, 512, min(512, b_s.shape[1]))
    over_lanes(acc_ref, guess_ref, jnp.max)
    set_source(a_ref, r_ref[...] - guess_ref[...], ready_ref)
    acc_ref[...] = jnp.zeros_like(acc_ref)
    row_sums(ready_ref, b_s, acc_ref, NEAR)


def row_finish(a_ref, r_ref, near_b_ref, near_of, ready_ref, guess_ref, acc_ref, out_ref, a_s, near_s, far_s, acc_s, guess_s, total_s):
    acc_s[...] = acc_ref[...]
    row_sums(ready_ref, far_s, acc_s, FAR)
    over_lanes(acc_s, total_s, jnp.sum)
    guess_s[...] = guess_ref[...]

    @pl.when(jnp.logical_not(in_range(total_s[...])))
    def _():
        loop_target(near_b_ref, near_of, near_s)
        loop_source(a_ref, lambda cut: r_ref[:, cut], a_s)
        acc_s[...] = jnp.full(acc_s.shape, -jnp.inf, jnp.float32)
        row_tops(a_s, near_s, acc_s, SMALL)
        row_tops(a_s, far_s, acc_s, SMALL)
        loop_over_lanes(acc_s, guess_s, jnp.max)
        loop_source(a_ref, lambda cut: r_ref[:, cut] - guess_s[:, cut], a_s)
        acc_s[...] = jnp.zeros_like(acc_s)
        row_sums(a_s, near_s, acc_s, SMALL)
        row_sums(a_s, far_s, acc_s, SMALL)
        loop_over_lanes(acc_s, total_s, jnp.sum)

    out_ref[...] = guess_s[...] + jnp.log(total_s[...])


def first_kernel(a_ref, r_ref, near_b_ref, near_c_ref, near_w_ref, pack_ref, ready_ref, guess_ref, acc_ref, out_ref, b_ref, c_ref, w_ref, a_s, near_s, far_s, *rest):
    c_ref[...], w_ref[...] = target_static(pack_ref, 0, b_ref)
    set_target(b_ref, c_ref[...] + w_ref[...], far_s)
    near_of = lambda cut: near_c_ref[:, cut] + near_w_ref[:, cut]
    row_finish(a_ref, r_ref, near_b_ref, near_of, ready_ref, guess_ref, acc_ref, out_ref, a_s, near_s, far_s, *rest)


def near_kernel(b_ref, c_ref, w_ref, lse_ref, ready_ref, acc_ref, b_s):
    set_target(b_ref, c_ref[...] + w_ref[...] - LAM * lse_ref[...], b_s)
    acc_ref[...] = jnp.zeros_like(acc_ref)
    row_sums(ready_ref, b_s, acc_ref, NEAR)


def row_kernel(a_ref, r_ref, near_b_ref, near_c_ref, near_w_ref, near_lse_ref, b_ref, c_ref, w_ref, lse_ref, ready_ref, guess_ref, acc_ref, out_ref, a_s, near_s, far_s, *rest):
    set_target(b_ref, c_ref[...] + w_ref[...] - LAM * lse_ref[...], far_s)
    near_of = lambda cut: near_c_ref[:, cut] + near_w_ref[:, cut] - LAM * near_lse_ref[:, cut]
    row_finish(a_ref, r_ref, near_b_ref, near_of, ready_ref, guess_ref, acc_ref, out_ref, a_s, near_s, far_s, *rest)


def joined(first, second):
    top = jnp.maximum(first, second)
    return top + jnp.log(jnp.exp(first - top) + jnp.exp(second - top))


def prepare_kernel(a_ref, r_ref, lse_ref, near_b_ref, near_c_ref, near_guess_ref, far_b_ref, far_c_ref, far_guess_ref, *outs):
    near_ref, far_ref, *rest = outs
    set_target(far_b_ref, far_c_ref[...] - far_guess_ref[...], far_ref)
    set_target(near_b_ref, near_c_ref[...] - near_guess_ref[...], near_ref)
    for ready_ref in rest:
        set_source(a_ref, r_ref[...] - lse_ref[...], ready_ref)


def guess_kernel(a_ref, r_ref, lse_ref, near_b_ref, near_c_ref, far_b_ref, far_c_ref, logw_ref, near_ref, far_ref, ready_ref, near_guess_ref, far_guess_ref):
    set_source(a_ref, r_ref[...] + logw_ref[...] - LAM * lse_ref[...], ready_ref)
    for b_ref, c_ref, out_ref, top_ref in (
        (near_b_ref, near_c_ref, near_ref, near_guess_ref),
        (far_b_ref, far_c_ref, far_ref, far_guess_ref),
    ):
        set_target(b_ref, c_ref[...], out_ref)
        col_tops(ready_ref, out_ref, top_ref, 512)
        out_ref[EMB:PACK, :] = target_parts(b_ref[EMB:PACK, :], c_ref[...] - top_ref[...])
    set_source(a_ref, r_ref[...] - lse_ref[...], ready_ref)


def col_finish(left, b_ref, c_ref, ready_ref, guess_ref, out_ref, b_s, guess_s, total_s):
    col_sums(left, ready_ref, total_s, COLS)
    guess_s[...] = guess_ref[...]

    @pl.when(jnp.logical_not(in_range(total_s[...])))
    def _():
        loop_target(b_ref, lambda cut: c_ref[:, cut], b_s)
        col_tops(left, b_s, guess_s, SMALL)
        loop_target(b_ref, lambda cut: c_ref[:, cut] - guess_s[:, cut], b_s)
        col_sums(left, b_s, total_s, SMALL)

    out_ref[...] = guess_s[...] + jnp.log(total_s[...])


def far_col_kernel(a_ref, r_ref, logw_ref, one_ref, two_ref, b_ref, c_ref, ready_ref, guess_ref, out_ref, f_ref, left_ref, *rest):
    lse = joined(one_ref[...], two_ref[...])
    f_ref[...] = -LAM * EPS * lse
    set_source(a_ref, r_ref[...] + logw_ref[...] - LAM * lse, left_ref)
    col_finish(left_ref, b_ref, c_ref, ready_ref, guess_ref, out_ref, *rest)


def near_col_kernel(left_ref, b_ref, c_ref, ready_ref, guess_ref, out_ref, *rest):
    col_finish(left_ref, b_ref, c_ref, ready_ref, guess_ref, out_ref, *rest)


def plan_sums(left, b_s, mass_s, pull_s, tile):
    def work(cut, value):
        plan = jnp.exp(value)
        mass_s[...] += folded(plan, jnp.add)
        pull_s[...] += lax.dot_general(
            plan.astype(jnp.bfloat16),
            b_s[0:EMB, cut],
            (((1,), (1,)), ((), ())),
            preferred_element_type=jnp.float32,
        )

    over_tiles(left, b_s, tile, work)


def near_plan_kernel(left_ref, b_ref, c_ref, w_ref, lse_ref, mass_ref, pull_ref, b_s):
    set_target(b_ref, c_ref[...] + w_ref[...] - LAM * lse_ref[...], b_s)
    mass_ref[...] = jnp.zeros_like(mass_ref)
    pull_ref[...] = jnp.zeros_like(pull_ref)
    plan_sums(left_ref, b_s, mass_ref, pull_ref, PLAN)


def plan_kernel(emb_ref, left_ref, b_ref, c_ref, w_ref, lse_ref, mass_ref, pull_ref, out_ref, b_s, mass_s, pull_s, *, begin):
    rows = out_ref.shape[1]
    span = slice(begin, begin + rows)
    set_target(b_ref, c_ref[...] + w_ref[...] - LAM * lse_ref[...], b_s)
    mass_s[...] = mass_ref[span, :]
    pull_s[...] = pull_ref[span, :]
    plan_sums(left_ref.at[span, :], b_s, mass_s, pull_s, 2 * PLAN)
    for at in range(0, rows, 128):
        mass = jnp.sum(mass_s[at : at + 128, :].T, axis=0, keepdims=True)
        pull = jnp.concatenate([pull_s[at : at + 128, :], jnp.zeros((128, 128 - EMB), jnp.float32)], axis=1).T
        grad = mass * emb_ref[:, begin + at : begin + at + 128].astype(jnp.float32) - pull[0:EMB, :]
        out_ref[:, at : at + 128] = grad.astype(out_ref.dtype)


NEAR, FAR, COLS, PLAN = 1024, 2048, 1024, 512
SMALL = 128


def f32(*shape):
    return jax.ShapeDtypeStruct(shape, jnp.float32)


def bf16(*shape):
    return jax.ShapeDtypeStruct(shape, jnp.bfloat16)


def call(kernel, out_shape, scratch, name, *args, flops=10**8):
    return pl.pallas_call(
        kernel,
        out_shape=out_shape,
        scratch_shapes=[pltpu.VMEM(like.shape, like.dtype) for like in scratch],
        compiler_params=pltpu.CompilerParams(vmem_limit_bytes=32 * MIB),
        cost_estimate=pl.CostEstimate(flops=flops, bytes_accessed=2 * 10**6, transcendentals=0),
        name=name,
    )(*args)


def rounded_sum(first, second):
    total = first.astype(jnp.float32) + second.astype(jnp.float32)
    return lax.reduce_precision(total, 8, 7).astype(jnp.bfloat16)


def swapped(value, axis, mask):
    return lax.ppermute(value, axis, [(k, k ^ mask) for k in range(lax.axis_size(axis))])


def exchanged(value, join):
    value = join(value, swapped(value, "tgt", 1))
    return value, swapped(value, "tgt", 3)


def spread(block):
    size = lax.axis_size("src")
    groups = [list(range(core, size, 2)) for core in range(2)]
    block = jnp.broadcast_to(block, (size // 2,) + block.shape)
    return lax.all_to_all(block, "src", 0, 0, axis_index_groups=groups, tiled=True)


def per_device(src_emb, src_pos, src_logw, tgt_emb, tgt_pos, tgt_logw):
    piece = tgt_emb.shape[1]
    half = piece * (lax.axis_size("src") // 2)
    rows = src_emb.shape[1]
    logw = src_logw[None, :]
    pass_flops = 2 * rows * half * DEPTH
    left_like, right_like = bf16(rows, DEPTH), bf16(DEPTH, half)
    row_line, half_line, acc_like = f32(1, rows), f32(1, half), f32(rows, 128)
    row_scratch = (left_like, right_like, right_like, acc_like, row_line, row_line)
    col_scratch = (right_like, half_line, half_line)

    count = EMB + 4
    own = jnp.concatenate([tgt_emb, tgt_pos, tgt_logw[None, :], tgt_logw[None, :]], 0).reshape(count * piece // 128, 128)
    own = spread(own).reshape(-1, count, piece).transpose(1, 0, 2).reshape(count, half)
    other = swapped(own, "src", 1)
    a, r, near_b, near_c, near_w, ready, guess, acc = call(
        static_kernel,
        (left_like, row_line, right_like, half_line, half_line, left_like, row_line, acc_like),
        (right_like,),
        "static_parts",
        src_emb, src_pos, own,
        flops=pass_flops,
    )
    lse, far_b, far_c, far_w = call(
        first_kernel,
        (row_line, right_like, half_line, half_line),
        row_scratch,
        "first_row_lse",
        a, r, near_b, near_c, near_w, other, ready, guess, acc,
        flops=pass_flops,
    )
    near, far = (near_b, near_c, near_w), (far_b, far_c, far_w)

    for step in range(ITERS):
        if step:
            acc = call(near_kernel, acc_like, (right_like,), "near_row_lse", *near, col, ready, flops=pass_flops)
            lse = call(
                row_kernel, row_line, row_scratch, "row_lse",
                a, r, *near, col, *far, far_col, ready, lse, acc,
                flops=pass_flops,
            )
            more = () if step == ITERS - 1 else (left_like,)
            near_ready, far_ready, *ready = call(
                prepare_kernel, (right_like, right_like, *more), (), "prepare",
                a, r, lse, near_b, near_c, mine, far_b, far_c, theirs,
            )
            ready = ready[0] if ready else None
        else:
            near_ready, far_ready, ready, mine, theirs = call(
                guess_kernel, (right_like, right_like, left_like, half_line, half_line), (), "col_guess",
                a, r, lse, near_b, near_c, far_b, far_c, logw,
                flops=2 * pass_flops,
            )
        theirs, f, left = call(
            far_col_kernel, (half_line, row_line, left_like), col_scratch, "far_col_lse",
            a, r, logw, *exchanged(lse, joined), far_b, far_c, far_ready, theirs,
            flops=pass_flops,
        )
        moved = swapped(theirs, "src", 1)
        mine = call(
            near_col_kernel, half_line, col_scratch, "near_col_lse",
            left, near_b, near_c, near_ready, mine,
            flops=pass_flops,
        )
        col = spread(joined(mine, moved).reshape(half // 128, 128))
        top = jnp.max(col, axis=0)
        col = (top + jnp.log(jnp.sum(jnp.exp(col - top), axis=0))).reshape(1, half)
        far_col = swapped(col, "src", 1)
    begin = lax.axis_index("src") // 2 * piece
    g_own = -LAM * EPS * lax.dynamic_slice_in_dim(col[0], begin, piece, 0)
    mass, pull = call(
        near_plan_kernel, (acc_like, f32(rows, EMB)), (right_like,), "near_plan",
        left, *near, col,
        flops=2 * pass_flops,
    )
    grads = []
    for begin in range(0, rows, rows // 2):
        grad = call(
            functools.partial(plan_kernel, begin=begin),
            bf16(EMB, rows // 2),
            (right_like, f32(rows // 2, 128), f32(rows // 2, EMB)),
            "plan_grad",
            src_emb, left, *far, far_col, mass, pull,
            flops=pass_flops,
        )
        grads.append(exchanged(grad, rounded_sum))
    first, second = (jnp.concatenate(part, axis=1).astype(jnp.float32) for part in zip(*grads))
    return f[0], g_own, first + second


def solution(mesh):
    placed = (
        P(None, "src"),
        P(None, "src"),
        P("src"),
        P(None, ("src", "tgt")),
        P(None, ("src", "tgt")),
        P(("src", "tgt")),
    )
    return jax.shard_map(
        per_device,
        mesh=mesh,
        in_specs=placed,
        out_specs=(P("src"), P(("src", "tgt")), P(None, "src")),
        check_vma=False,
    )
```

time: 154 us -> 143 us (0.929)
  starting transfers between devices: 37 us -> 30.2 us
  waiting for transfers between devices: 25.1 us -> 20.1 us
    ppermute x15 -> x17, starting transfers between devices: 37 us -> 30.2 us  [swapped(): lax.ppermute(value, axis, [(k, k ^ mask) for k in range(lax.axis_size(axi...]
    ppermute x15 -> x17, waiting for transfers between devices: 25.1 us -> 20.1 us  [swapped(): lax.ppermute(value, axis, [(k, k ^ mask) for k in range(lax.axis_size(axi...]
    pallas_call x7 -> x18, Pallas kernels: 31 us -> 32.3 us  [call(): pl.pallas_call(kernel, out_shape=out_shape, scratch_shapes=[pltpu.VMEM(li...]
  transfers between devices with their start and end apart: 15 -> 17, of which waited for: 15 -> 9; matrix products, arithmetic and copies ran while one was open for 0% -> 0% of each run, Pallas kernels for 0% -> 13%
where the time goes in v2:
time: 143 us; the launch traced here: 142 us
  blocking collectives  54.4 us (38%)
  Pallas kernels  32.3 us (23%)
  starting transfers between devices  30.2 us (21%)
  waiting for transfers between devices  20.1 us (14%)
  other arithmetic  2.61 us (2%)
  local copies, waits for them, and re-layouts  1.75 us (1%)
    all_to_all x4, blocking collectives, spread(): lax.all_to_all(block, 'src', 0, 0, axis_index_groups=groups, tiled=True)  54.4 us
    pallas_call x18, Pallas kernels, call(): pl.pallas_call(kernel, out_shape=out_shape, scratch_shapes=[pltpu.VMEM(li...  32.3 us
    ppermute x17, starting transfers between devices, swapped(): lax.ppermute(value, axis, [(k, k ^ mask) for k in range(lax.axis_size(axi...  30.2 us
    ppermute x17, waiting for transfers between devices, swapped(): lax.ppermute(value, axis, [(k, k ^ mask) for k in range(lax.axis_size(axi...  20.1 us
  transfers between devices with their start and end apart: 17, of which 9 were waited for; matrix products, arithmetic and copies ran while one was open for 0% of the time, Pallas kernels for 13%

profile of v2, /device:TPU:1, one launch (start us, length us, event | category | flops | bytes accessed | tf_op | source)
XLA Modules:
  0.0 142.3 jit_solution(865414950182247194)
XLA Ops:
  0.7 0.6 copy-done.3
  1.3 0.0 copy-done.4
  1.3 0.7 pad_maximum_fusion
  2.0 0.1 reshape.100
  2.2 18.2 %all_to_all.20 = bf16[32,34,128]{2,1,0:T(8,128)(2,1)S(1)} all-to-all(bf16[32,34,128]{2,1,0:T(8,128)(2,1)S(1)} %broadcast_in_dim.23), channel_id=1, replica_groups={{0,8,16,24,32,40,48,56,64,72,80,88,96,104,112,120,128,136,144,152,160,1..., dimensions={0} | all-to-all | bytes 557056 | tf_op jit(solution)/shard_map/all_to_all | solution.py:370
  20.4 0.4 reshape.101
  20.8 0.1 copy.10
  20.9 0.0 copy-start
  20.9 0.0 copy-start.1
  20.9 0.4 reshape.102.pack_ref
  21.3 2.0 %collective-permute-start = (bf16[68,2048]{1,0:T(8,128)(2,1)S(1)}, bf16[68,2048]{1,0:T(8,128)(2,1)S(1)}, u32[]{:S(2)}, u32[]{:S(2)}) collective-permute-start(bf16[68,2048]{1,0:T(8,128)(2,1)S(1)} %reshape.102.pack_ref), channel_id=1, source_target_pairs={{0,4},{4,0},{8,12},{12,8},{16,20},{20,16},{24,28},{28,24},{32,36},... | collective-permute-start | bytes 835592 | tf_op jit(solution)/shard_map/ppermute | solution.py:358
  23.4 2.3 %static_parts.1 = (bf16[1024,128]{1,0:T(8,128)(2,1)S(1)}, f32[1,1024]{1,0:T(1,128)S(1)}, bf16[128,2048]{1,0:T(8,128)(2,1)S(1)}, f32[1,2048]{1,0:T(1,128)S(1)}, f...) custom-call(bf16[64,1024]{1,0:T(8,128)(2,1)S(1)} %copy-done, ...), custom_call_target="tpu_custom_call" | custom-call | flops 536870912 | bytes 2000000 | tf_op jit(solution)/shard_map/static_parts/pallas_call | solution.py:342
  25.7 0.0 collective-permute-done.pack_ref
  25.7 1.6 %first_row_lse.1 = (f32[1,1024]{1,0:T(1,128)S(1)}, bf16[128,2048]{1,0:T(8,128)(2,1)S(1)}, f32[1,2048]{1,0:T(1,128)S(1)}, f32[1,2048]{1,0:T(1,128)S(1)}) custom-call(bf16[1024,128]{1,0:T(8,128)(2,1)S(1)} %get-tuple-element.34.a_ref, f32[1,1024]{1,0:T(1,128)S(1)} %get-tuple-element.35.r_ref, bf16[128,2048]{1,0:T(8,128)(2,1)S(1)} %get-tuple-element.36.near_b_ref.b_ref, ...), custom_call_target="tpu_custom_call" | custom-call | flops 536870912 | bytes 2000000 | tf_op jit(solution)/shard_map/first_row_lse/pallas_call | solution.py:342
  27.3 3.1 %collective-permute-start.1 = (f32[1,1024]{1,0:T(1,128)S(1)}, f32[1,1024]{1,0:T(1,128)S(1)}, u32[]{:S(2)}, u32[]{:S(2)}) collective-permute-start(f32[1,1024]{1,0:T(1,128)S(1)} %get-tuple-element.42.lse_ref.guess_ref), channel_id=1, source_target_pairs={{0,1},{1,0},{2,3},{3,2},{4,5},{5,4},{6,7},{7,6},{8,9},{9,8},{10,11... | collective-permute-start | bytes 12296 | tf_op jit(solution)/shard_map/ppermute | solution.py:358
  30.4 1.0 collective-permute-done.1
  31.5 0.0 copy-start.2
  31.5 4.6 %collective-permute-start.2 = (f32[1,1024]{1,0:T(1,128)S(1)}, f32[1,1024]{1,0:T(1,128)S(1)}, u32[]{:S(2)}, u32[]{:S(2)}) collective-permute-start(f32[1,1024]{1,0:T(1,128)S(1)} %log_add_fusion.8.one_ref), channel_id=1, source_target_pairs={{0,3},{1,2},{2,1},{3,0},{4,7},{5,6},{6,5},{7,4},{8,11},{9,10},{10,... | collective-permute-start | bytes 12296 | tf_op jit(solution)/shard_map/ppermute | solution.py:358
  36.0 3.9 %col_guess.1 = (bf16[128,2048]{1,0:T(8,128)(2,1)S(1)}, bf16[128,2048]{1,0:T(8,128)(2,1)S(1)}, bf16[1024,128]{1,0:T(8,128)(2,1)S(1)}, f32[1,2048]{1,0:T(1,128)S(1)}, f32[1,2048]{1,0:T(1,128)S(1)}) custom-call(bf16[1024,128]{1,0:T(8,128)(2,1)S(1)} %get-tuple-element.34.a_ref, f32[1,1024]{1,0:T(1,128)S(1)} %get-tuple-element.35.r_ref, ...), custom_call_target="tpu_custom_call" | custom-call | flops 1073741824 | bytes 2000000 | tf_op jit(solution)/shard_map/col_guess/pallas_call | solution.py:342
  40.0 2.3 %far_col_lse.3 = (f32[1,2048]{1,0:T(1,128)S(1)}, f32[1,1024]{1,0:T(1,128)}, bf16[1024,128]{1,0:T(8,128)(2,1)S(1)}) custom-call(bf16[1024,128]{1,0:T(8,128)(2,1)S(1)} %get-tuple-element.34.a_ref, f32[1,1024]{1,0:T(1,128)S(1)} %get-tuple-element.35.r_ref, f32[1,1024]{1,0:T(1,128)S(1)} %bitcast.21, f32[1,1024]{1,0:T(1,128)S(1)} %log_add_fusion.8.one_ref, ...), custom_call_target="tpu_custom_call" | custom-call | flops 536870912 | bytes 2000000 | tf_op jit(solution)/shard_map/far_col_lse/pallas_call | solution.py:342
  42.3 1.8 %collective-permute-start.3 = (f32[1,2048]{1,0:T(1,128)S(1)}, f32[1,2048]{1,0:T(1,128)S(1)}, u32[]{:S(2)}, u32[]{:S(2)}) collective-permute-start(f32[1,2048]{1,0:T(1,128)S(1)} %get-tuple-element.50.far_guess_ref.guess_ref), channel_id=1, source_target_pairs={{0,4},{4,0},{8,12},{12,8},{16,20},{20,16},{24,28},{28,24},{32,36},... | collective-permute-start | bytes 24584 | tf_op jit(solution)/shard_map/ppermute | solution.py:358
  44.1 1.6 %near_col_lse.3.near_guess_ref.guess_ref = f32[1,2048]{1,0:T(1,128)S(1)} custom-call(bf16[1024,128]{1,0:T(8,128)(2,1)S(1)} %get-tuple-element.47.left_ref, bf16[128,2048]{1,0:T(8,128)(2,1)S(1)} %get-tuple-element.36.near_b_ref.b_ref, f32[1,2048]{1,0:T(1,128)S(1)} %get-tuple-element.37.near_c_ref.c_ref, bf16[128,2048]{1,0:T(8,128)(2,1)S(1)} %get-tuple-element.48.ready_ref, ...), custom_call_target="tpu_custom_call" | custom-call | flops 536870912 | bytes 2000000 | tf_op jit(solution)/shard_map/near_col_lse/pallas_call | solution.py:342
  45.8 12.0 %all_to_all.21 = f32[32,16,128]{2,1,0:T(8,128)S(1)} all-to-all(f32[32,16,128]{2,1,0:T(8,128)S(1)} %broadcast_in_dim.25), channel_id=1, replica_groups={{0,8,16,24,32,40,48,56,64,72,80,88,96,104,112,120,128,136,144,152,160,1..., dimensions={0} | all-to-all | bytes 524288 | tf_op jit(solution)/shard_map/all_to_all | solution.py:370
  57.8 0.1 exponential_reduce_fusion.2
  57.9 1.7 %collective-permute-start.4 = (f32[1,2048]{1,0:T(1,128)S(1)}, f32[1,2048]{1,0:T(1,128)S(1)}, u32[]{:S(2)}, u32[]{:S(2)}) collective-permute-start(f32[1,2048]{1,0:T(1,128)S(1)} %bitcast.11), channel_id=1, source_target_pairs={{0,4},{4,0},{8,12},{12,8},{16,20},{20,16},{24,28},{28,24},{32,36},... | collective-permute-start | bytes 24584 | tf_op jit(solution)/shard_map/ppermute | solution.py:358
  59.6 1.5 %near_row_lse.2.acc_ref = f32[1024,128]{1,0:T(8,128)S(1)} custom-call(bf16[128,2048]{1,0:T(8,128)(2,1)S(1)} %get-tuple-element.36.near_b_ref.b_ref, f32[1,2048]{1,0:T(1,128)S(1)} %get-tuple-element.37.near_c_ref.c_ref, f32[1,2048]{1,0:T(1,128)S(1)} %get-tuple-element.38.near_w_ref.w_ref, f32[1,2048]{1,0:T(1,128)S(1)} %bitcast.12, ...), custom_call_target="tpu_custom_call" | custom-call | flops 536870912 | bytes 2000000 | tf_op jit(solution)/shard_map/near_row_lse/pallas_call | solution.py:342
  61.1 1.5 %row_lse.2.lse_ref.guess_ref = f32[1,1024]{1,0:T(1,128)S(1)} custom-call(bf16[1024,128]{1,0:T(8,128)(2,1)S(1)} %get-tuple-element.34.a_ref, f32[1,1024]{1,0:T(1,128)S(1)} %get-tuple-element.35.r_ref, bf16[128,2048]{1,0:T(8,128)(2,1)S(1)} %get-tuple-element.36.near_b_ref.b_ref, f32[1,2048]{1,0:T(1,128)S(1)} %get-tuple-element.37.near_c_ref.c_ref, ...), custom_call_target="tpu_custom_call" | custom-call | flops 536870912 | bytes 2000000 | tf_op jit(solution)/shard_map/row_lse/pallas_call | solution.py:342
  62.6 1.2 collective-permute-start.5
  63.9 2.2 %collective-permute-done.5 = f32[1,1024]{1,0:T(1,128)S(1)} collective-permute-done((f32[1,1024]{1,0:T(1,128)S(1)}, f32[1,1024]{1,0:T(1,128)S(1)}, u32[]{:S(2)}, u32[]{:S(2)}) %collective-permute-start.5) | collective-permute-done | bytes 4128 | tf_op jit(solution)/shard_map/ppermute | solution.py:358
  66.1 1.6 %collective-permute-start.6 = (f32[1,1024]{1,0:T(1,128)S(1)}, f32[1,1024]{1,0:T(1,128)S(1)}, u32[]{:S(2)}, u32[]{:S(2)}) collective-permute-start(f32[1,1024]{1,0:T(1,128)S(1)} %log_add_fusion.7.one_ref), channel_id=1, source_target_pairs={{0,3},{1,2},{2,1},{3,0},{4,7},{5,6},{6,5},{7,4},{8,11},{9,10},{10,... | collective-permute-start | bytes 12296 | tf_op jit(solution)/shard_map/ppermute | solution.py:358
  67.7 0.3 prepare.2
  68.0 2.8 %collective-permute-done.6.two_ref = f32[1,1024]{1,0:T(1,128)S(1)} collective-permute-done((f32[1,1024]{1,0:T(1,128)S(1)}, f32[1,1024]{1,0:T(1,128)S(1)}, u32[]{:S(2)}, u32[]{:S(2)}) %collective-permute-start.6) | collective-permute-done | bytes 4128 | tf_op jit(solution)/shard_map/ppermute | solution.py:358
  70.8 2.3 %far_col_lse.4 = (f32[1,2048]{1,0:T(1,128)S(1)}, f32[1,1024]{1,0:T(1,128)}, bf16[1024,128]{1,0:T(8,128)(2,1)S(1)}) custom-call(bf16[1024,128]{1,0:T(8,128)(2,1)S(1)} %get-tuple-element.34.a_ref, f32[1,1024]{1,0:T(1,128)S(1)} %get-tuple-element.35.r_ref, f32[1,1024]{1,0:T(1,128)S(1)} %bitcast.22, f32[1,1024]{1,0:T(1,128)S(1)} %log_add_fusion.7.one_ref, ...), custom_call_target="tpu_custom_call" | custom-call | flops 536870912 | bytes 2000000 | tf_op jit(solution)/shard_map/far_col_lse/pallas_call | solution.py:342
  73.1 2.4 %collective-permute-start.7 = (f32[1,2048]{1,0:T(1,128)S(1)}, f32[1,2048]{1,0:T(1,128)S(1)}, u32[]{:S(2)}, u32[]{:S(2)}) collective-permute-start(f32[1,2048]{1,0:T(1,128)S(1)} %get-tuple-element.56.far_guess_ref.guess_ref), channel_id=1, source_target_pairs={{0,4},{4,0},{8,12},{12,8},{16,20},{20,16},{24,28},{28,24},{32,36},... | collective-permute-start | bytes 24584 | tf_op jit(solution)/shard_map/ppermute | solution.py:358
  75.5 1.6 %near_col_lse.4.near_guess_ref.guess_ref = f32[1,2048]{1,0:T(1,128)S(1)} custom-call(bf16[1024,128]{1,0:T(8,128)(2,1)S(1)} %get-tuple-element.54.left_ref, bf16[128,2048]{1,0:T(8,128)(2,1)S(1)} %get-tuple-element.36.near_b_ref.b_ref, f32[1,2048]{1,0:T(1,128)S(1)} %get-tuple-element.37.near_c_ref.c_ref, bf16[128,2048]{1,0:T(8,128)(2,1)S(1)} %get-tuple-element.55.ready_ref, ...), custom_call_target="tpu_custom_call" | custom-call | flops 536870912 | bytes 2000000 | tf_op jit(solution)/shard_map/near_col_lse/pallas_call | solution.py:342
  77.1 12.1 %all_to_all.22 = f32[32,16,128]{2,1,0:T(8,128)S(1)} all-to-all(f32[32,16,128]{2,1,0:T(8,128)S(1)} %broadcast_in_dim.26), channel_id=1, replica_groups={{0,8,16,24,32,40,48,56,64,72,80,88,96,104,112,120,128,136,144,152,160,1..., dimensions={0} | all-to-all | bytes 524288 | tf_op jit(solution)/shard_map/all_to_all | solution.py:370
  89.3 0.1 exponential_reduce_fusion.1
  89.3 1.5 %collective-permute-start.8 = (f32[1,2048]{1,0:T(1,128)S(1)}, f32[1,2048]{1,0:T(1,128)S(1)}, u32[]{:S(2)}, u32[]{:S(2)}) collective-permute-start(f32[1,2048]{1,0:T(1,128)S(1)} %bitcast.14), channel_id=1, source_target_pairs={{0,4},{4,0},{8,12},{12,8},{16,20},{20,16},{24,28},{28,24},{32,36},... | collective-permute-start | bytes 24584 | tf_op jit(solution)/shard_map/ppermute | solution.py:358
  90.8 1.5 %near_row_lse.3.acc_ref = f32[1024,128]{1,0:T(8,128)S(1)} custom-call(bf16[128,2048]{1,0:T(8,128)(2,1)S(1)} %get-tuple-element.36.near_b_ref.b_ref, f32[1,2048]{1,0:T(1,128)S(1)} %get-tuple-element.37.near_c_ref.c_ref, f32[1,2048]{1,0:T(1,128)S(1)} %get-tuple-element.38.near_w_ref.w_ref, f32[1,2048]{1,0:T(1,128)S(1)} %bitcast.15, ...), custom_call_target="tpu_custom_call" | custom-call | flops 536870912 | bytes 2000000 | tf_op jit(solution)/shard_map/near_row_lse/pallas_call | solution.py:342
  92.4 1.5 %row_lse.3.lse_ref = f32[1,1024]{1,0:T(1,128)S(1)} custom-call(bf16[1024,128]{1,0:T(8,128)(2,1)S(1)} %get-tuple-element.34.a_ref, f32[1,1024]{1,0:T(1,128)S(1)} %get-tuple-element.35.r_ref, bf16[128,2048]{1,0:T(8,128)(2,1)S(1)} %get-tuple-element.36.near_b_ref.b_ref, f32[1,2048]{1,0:T(1,128)S(1)} %get-tuple-element.37.near_c_ref.c_ref, ...), custom_call_target="tpu_custom_call" | custom-call | flops 536870912 | bytes 2000000 | tf_op jit(solution)/shard_map/row_lse/pallas_call | solution.py:342
  93.9 1.2 collective-permute-start.9
  95.1 2.2 %collective-permute-done.9 = f32[1,1024]{1,0:T(1,128)S(1)} collective-permute-done((f32[1,1024]{1,0:T(1,128)S(1)}, f32[1,1024]{1,0:T(1,128)S(1)}, u32[]{:S(2)}, u32[]{:S(2)}) %collective-permute-start.9) | collective-permute-done | bytes 4128 | tf_op jit(solution)/shard_map/ppermute | solution.py:358
  97.4 1.8 %collective-permute-start.10 = (f32[1,1024]{1,0:T(1,128)S(1)}, f32[1,1024]{1,0:T(1,128)S(1)}, u32[]{:S(2)}, u32[]{:S(2)}) collective-permute-start(f32[1,1024]{1,0:T(1,128)S(1)} %log_add_fusion.6.one_ref), channel_id=1, source_target_pairs={{0,3},{1,2},{2,1},{3,0},{4,7},{5,6},{6,5},{7,4},{8,11},{9,10},{10,... | collective-permute-start | bytes 12296 | tf_op jit(solution)/shard_map/ppermute | solution.py:358
  99.1 0.1 prepare.3
  99.3 3.0 %collective-permute-done.10.two_ref = f32[1,1024]{1,0:T(1,128)S(1)} collective-permute-done((f32[1,1024]{1,0:T(1,128)S(1)}, f32[1,1024]{1,0:T(1,128)S(1)}, u32[]{:S(2)}, u32[]{:S(2)}) %collective-permute-start.10) | collective-permute-done | bytes 4128 | tf_op jit(solution)/shard_map/ppermute | solution.py:358
  102.2 2.3 %far_col_lse.5 = (f32[1,2048]{1,0:T(1,128)S(1)}, f32[1,1024]{1,0:T(1,128)}, bf16[1024,128]{1,0:T(8,128)(2,1)S(1)}) custom-call(bf16[1024,128]{1,0:T(8,128)(2,1)S(1)} %get-tuple-element.34.a_ref, f32[1,1024]{1,0:T(1,128)S(1)} %get-tuple-element.35.r_ref, f32[1,1024]{1,0:T(1,128)S(1)} %bitcast.23, f32[1,1024]{1,0:T(1,128)S(1)} %log_add_fusion.6.one_ref, ...), custom_call_target="tpu_custom_call" | custom-call | flops 536870912 | bytes 2000000 | tf_op jit(solution)/shard_map/far_col_lse/pallas_call | solution.py:342
  104.6 2.3 %collective-permute-start.11 = (f32[1,2048]{1,0:T(1,128)S(1)}, f32[1,2048]{1,0:T(1,128)S(1)}, u32[]{:S(2)}, u32[]{:S(2)}) collective-permute-start(f32[1,2048]{1,0:T(1,128)S(1)} %get-tuple-element.62), channel_id=1, source_target_pairs={{0,4},{4,0},{8,12},{12,8},{16,20},{20,16},{24,28},{28,24},{32,36},... | collective-permute-start | bytes 24584 | tf_op jit(solution)/shard_map/ppermute | solution.py:358
  106.9 1.6 %near_col_lse.5 = f32[1,2048]{1,0:T(1,128)S(1)} custom-call(bf16[1024,128]{1,0:T(8,128)(2,1)S(1)} %get-tuple-element.60.left_ref, bf16[128,2048]{1,0:T(8,128)(2,1)S(1)} %get-tuple-element.36.near_b_ref.b_ref, f32[1,2048]{1,0:T(1,128)S(1)} %get-tuple-element.37.near_c_ref.c_ref, bf16[128,2048]{1,0:T(8,128)(2,1)S(1)} %get-tuple-element.61.ready_ref, ...), custom_call_target="tpu_custom_call" | custom-call | flops 536870912 | bytes 2000000 | tf_op jit(solution)/shard_map/near_col_lse/pallas_call | solution.py:342
  108.6 12.1 %all_to_all.23 = f32[32,16,128]{2,1,0:T(8,128)S(1)} all-to-all(f32[32,16,128]{2,1,0:T(8,128)S(1)} %broadcast_in_dim.27), channel_id=1, replica_groups={{0,8,16,24,32,40,48,56,64,72,80,88,96,104,112,120,128,136,144,152,160,1..., dimensions={0} | all-to-all | bytes 524288 | tf_op jit(solution)/shard_map/all_to_all | solution.py:370
  120.7 0.1 exponential_reduce_fusion
  120.8 1.5 %collective-permute-start.12 = (f32[1,2048]{1,0:T(1,128)S(1)}, f32[1,2048]{1,0:T(1,128)S(1)}, u32[]{:S(2)}, u32[]{:S(2)}) collective-permute-start(f32[1,2048]{1,0:T(1,128)S(1)} %bitcast.17), channel_id=1, source_target_pairs={{0,4},{4,0},{8,12},{12,8},{16,20},{20,16},{24,28},{28,24},{32,36},... | collective-permute-start | bytes 24584 | tf_op jit(solution)/shard_map/ppermute | solution.py:358
  122.3 2.9 %near_plan.1 = (f32[1024,128]{1,0:T(8,128)S(1)}, f32[1024,64]{1,0:T(8,128)S(1)}) custom-call(bf16[1024,128]{1,0:T(8,128)(2,1)S(1)} %get-tuple-element.60.left_ref, bf16[128,2048]{1,0:T(8,128)(2,1)S(1)} %get-tuple-element.36.near_b_ref.b_ref, f32[1,2048]{1,0:T(1,128)S(1)} %get-tuple-element.37.near_c_ref.c_ref, ...), custom_call_target="tpu_custom_call" | custom-call | flops 1073741824 | bytes 2000000 | tf_op jit(solution)/shard_map/near_plan/pallas_call | solution.py:342
  125.2 1.7 %plan_grad.2 = bf16[64,512]{1,0:T(8,128)(2,1)S(1)} custom-call(bf16[64,1024]{1,0:T(8,128)(2,1)S(1)} %copy-done, bf16[1024,128]{1,0:T(8,128)(2,1)S(1)} %get-tuple-element.60.left_ref, bf16[128,2048]{1,0:T(8,128)(2,1)S(1)} %get-tuple-element.43.far_b_ref.b_ref, f32[1,2048]{1,0:T(1,128)S(1)} %get-tuple-element.44.far_c_ref.c_ref, ...), custom_call_target="tpu_custom_call" | custom-call | flops 536870912 | bytes 2000000 | tf_op jit(solution)/shard_map/plan_grad/pallas_call | solution.py:342
  126.9 1.2 collective-permute-start.13
  128.1 1.7 %plan_grad.3 = bf16[64,512]{1,0:T(8,128)(2,1)S(1)} custom-call(bf16[64,1024]{1,0:T(8,128)(2,1)S(1)} %copy-done, bf16[1024,128]{1,0:T(8,128)(2,1)S(1)} %get-tuple-element.60.left_ref, bf16[128,2048]{1,0:T(8,128)(2,1)S(1)} %get-tuple-element.43.far_b_ref.b_ref, f32[1,2048]{1,0:T(1,128)S(1)} %get-tuple-element.44.far_c_ref.c_ref, ...), custom_call_target="tpu_custom_call" | custom-call | flops 536870912 | bytes 2000000 | tf_op jit(solution)/shard_map/plan_grad/pallas_call | solution.py:342
  129.8 1.3 collective-permute-start.14
  131.2 2.1 %collective-permute-done.13 = bf16[64,512]{1,0:T(8,128)(2,1)S(1)} collective-permute-done((bf16[64,512]{1,0:T(8,128)(2,1)S(1)}, bf16[64,512]{1,0:T(8,128)(2,1)S(1)}, u32[]{:S(2)}, u32[]{:S(2)}) %collective-permute-start.13) | collective-permute-done | bytes 65568 | tf_op jit(solution)/shard_map/ppermute | solution.py:358
  133.3 0.1 collective-permute-start.15
  133.4 2.8 %collective-permute-done.14 = bf16[64,512]{1,0:T(8,128)(2,1)S(1)} collective-permute-done((bf16[64,512]{1,0:T(8,128)(2,1)S(1)}, bf16[64,512]{1,0:T(8,128)(2,1)S(1)}, u32[]{:S(2)}, u32[]{:S(2)}) %collective-permute-start.14) | collective-permute-done | bytes 65568 | tf_op jit(solution)/shard_map/ppermute | solution.py:358
  136.2 0.9 collective-permute-start.16
  137.1 0.6 dynamic-slice_multiply_fusion
  137.7 1.0 collective-permute-done.15
  138.7 2.9 %collective-permute-done.16 = bf16[64,512]{1,0:T(8,128)(2,1)S(1)} collective-permute-done((bf16[64,512]{1,0:T(8,128)(2,1)S(1)}, bf16[64,512]{1,0:T(8,128)(2,1)S(1)}, u32[]{:S(2)}, u32[]{:S(2)}) %collective-permute-start.16) | collective-permute-done | bytes 65568 | tf_op jit(solution)/shard_map/ppermute | solution.py:358
  141.5 0.7 convert_add_fusion
  (30 shorter events, 0.5 us)
Async XLA Ops:
  0.6 0.7 copy-start.3
  0.6 0.7 copy-start.4
  20.9 2.5 %copy-start = (bf16[64,1024]{1,0:T(8,128)(2,1)S(1)}, bf16[64,1024]{1,0:T(8,128)(2,1)}, u32[]{:S(2)}) copy-start(bf16[64,1024]{1,0:T(8,128)(2,1)} %emb_ref.5) | copy-start | bytes 393220
  20.9 2.5 %copy-start.1 = (f32[2,1024]{1,0:T(2,128)S(1)}, f32[2,1024]{1,0:T(2,128)}, u32[]{:S(2)}) copy-start(f32[2,1024]{1,0:T(2,128)} %pos_ref.1) | copy-start | bytes 24580
  21.3 4.4 %collective-permute-start = (bf16[68,2048]{1,0:T(8,128)(2,1)S(1)}, bf16[68,2048]{1,0:T(8,128)(2,1)S(1)}, u32[]{:S(2)}, u32[]{:S(2)}) collective-permute-start(bf16[68,2048]{1,0:T(8,128)(2,1)S(1)} %reshape.102.pack_ref), channel_id=1, source_target_pairs={{0,4},{4,0},{8,12},{12,8},{16,20},{20,16},{24,28},{28,24},{32,36},... | collective-permute-start | bytes 835592 | tf_op jit(solution)/shard_map/ppermute | solution.py:358
  27.3 4.1 %collective-permute-start.1 = (f32[1,1024]{1,0:T(1,128)S(1)}, f32[1,1024]{1,0:T(1,128)S(1)}, u32[]{:S(2)}, u32[]{:S(2)}) collective-permute-start(f32[1,1024]{1,0:T(1,128)S(1)} %get-tuple-element.42.lse_ref.guess_ref), channel_id=1, source_target_pairs={{0,1},{1,0},{2,3},{3,2},{4,5},{5,4},{6,7},{7,6},{8,9},{9,8},{10,11... | collective-permute-start | bytes 12296 | tf_op jit(solution)/shard_map/ppermute | solution.py:358
  31.5 4.6 %copy-start.2 = (f32[1024]{0:T(1024)S(1)}, f32[1024]{0:T(1024)}, u32[]{:S(2)}) copy-start(f32[1024]{0:T(1024)} %param.8) | copy-start | bytes 12292
  31.5 8.5 %collective-permute-start.2 = (f32[1,1024]{1,0:T(1,128)S(1)}, f32[1,1024]{1,0:T(1,128)S(1)}, u32[]{:S(2)}, u32[]{:S(2)}) collective-permute-start(f32[1,1024]{1,0:T(1,128)S(1)} %log_add_fusion.8.one_ref), channel_id=1, source_target_pairs={{0,3},{1,2},{2,1},{3,0},{4,7},{5,6},{6,5},{7,4},{8,11},{9,10},{10,... | collective-permute-start | bytes 12296 | tf_op jit(solution)/shard_map/ppermute | solution.py:358
  42.3 3.4 %collective-permute-start.3 = (f32[1,2048]{1,0:T(1,128)S(1)}, f32[1,2048]{1,0:T(1,128)S(1)}, u32[]{:S(2)}, u32[]{:S(2)}) collective-permute-start(f32[1,2048]{1,0:T(1,128)S(1)} %get-tuple-element.50.far_guess_ref.guess_ref), channel_id=1, source_target_pairs={{0,4},{4,0},{8,12},{12,8},{16,20},{20,16},{24,28},{28,24},{32,36},... | collective-permute-start | bytes 24584 | tf_op jit(solution)/shard_map/ppermute | solution.py:358
  57.9 3.2 %collective-permute-start.4 = (f32[1,2048]{1,0:T(1,128)S(1)}, f32[1,2048]{1,0:T(1,128)S(1)}, u32[]{:S(2)}, u32[]{:S(2)}) collective-permute-start(f32[1,2048]{1,0:T(1,128)S(1)} %bitcast.11), channel_id=1, source_target_pairs={{0,4},{4,0},{8,12},{12,8},{16,20},{20,16},{24,28},{28,24},{32,36},... | collective-permute-start | bytes 24584 | tf_op jit(solution)/shard_map/ppermute | solution.py:358
  62.6 3.5 %collective-permute-start.5 = (f32[1,1024]{1,0:T(1,128)S(1)}, f32[1,1024]{1,0:T(1,128)S(1)}, u32[]{:S(2)}, u32[]{:S(2)}) collective-permute-start(f32[1,1024]{1,0:T(1,128)S(1)} %row_lse.2.lse_ref.guess_ref), channel_id=1, source_target_pairs={{0,1},{1,0},{2,3},{3,2},{4,5},{5,4},{6,7},{7,6},{8,9},{9,8},{10,11... | collective-permute-start | bytes 12296 | tf_op jit(solution)/shard_map/ppermute | solution.py:358
  66.1 4.7 %collective-permute-start.6 = (f32[1,1024]{1,0:T(1,128)S(1)}, f32[1,1024]{1,0:T(1,128)S(1)}, u32[]{:S(2)}, u32[]{:S(2)}) collective-permute-start(f32[1,1024]{1,0:T(1,128)S(1)} %log_add_fusion.7.one_ref), channel_id=1, source_target_pairs={{0,3},{1,2},{2,1},{3,0},{4,7},{5,6},{6,5},{7,4},{8,11},{9,10},{10,... | collective-permute-start | bytes 12296 | tf_op jit(solution)/shard_map/ppermute | solution.py:358
  73.1 3.9 %collective-permute-start.7 = (f32[1,2048]{1,0:T(1,128)S(1)}, f32[1,2048]{1,0:T(1,128)S(1)}, u32[]{:S(2)}, u32[]{:S(2)}) collective-permute-start(f32[1,2048]{1,0:T(1,128)S(1)} %get-tuple-element.56.far_guess_ref.guess_ref), channel_id=1, source_target_pairs={{0,4},{4,0},{8,12},{12,8},{16,20},{20,16},{24,28},{28,24},{32,36},... | collective-permute-start | bytes 24584 | tf_op jit(solution)/shard_map/ppermute | solution.py:358
  89.3 3.0 %collective-permute-start.8 = (f32[1,2048]{1,0:T(1,128)S(1)}, f32[1,2048]{1,0:T(1,128)S(1)}, u32[]{:S(2)}, u32[]{:S(2)}) collective-permute-start(f32[1,2048]{1,0:T(1,128)S(1)} %bitcast.14), channel_id=1, source_target_pairs={{0,4},{4,0},{8,12},{12,8},{16,20},{20,16},{24,28},{28,24},{32,36},... | collective-permute-start | bytes 24584 | tf_op jit(solution)/shard_map/ppermute | solution.py:358
  93.9 3.5 %collective-permute-start.9 = (f32[1,1024]{1,0:T(1,128)S(1)}, f32[1,1024]{1,0:T(1,128)S(1)}, u32[]{:S(2)}, u32[]{:S(2)}) collective-permute-start(f32[1,1024]{1,0:T(1,128)S(1)} %row_lse.3.lse_ref), channel_id=1, source_target_pairs={{0,1},{1,0},{2,3},{3,2},{4,5},{5,4},{6,7},{7,6},{8,9},{9,8},{10,11... | collective-permute-start | bytes 12296 | tf_op jit(solution)/shard_map/ppermute | solution.py:358
  97.4 4.9 %collective-permute-start.10 = (f32[1,1024]{1,0:T(1,128)S(1)}, f32[1,1024]{1,0:T(1,128)S(1)}, u32[]{:S(2)}, u32[]{:S(2)}) collective-permute-start(f32[1,1024]{1,0:T(1,128)S(1)} %log_add_fusion.6.one_ref), channel_id=1, source_target_pairs={{0,3},{1,2},{2,1},{3,0},{4,7},{5,6},{6,5},{7,4},{8,11},{9,10},{10,... | collective-permute-start | bytes 12296 | tf_op jit(solution)/shard_map/ppermute | solution.py:358
  104.6 3.9 %collective-permute-start.11 = (f32[1,2048]{1,0:T(1,128)S(1)}, f32[1,2048]{1,0:T(1,128)S(1)}, u32[]{:S(2)}, u32[]{:S(2)}) collective-permute-start(f32[1,2048]{1,0:T(1,128)S(1)} %get-tuple-element.62), channel_id=1, source_target_pairs={{0,4},{4,0},{8,12},{12,8},{16,20},{20,16},{24,28},{28,24},{32,36},... | collective-permute-start | bytes 24584 | tf_op jit(solution)/shard_map/ppermute | solution.py:358
  120.8 4.5 %collective-permute-start.12 = (f32[1,2048]{1,0:T(1,128)S(1)}, f32[1,2048]{1,0:T(1,128)S(1)}, u32[]{:S(2)}, u32[]{:S(2)}) collective-permute-start(f32[1,2048]{1,0:T(1,128)S(1)} %bitcast.17), channel_id=1, source_target_pairs={{0,4},{4,0},{8,12},{12,8},{16,20},{20,16},{24,28},{28,24},{32,36},... | collective-permute-start | bytes 24584 | tf_op jit(solution)/shard_map/ppermute | solution.py:358
  126.9 6.4 %collective-permute-start.13 = (bf16[64,512]{1,0:T(8,128)(2,1)S(1)}, bf16[64,512]{1,0:T(8,128)(2,1)S(1)}, u32[]{:S(2)}, u32[]{:S(2)}) collective-permute-start(bf16[64,512]{1,0:T(8,128)(2,1)S(1)} %plan_grad.2), channel_id=1, source_target_pairs={{0,1},{1,0},{2,3},{3,2},{4,5},{5,4},{6,7},{7,6},{8,9},{9,8},{10,11... | collective-permute-start | bytes 196616 | tf_op jit(solution)/shard_map/ppermute | solution.py:358
  129.8 6.4 %collective-permute-start.14 = (bf16[64,512]{1,0:T(8,128)(2,1)S(1)}, bf16[64,512]{1,0:T(8,128)(2,1)S(1)}, u32[]{:S(2)}, u32[]{:S(2)}) collective-permute-start(bf16[64,512]{1,0:T(8,128)(2,1)S(1)} %plan_grad.3), channel_id=1, source_target_pairs={{0,1},{1,0},{2,3},{3,2},{4,5},{5,4},{6,7},{7,6},{8,9},{9,8},{10,11... | collective-permute-start | bytes 196616 | tf_op jit(solution)/shard_map/ppermute | solution.py:358
  133.3 5.3 %collective-permute-start.15 = (bf16[64,512]{1,0:T(8,128)(2,1)S(1)}, bf16[64,512]{1,0:T(8,128)(2,1)S(1)}, u32[]{:S(2)}, u32[]{:S(2)}) collective-permute-start(bf16[64,512]{1,0:T(8,128)(2,1)S(1)} %reduce-precision_convert_fusion.1), channel_id=1, source_target_pairs={{0,3},{1,2},{2,1},{3,0},{4,7},{5,6},{6,5},{7,4},{8,11},{9,10},{10,... | collective-permute-start | bytes 196616 | tf_op jit(solution)/shard_map/ppermute | solution.py:358
  136.2 5.3 %collective-permute-start.16 = (bf16[64,512]{1,0:T(8,128)(2,1)S(1)}, bf16[64,512]{1,0:T(8,128)(2,1)S(1)}, u32[]{:S(2)}, u32[]{:S(2)}) collective-permute-start(bf16[64,512]{1,0:T(8,128)(2,1)S(1)} %reduce-precision_convert_fusion), channel_id=1, source_target_pairs={{0,3},{1,2},{2,1},{3,0},{4,7},{5,6},{6,5},{7,4},{8,11},{9,10},{10,... | collective-permute-start | bytes 196616 | tf_op jit(solution)/shard_map/ppermute | solution.py:358

commit v3 on v2

--- a/solution.py
+++ b/solution.py
@@ -35,22 +35,21 @@
     return block
 
 
-def source_static(emb_ref, pos_ref, out_ref):
+def source_static(emb_ref, pos_ref, out_ref, shift_ref):
     width = emb_ref.shape[1]
     pos = pos_ref[...]
     emb = emb_ref[...].astype(jnp.float32)
     sq = jnp.sum(emb * emb, axis=0, keepdims=True)
     shift = -(sq * (1.0 / EMB) + pos[0:1] * pos[0:1] + pos[1:2] * pos[1:2]) * (1.0 / EPS)
     pos = pos * (2.0 / EPS)
-    zero, one = jnp.zeros((1, width), jnp.float32), jnp.ones((1, width), jnp.float32)
-    rows = [*pieces(pos[0:1]), *pieces(pos[1:2]), zero, zero, zero, one, one, one]
-    extra = stacked(rows, 16, width)
+    one = jnp.ones((1, width), jnp.float32)
+    extra = stacked([*pieces(pos[0:1]), *pieces(pos[1:2]), one, one, one], 16, width)
     emb = emb * (2.0 / (EMB * EPS))
     pad = jnp.zeros((DEPTH - PACK, 128), jnp.float32)
     for at in range(0, width, 128):
         block = jnp.concatenate([emb[:, at : at + 128], extra[:, at : at + 128], pad], axis=0)
         out_ref[at : at + 128, :] = block.T.astype(jnp.bfloat16)
-    return shift
+        shift_ref[at // 128 : at // 128 + 1, :] = shift[:, at : at + 128]
 
 
 def target_static(pack_ref, at, out_ref):
@@ -60,32 +59,26 @@
     sq = jnp.sum(emb * emb, axis=0, keepdims=True)
     x, y = geo[0:1], geo[1:2]
     shift = -(sq * (1.0 / EMB) + x * x + y * y) * (1.0 / EPS)
-    one = jnp.ones((1, width), jnp.float32)
     cut = slice(at, at + width)
     out_ref[0:EMB, cut] = pack_ref[0:EMB, :]
-    out_ref[EMB:PACK, cut] = stacked([x, x, x, y, y, y, one, one, one], 16, width).astype(jnp.bfloat16)
-    out_ref[PACK:DEPTH, cut] = jnp.zeros((DEPTH - PACK, width), jnp.bfloat16)
+    out_ref[EMB:PACK, cut] = stacked([x, x, x, y, y, y], 16, width).astype(jnp.bfloat16)
+    depth = lax.broadcasted_iota(jnp.int32, (DEPTH - PACK, width), 0)
+    out_ref[PACK:DEPTH, cut] = jnp.where(depth < 24, 1.0, 0.0).astype(jnp.bfloat16)
     return shift, geo[2:3]
 
 
-def source_parts(shift):
-    block = stacked([None] * 6 + [*pieces(shift)], 16, shift.shape[1]).astype(jnp.bfloat16)
-    above = jnp.zeros((EMB, 128), jnp.bfloat16)
-    below = jnp.zeros((DEPTH - PACK, 128), jnp.bfloat16)
-    return [
-        jnp.concatenate([above, block[:, at : at + 128], below], axis=0).T
-        for at in range(0, shift.shape[1], 128)
-    ]
-
-
 def set_source(a_ref, shift, a_s):
-    for index, part in enumerate(source_parts(shift)):
+    above = jnp.zeros((PACK, 128), jnp.float32)
+    below = jnp.zeros((DEPTH - PACK - 24, 128), jnp.float32)
+    turned = jnp.concatenate([above, *pieces(shift), below], axis=0).T
+    own = lax.rem(lax.broadcasted_iota(jnp.int32, (128, DEPTH), 1), 8)
+    for index in range(8):
         cut = slice(index * 128, index * 128 + 128)
-        a_s[cut, :] = a_ref[cut, :] + part
+        a_s[cut, :] = a_ref[cut, :] + jnp.where(own == index, turned, 0.0).astype(jnp.bfloat16)
 
 
 def target_parts(rows, shift):
-    block = stacked([None] * 9 + [*pieces(shift)], 16, shift.shape[1])
+    block = stacked([None] * 6 + [*pieces(shift)], 16, shift.shape[1])
     return (rows.astype(jnp.float32) + block).astype(jnp.bfloat16)
 
 
@@ -101,13 +94,6 @@
         return carry
 
     lax.fori_loop(0, width // 128, step, 0)
-
-
-def loop_source(a_ref, shift_of, a_s):
-    def work(cut):
-        a_s[cut, :] = a_ref[cut, :] + source_parts(shift_of(cut))[0]
-
-    loop_lanes(a_ref.shape[0], work)
 
 
 def loop_target(b_ref, shift_of, b_s):
@@ -120,15 +106,17 @@
 
 
 def over_lanes(acc_s, out_s, join):
-    for at in range(0, acc_s.shape[0], 128):
-        out_s[:, at : at + 128] = join(acc_s[at : at + 128, :].T, axis=0, keepdims=True)
+    for index in range(8):
+        out_s[index : index + 1, :] = join(acc_s[index * 128 : index * 128 + 128, :].T, axis=0, keepdims=True)
 
 
 def loop_over_lanes(acc_s, out_s, join):
-    def work(cut):
-        out_s[:, cut] = join(acc_s[cut, :].T, axis=0, keepdims=True)
-
-    loop_lanes(acc_s.shape[0], work)
+    def step(index, carry):
+        cut = pl.ds(pl.multiple_of(index * 128, 128), 128)
+        out_s[pl.ds(index, 1), :] = join(acc_s[cut, :].T, axis=0, keepdims=True)
+        return carry
+
+    lax.fori_loop(0, 8, step, 0)
 
 
 def score(a, b):
@@ -170,7 +158,8 @@
 
 def col_sums(left, right, out, tile):
     def work(cut, value):
-        out[:, cut] = jnp.sum(jnp.exp(value), axis=0, keepdims=True)
+        part = jnp.sum(jnp.exp(value).reshape(-1, 16, value.shape[1]), axis=0)
+        out[:, cut] = jnp.sum(part, axis=0, keepdims=True)
 
     over_tiles(left, right, tile, work)
 
@@ -187,7 +176,7 @@
 
 
 def static_kernel(emb_ref, pos_ref, pack_ref, a_ref, r_ref, b_ref, c_ref, w_ref, ready_ref, guess_ref, acc_ref, b_s):
-    r_ref[...] = source_static(emb_ref, pos_ref, a_ref)
+    source_static(emb_ref, pos_ref, a_ref, r_ref)
     c_ref[...], w_ref[...] = target_static(pack_ref, 0, b_ref)
     set_target(b_ref, c_ref[...] + w_ref[...], b_s)
     set_source(a_ref, r_ref[...], ready_ref)
@@ -208,12 +197,12 @@
     @pl.when(jnp.logical_not(in_range(total_s[...])))
     def _():
         loop_target(near_b_ref, near_of, near_s)
-        loop_source(a_ref, lambda cut: r_ref[:, cut], a_s)
+        set_source(a_ref, r_ref[...], a_s)
         acc_s[...] = jnp.full(acc_s.shape, -jnp.inf, jnp.float32)
         row_tops(a_s, near_s, acc_s, SMALL)
         row_tops(a_s, far_s, acc_s, SMALL)
         loop_over_lanes(acc_s, guess_s, jnp.max)
-        loop_source(a_ref, lambda cut: r_ref[:, cut] - guess_s[:, cut], a_s)
+        set_source(a_ref, r_ref[...] - guess_s[...], a_s)
         acc_s[...] = jnp.zeros_like(acc_s)
         row_sums(a_s, near_s, acc_s, SMALL)
         row_sums(a_s, far_s, acc_s, SMALL)
@@ -305,25 +294,40 @@
     over_tiles(left, b_s, tile, work)
 
 
+def plan_pass(left_ref, b_ref, c_ref, w_ref, lse_ref, b_s, mass_s, pull_s, tile):
+    set_target(b_ref, c_ref[...] + w_ref[...] - LAM * lse_ref[...], b_s)
+    plan_sums(left_ref, b_s, mass_s, pull_s, tile)
+
+
 def near_plan_kernel(left_ref, b_ref, c_ref, w_ref, lse_ref, mass_ref, pull_ref, b_s):
-    set_target(b_ref, c_ref[...] + w_ref[...] - LAM * lse_ref[...], b_s)
     mass_ref[...] = jnp.zeros_like(mass_ref)
     pull_ref[...] = jnp.zeros_like(pull_ref)
-    plan_sums(left_ref, b_s, mass_ref, pull_ref, PLAN)
-
-
-def plan_kernel(emb_ref, left_ref, b_ref, c_ref, w_ref, lse_ref, mass_ref, pull_ref, out_ref, b_s, mass_s, pull_s, *, begin):
-    rows = out_ref.shape[1]
-    span = slice(begin, begin + rows)
-    set_target(b_ref, c_ref[...] + w_ref[...] - LAM * lse_ref[...], b_s)
-    mass_s[...] = mass_ref[span, :]
-    pull_s[...] = pull_ref[span, :]
-    plan_sums(left_ref.at[span, :], b_s, mass_s, pull_s, 2 * PLAN)
-    for at in range(0, rows, 128):
+    plan_pass(left_ref.at[0 : mass_ref.shape[0], :], b_ref, c_ref, w_ref, lse_ref, b_s, mass_ref, pull_ref, PLAN)
+
+
+def plan_finish(emb_ref, begin, mass_s, pull_s, out_ref):
+    for at in range(0, out_ref.shape[1], 128):
         mass = jnp.sum(mass_s[at : at + 128, :].T, axis=0, keepdims=True)
         pull = jnp.concatenate([pull_s[at : at + 128, :], jnp.zeros((128, 128 - EMB), jnp.float32)], axis=1).T
         grad = mass * emb_ref[:, begin + at : begin + at + 128].astype(jnp.float32) - pull[0:EMB, :]
         out_ref[:, at : at + 128] = grad.astype(out_ref.dtype)
+
+
+def first_plan_kernel(emb_ref, left_ref, b_ref, c_ref, w_ref, lse_ref, mass_ref, pull_ref, out_ref, b_s, mass_s, pull_s):
+    mass_s[...] = mass_ref[...]
+    pull_s[...] = pull_ref[...]
+    plan_pass(left_ref.at[0 : out_ref.shape[1], :], b_ref, c_ref, w_ref, lse_ref, b_s, mass_s, pull_s, 2 * PLAN)
+    plan_finish(emb_ref, 0, mass_s, pull_s, out_ref)
+
+
+def last_plan_kernel(emb_ref, left_ref, near_b_ref, near_c_ref, near_w_ref, near_lse_ref, b_ref, c_ref, w_ref, lse_ref, out_ref, b_s, mass_s, pull_s):
+    mass_s[...] = jnp.zeros_like(mass_s)
+    pull_s[...] = jnp.zeros_like(pull_s)
+    begin = emb_ref.shape[1] - out_ref.shape[1]
+    left = left_ref.at[begin : emb_ref.shape[1], :]
+    plan_pass(left, near_b_ref, near_c_ref, near_w_ref, near_lse_ref, b_s, mass_s, pull_s, PLAN)
+    plan_pass(left, b_ref, c_ref, w_ref, lse_ref, b_s, mass_s, pull_s, PLAN)
+    plan_finish(emb_ref, begin, mass_s, pull_s, out_ref)
 
 
 NEAR, FAR, COLS, PLAN = 1024, 2048, 1024, 512
@@ -374,10 +378,10 @@
     piece = tgt_emb.shape[1]
     half = piece * (lax.axis_size("src") // 2)
     rows = src_emb.shape[1]
-    logw = src_logw[None, :]
+    logw = src_logw.reshape(8, rows // 8)
     pass_flops = 2 * rows * half * DEPTH
     left_like, right_like = bf16(rows, DEPTH), bf16(DEPTH, half)
-    row_line, half_line, acc_like = f32(1, rows), f32(1, half), f32(rows, 128)
+    row_line, half_line, acc_like = f32(8, rows // 8), f32(1, half), f32(rows, 128)
     row_scratch = (left_like, right_like, right_like, acc_like, row_line, row_line)
     col_scratch = (right_like, half_line, half_line)
 
@@ -440,24 +444,27 @@
         far_col = swapped(col, "src", 1)
     begin = lax.axis_index("src") // 2 * piece
     g_own = -LAM * EPS * lax.dynamic_slice_in_dim(col[0], begin, piece, 0)
-    mass, pull = call(
-        near_plan_kernel, (acc_like, f32(rows, EMB)), (right_like,), "near_plan",
+    part = rows // 2
+    sums_like = (f32(part, 128), f32(part, EMB))
+    sums = call(
+        near_plan_kernel, sums_like, (right_like,), "near_plan",
         left, *near, col,
+        flops=pass_flops,
+    )
+    grad = call(
+        first_plan_kernel, bf16(EMB, part), (right_like, *sums_like), "first_plan",
+        src_emb, left, *far, far_col, *sums,
+        flops=pass_flops,
+    )
+    grads = [exchanged(grad, rounded_sum)]
+    grad = call(
+        last_plan_kernel, bf16(EMB, part), (right_like, *sums_like), "last_plan",
+        src_emb, left, *near, col, *far, far_col,
         flops=2 * pass_flops,
     )
-    grads = []
-    for begin in range(0, rows, rows // 2):
-        grad = call(
-            functools.partial(plan_kernel, begin=begin),
-            bf16(EMB, rows // 2),
-            (right_like, f32(rows // 2, 128), f32(rows // 2, EMB)),
-            "plan_grad",
-            src_emb, left, *far, far_col, mass, pull,
-            flops=pass_flops,
-        )
-        grads.append(exchanged(grad, rounded_sum))
+    grads.append(exchanged(grad, rounded_sum))
     first, second = (jnp.concatenate(part, axis=1).astype(jnp.float32) for part in zip(*grads))
-    return f[0], g_own, first + second
+    return f.reshape(rows), g_own, first + second
 
 
 def solution(mesh):

time: 143 us -> 145 us (1.014)
  blocking collectives: 54.4 us -> 42.4 us
  waiting for transfers between devices: 20.1 us -> 28.6 us
  starting transfers between devices: 30.2 us -> 34.6 us
    all_to_all x4 -> x3, blocking collectives: 54.4 us -> 42.4 us  [spread(): lax.all_to_all(block, 'src', 0, 0, axis_index_groups=groups, tiled=True)]
    all_to_all x0 -> x1, waiting for transfers between devices: none -> 9.34 us  [spread(): lax.all_to_all(block, 'src', 0, 0, axis_index_groups=groups, tiled=True)]
    all_to_all x0 -> x1, starting transfers between devices: none -> 3.87 us  [spread(): lax.all_to_all(block, 'src', 0, 0, axis_index_groups=groups, tiled=True)]
  transfers between devices with their start and end apart: 17 -> 18, of which waited for: 9 -> 10; matrix products, arithmetic and copies ran while one was open for 0% -> 0% of each run, Pallas kernels for 13% -> 14%
where the time goes in v3:
time: 145 us; the launch traced here: 144 us
  blocking collectives  42.4 us (29%)
  starting transfers between devices  34.6 us (24%)
  Pallas kernels  32.8 us (23%)
  waiting for transfers between devices  28.6 us (20%)
  other arithmetic  2.56 us (2%)
  local copies, waits for them, and re-layouts  2.45 us (2%)
    all_to_all x3, blocking collectives, spread(): lax.all_to_all(block, 'src', 0, 0, axis_index_groups=groups, tiled=True)  42.4 us
    pallas_call x18, Pallas kernels, call(): pl.pallas_call(kernel, out_shape=out_shape, scratch_shapes=[pltpu.VMEM(li...  32.8 us
    ppermute x17, starting transfers between devices, swapped(): lax.ppermute(value, axis, [(k, k ^ mask) for k in range(lax.axis_size(axi...  30.7 us
    ppermute x17, waiting for transfers between devices, swapped(): lax.ppermute(value, axis, [(k, k ^ mask) for k in range(lax.axis_size(axi...  19.2 us
    all_to_all x1, waiting for transfers between devices, spread(): lax.all_to_all(block, 'src', 0, 0, axis_index_groups=groups, tiled=True)  9.34 us
    all_to_all x1, starting transfers between devices, spread(): lax.all_to_all(block, 'src', 0, 0, axis_index_groups=groups, tiled=True)  3.87 us
  transfers between devices with their start and end apart: 18, of which 10 were waited for; matrix products, arithmetic and copies ran while one was open for 0% of the time, Pallas kernels for 14%

profile of v3, /device:TPU:1, one launch (start us, length us, event | category | flops | bytes accessed | tf_op | source)
XLA Modules:
  0.0 144.3 jit_solution(14594526272678913021)
XLA Ops:
  0.7 0.6 copy-done.3
  1.3 0.0 copy-done.4
  1.3 0.7 pad_maximum_fusion
  2.0 0.1 reshape.106
  2.2 18.2 %all_to_all.20 = bf16[32,34,128]{2,1,0:T(8,128)(2,1)S(1)} all-to-all(bf16[32,34,128]{2,1,0:T(8,128)(2,1)S(1)} %broadcast_in_dim.20), channel_id=1, replica_groups={{0,8,16,24,32,40,48,56,64,72,80,88,96,104,112,120,128,136,144,152,160,1..., dimensions={0} | all-to-all | bytes 557056 | tf_op jit(solution)/shard_map/all_to_all | solution.py:374
  20.4 0.4 reshape.107
  20.8 0.1 copy.10
  20.9 0.0 copy-start
  20.9 0.4 reshape.108.pack_ref
  21.3 2.0 %collective-permute-start = (bf16[68,2048]{1,0:T(8,128)(2,1)S(1)}, bf16[68,2048]{1,0:T(8,128)(2,1)S(1)}, u32[]{:S(2)}, u32[]{:S(2)}) collective-permute-start(bf16[68,2048]{1,0:T(8,128)(2,1)S(1)} %reshape.108.pack_ref), channel_id=1, source_target_pairs={{0,4},{4,0},{8,12},{12,8},{16,20},{20,16},{24,28},{28,24},{32,36},... | collective-permute-start | bytes 835592 | tf_op jit(solution)/shard_map/ppermute | solution.py:362
  23.4 2.2 %static_parts.1 = (bf16[1024,128]{1,0:T(8,128)(2,1)S(1)}, f32[8,128]{1,0:T(8,128)S(1)}, bf16[128,2048]{1,0:T(8,128)(2,1)S(1)}, f32[1,2048]{1,0:T(1,128)S(1)}, f3...) custom-call(bf16[64,1024]{1,0:T(8,128)(2,1)S(1)} %copy-done, ...), custom_call_target="tpu_custom_call" | custom-call | flops 536870912 | bytes 2000000 | tf_op jit(solution)/shard_map/static_parts/pallas_call | solution.py:346
  25.6 1.6 %first_row_lse.1 = (f32[8,128]{1,0:T(8,128)S(1)}, bf16[128,2048]{1,0:T(8,128)(2,1)S(1)}, f32[1,2048]{1,0:T(1,128)S(1)}, f32[1,2048]{1,0:T(1,128)S(1)}) custom-call(bf16[1024,128]{1,0:T(8,128)(2,1)S(1)} %get-tuple-element.34.a_ref, f32[8,128]{1,0:T(8,128)S(1)} %get-tuple-element.35.r_ref, bf16[128,2048]{1,0:T(8,128)(2,1)S(1)} %get-tuple-element.36.near_b_ref.b_ref, ...), custom_call_target="tpu_custom_call" | custom-call | flops 536870912 | bytes 2000000 | tf_op jit(solution)/shard_map/first_row_lse/pallas_call | solution.py:346
  27.2 3.1 %collective-permute-start.1 = (f32[8,128]{1,0:T(8,128)S(1)}, f32[8,128]{1,0:T(8,128)S(1)}, u32[]{:S(2)}, u32[]{:S(2)}) collective-permute-start(f32[8,128]{1,0:T(8,128)S(1)} %get-tuple-element.42.lse_ref.guess_ref), channel_id=1, source_target_pairs={{0,1},{1,0},{2,3},{3,2},{4,5},{5,4},{6,7},{7,6},{8,9},{9,8},{10,11... | collective-permute-start | bytes 12296 | tf_op jit(solution)/shard_map/ppermute | solution.py:362
  30.3 1.0 collective-permute-done.1
  31.3 0.0 copy-start.2
  31.3 4.6 %collective-permute-start.2 = (f32[8,128]{1,0:T(8,128)S(1)}, f32[8,128]{1,0:T(8,128)S(1)}, u32[]{:S(2)}, u32[]{:S(2)}) collective-permute-start(f32[8,128]{1,0:T(8,128)S(1)} %log_add_fusion.8.one_ref), channel_id=1, source_target_pairs={{0,3},{1,2},{2,1},{3,0},{4,7},{5,6},{6,5},{7,4},{8,11},{9,10},{10,... | collective-permute-start | bytes 12296 | tf_op jit(solution)/shard_map/ppermute | solution.py:362
  35.9 3.9 %col_guess.1 = (bf16[128,2048]{1,0:T(8,128)(2,1)S(1)}, bf16[128,2048]{1,0:T(8,128)(2,1)S(1)}, bf16[1024,128]{1,0:T(8,128)(2,1)S(1)}, f32[1,2048]{1,0:T(1,128)S(1)}, f32[1,2048]{1,0:T(1,128)S(1)}) custom-call(bf16[1024,128]{1,0:T(8,128)(2,1)S(1)} %get-tuple-element.34.a_ref, f32[8,128]{1,0:T(8,128)S(1)} %get-tuple-element.35.r_ref, ...), custom_call_target="tpu_custom_call" | custom-call | flops 1073741824 | bytes 2000000 | tf_op jit(solution)/shard_map/col_guess/pallas_call | solution.py:346
  39.8 2.3 %far_col_lse.3 = (f32[1,2048]{1,0:T(1,128)S(1)}, f32[8,128]{1,0:T(8,128)}, bf16[1024,128]{1,0:T(8,128)(2,1)S(1)}) custom-call(bf16[1024,128]{1,0:T(8,128)(2,1)S(1)} %get-tuple-element.34.a_ref, f32[8,128]{1,0:T(8,128)S(1)} %get-tuple-element.35.r_ref, f32[8,128]{1,0:T(8,128)S(1)} %bitcast.22, f32[8,128]{1,0:T(8,128)S(1)} %log_add_fusion.8.one_ref, ...), custom_call_target="tpu_custom_call" | custom-call | flops 536870912 | bytes 2000000 | tf_op jit(solution)/shard_map/far_col_lse/pallas_call | solution.py:346
  42.1 1.8 %collective-permute-start.3 = (f32[1,2048]{1,0:T(1,128)S(1)}, f32[1,2048]{1,0:T(1,128)S(1)}, u32[]{:S(2)}, u32[]{:S(2)}) collective-permute-start(f32[1,2048]{1,0:T(1,128)S(1)} %get-tuple-element.50.far_guess_ref.guess_ref), channel_id=1, source_target_pairs={{0,4},{4,0},{8,12},{12,8},{16,20},{20,16},{24,28},{28,24},{32,36},... | collective-permute-start | bytes 24584 | tf_op jit(solution)/shard_map/ppermute | solution.py:362
  43.8 1.6 %near_col_lse.3.near_guess_ref.guess_ref = f32[1,2048]{1,0:T(1,128)S(1)} custom-call(bf16[1024,128]{1,0:T(8,128)(2,1)S(1)} %get-tuple-element.47.left_ref, bf16[128,2048]{1,0:T(8,128)(2,1)S(1)} %get-tuple-element.36.near_b_ref.b_ref, f32[1,2048]{1,0:T(1,128)S(1)} %get-tuple-element.37.near_c_ref.c_ref, bf16[128,2048]{1,0:T(8,128)(2,1)S(1)} %get-tuple-element.48.ready_ref, ...), custom_call_target="tpu_custom_call" | custom-call | flops 536870912 | bytes 2000000 | tf_op jit(solution)/shard_map/near_col_lse/pallas_call | solution.py:346
  45.5 12.0 %all_to_all.21 = f32[32,16,128]{2,1,0:T(8,128)S(1)} all-to-all(f32[32,16,128]{2,1,0:T(8,128)S(1)} %broadcast_in_dim.21), channel_id=1, replica_groups={{0,8,16,24,32,40,48,56,64,72,80,88,96,104,112,120,128,136,144,152,160,1..., dimensions={0} | all-to-all | bytes 524288 | tf_op jit(solution)/shard_map/all_to_all | solution.py:374
  57.6 0.1 exponential_reduce_fusion.2
  57.7 1.7 %collective-permute-start.4 = (f32[1,2048]{1,0:T(1,128)S(1)}, f32[1,2048]{1,0:T(1,128)S(1)}, u32[]{:S(2)}, u32[]{:S(2)}) collective-permute-start(f32[1,2048]{1,0:T(1,128)S(1)} %bitcast.11), channel_id=1, source_target_pairs={{0,4},{4,0},{8,12},{12,8},{16,20},{20,16},{24,28},{28,24},{32,36},... | collective-permute-start | bytes 24584 | tf_op jit(solution)/shard_map/ppermute | solution.py:362
  59.3 1.5 %near_row_lse.2.acc_ref = f32[1024,128]{1,0:T(8,128)S(1)} custom-call(bf16[128,2048]{1,0:T(8,128)(2,1)S(1)} %get-tuple-element.36.near_b_ref.b_ref, f32[1,2048]{1,0:T(1,128)S(1)} %get-tuple-element.37.near_c_ref.c_ref, f32[1,2048]{1,0:T(1,128)S(1)} %get-tuple-element.38.near_w_ref.w_ref, f32[1,2048]{1,0:T(1,128)S(1)} %bitcast.12, ...), custom_call_target="tpu_custom_call" | custom-call | flops 536870912 | bytes 2000000 | tf_op jit(solution)/shard_map/near_row_lse/pallas_call | solution.py:346
  60.9 1.5 %row_lse.2.lse_ref.guess_ref = f32[8,128]{1,0:T(8,128)S(1)} custom-call(bf16[1024,128]{1,0:T(8,128)(2,1)S(1)} %get-tuple-element.34.a_ref, f32[8,128]{1,0:T(8,128)S(1)} %get-tuple-element.35.r_ref, bf16[128,2048]{1,0:T(8,128)(2,1)S(1)} %get-tuple-element.36.near_b_ref.b_ref, f32[1,2048]{1,0:T(1,128)S(1)} %get-tuple-element.37.near_c_ref.c_ref, ...), custom_call_target="tpu_custom_call" | custom-call | flops 536870912 | bytes 2000000 | tf_op jit(solution)/shard_map/row_lse/pallas_call | solution.py:346
  62.4 1.3 collective-permute-start.5
  63.7 2.2 %collective-permute-done.5 = f32[8,128]{1,0:T(8,128)S(1)} collective-permute-done((f32[8,128]{1,0:T(8,128)S(1)}, f32[8,128]{1,0:T(8,128)S(1)}, u32[]{:S(2)}, u32[]{:S(2)}) %collective-permute-start.5) | collective-permute-done | bytes 4128 | tf_op jit(solution)/shard_map/ppermute | solution.py:362
  65.9 1.6 %collective-permute-start.6 = (f32[8,128]{1,0:T(8,128)S(1)}, f32[8,128]{1,0:T(8,128)S(1)}, u32[]{:S(2)}, u32[]{:S(2)}) collective-permute-start(f32[8,128]{1,0:T(8,128)S(1)} %log_add_fusion.7.one_ref), channel_id=1, source_target_pairs={{0,3},{1,2},{2,1},{3,0},{4,7},{5,6},{6,5},{7,4},{8,11},{9,10},{10,... | collective-permute-start | bytes 12296 | tf_op jit(solution)/shard_map/ppermute | solution.py:362
  67.5 0.2 prepare.2
  67.7 2.8 %collective-permute-done.6.two_ref = f32[8,128]{1,0:T(8,128)S(1)} collective-permute-done((f32[8,128]{1,0:T(8,128)S(1)}, f32[8,128]{1,0:T(8,128)S(1)}, u32[]{:S(2)}, u32[]{:S(2)}) %collective-permute-start.6) | collective-permute-done | bytes 4128 | tf_op jit(solution)/shard_map/ppermute | solution.py:362
  70.5 2.3 %far_col_lse.4 = (f32[1,2048]{1,0:T(1,128)S(1)}, f32[8,128]{1,0:T(8,128)}, bf16[1024,128]{1,0:T(8,128)(2,1)S(1)}) custom-call(bf16[1024,128]{1,0:T(8,128)(2,1)S(1)} %get-tuple-element.34.a_ref, f32[8,128]{1,0:T(8,128)S(1)} %get-tuple-element.35.r_ref, f32[8,128]{1,0:T(8,128)S(1)} %bitcast.23, f32[8,128]{1,0:T(8,128)S(1)} %log_add_fusion.7.one_ref, ...), custom_call_target="tpu_custom_call" | custom-call | flops 536870912 | bytes 2000000 | tf_op jit(solution)/shard_map/far_col_lse/pallas_call | solution.py:346
  72.8 2.3 %collective-permute-start.7 = (f32[1,2048]{1,0:T(1,128)S(1)}, f32[1,2048]{1,0:T(1,128)S(1)}, u32[]{:S(2)}, u32[]{:S(2)}) collective-permute-start(f32[1,2048]{1,0:T(1,128)S(1)} %get-tuple-element.56.far_guess_ref.guess_ref), channel_id=1, source_target_pairs={{0,4},{4,0},{8,12},{12,8},{16,20},{20,16},{24,28},{28,24},{32,36},... | collective-permute-start | bytes 24584 | tf_op jit(solution)/shard_map/ppermute | solution.py:362
  75.1 1.6 %near_col_lse.4.near_guess_ref.guess_ref = f32[1,2048]{1,0:T(1,128)S(1)} custom-call(bf16[1024,128]{1,0:T(8,128)(2,1)S(1)} %get-tuple-element.54.left_ref, bf16[128,2048]{1,0:T(8,128)(2,1)S(1)} %get-tuple-element.36.near_b_ref.b_ref, f32[1,2048]{1,0:T(1,128)S(1)} %get-tuple-element.37.near_c_ref.c_ref, bf16[128,2048]{1,0:T(8,128)(2,1)S(1)} %get-tuple-element.55.ready_ref, ...), custom_call_target="tpu_custom_call" | custom-call | flops 536870912 | bytes 2000000 | tf_op jit(solution)/shard_map/near_col_lse/pallas_call | solution.py:346
  76.8 12.1 %all_to_all.22 = f32[32,16,128]{2,1,0:T(8,128)S(1)} all-to-all(f32[32,16,128]{2,1,0:T(8,128)S(1)} %broadcast_in_dim.22), channel_id=1, replica_groups={{0,8,16,24,32,40,48,56,64,72,80,88,96,104,112,120,128,136,144,152,160,1..., dimensions={0} | all-to-all | bytes 524288 | tf_op jit(solution)/shard_map/all_to_all | solution.py:374
  88.9 0.1 exponential_reduce_fusion.1
  89.0 1.5 %collective-permute-start.8 = (f32[1,2048]{1,0:T(1,128)S(1)}, f32[1,2048]{1,0:T(1,128)S(1)}, u32[]{:S(2)}, u32[]{:S(2)}) collective-permute-start(f32[1,2048]{1,0:T(1,128)S(1)} %bitcast.14), channel_id=1, source_target_pairs={{0,4},{4,0},{8,12},{12,8},{16,20},{20,16},{24,28},{28,24},{32,36},... | collective-permute-start | bytes 24584 | tf_op jit(solution)/shard_map/ppermute | solution.py:362
  90.5 1.5 %near_row_lse.3.acc_ref = f32[1024,128]{1,0:T(8,128)S(1)} custom-call(bf16[128,2048]{1,0:T(8,128)(2,1)S(1)} %get-tuple-element.36.near_b_ref.b_ref, f32[1,2048]{1,0:T(1,128)S(1)} %get-tuple-element.37.near_c_ref.c_ref, f32[1,2048]{1,0:T(1,128)S(1)} %get-tuple-element.38.near_w_ref.w_ref, f32[1,2048]{1,0:T(1,128)S(1)} %bitcast.15, ...), custom_call_target="tpu_custom_call" | custom-call | flops 536870912 | bytes 2000000 | tf_op jit(solution)/shard_map/near_row_lse/pallas_call | solution.py:346
  92.0 1.5 %row_lse.3.lse_ref = f32[8,128]{1,0:T(8,128)S(1)} custom-call(bf16[1024,128]{1,0:T(8,128)(2,1)S(1)} %get-tuple-element.34.a_ref, f32[8,128]{1,0:T(8,128)S(1)} %get-tuple-element.35.r_ref, bf16[128,2048]{1,0:T(8,128)(2,1)S(1)} %get-tuple-element.36.near_b_ref.b_ref, f32[1,2048]{1,0:T(1,128)S(1)} %get-tuple-element.37.near_c_ref.c_ref, ...), custom_call_target="tpu_custom_call" | custom-call | flops 536870912 | bytes 2000000 | tf_op jit(solution)/shard_map/row_lse/pallas_call | solution.py:346
  93.5 1.3 collective-permute-start.9
  94.8 2.2 %collective-permute-done.9 = f32[8,128]{1,0:T(8,128)S(1)} collective-permute-done((f32[8,128]{1,0:T(8,128)S(1)}, f32[8,128]{1,0:T(8,128)S(1)}, u32[]{:S(2)}, u32[]{:S(2)}) %collective-permute-start.9) | collective-permute-done | bytes 4128 | tf_op jit(solution)/shard_map/ppermute | solution.py:362
  97.0 1.9 %collective-permute-start.10 = (f32[8,128]{1,0:T(8,128)S(1)}, f32[8,128]{1,0:T(8,128)S(1)}, u32[]{:S(2)}, u32[]{:S(2)}) collective-permute-start(f32[8,128]{1,0:T(8,128)S(1)} %log_add_fusion.6.one_ref), channel_id=1, source_target_pairs={{0,3},{1,2},{2,1},{3,0},{4,7},{5,6},{6,5},{7,4},{8,11},{9,10},{10,... | collective-permute-start | bytes 12296 | tf_op jit(solution)/shard_map/ppermute | solution.py:362
  98.9 0.1 prepare.3
  99.0 2.9 %collective-permute-done.10.two_ref = f32[8,128]{1,0:T(8,128)S(1)} collective-permute-done((f32[8,128]{1,0:T(8,128)S(1)}, f32[8,128]{1,0:T(8,128)S(1)}, u32[]{:S(2)}, u32[]{:S(2)}) %collective-permute-start.10) | collective-permute-done | bytes 4128 | tf_op jit(solution)/shard_map/ppermute | solution.py:362
  101.9 2.3 %far_col_lse.5 = (f32[1,2048]{1,0:T(1,128)S(1)}, f32[8,128]{1,0:T(8,128)}, bf16[1024,128]{1,0:T(8,128)(2,1)S(1)}) custom-call(bf16[1024,128]{1,0:T(8,128)(2,1)S(1)} %get-tuple-element.34.a_ref, f32[8,128]{1,0:T(8,128)S(1)} %get-tuple-element.35.r_ref, f32[8,128]{1,0:T(8,128)S(1)} %bitcast.24, f32[8,128]{1,0:T(8,128)S(1)} %log_add_fusion.6.one_ref, ...), custom_call_target="tpu_custom_call" | custom-call | flops 536870912 | bytes 2000000 | tf_op jit(solution)/shard_map/far_col_lse/pallas_call | solution.py:346
  104.2 2.3 %collective-permute-start.11 = (f32[1,2048]{1,0:T(1,128)S(1)}, f32[1,2048]{1,0:T(1,128)S(1)}, u32[]{:S(2)}, u32[]{:S(2)}) collective-permute-start(f32[1,2048]{1,0:T(1,128)S(1)} %get-tuple-element.62), channel_id=1, source_target_pairs={{0,4},{4,0},{8,12},{12,8},{16,20},{20,16},{24,28},{28,24},{32,36},... | collective-permute-start | bytes 24584 | tf_op jit(solution)/shard_map/ppermute | solution.py:362
  106.5 1.6 %near_col_lse.5 = f32[1,2048]{1,0:T(1,128)S(1)} custom-call(bf16[1024,128]{1,0:T(8,128)(2,1)S(1)} %get-tuple-element.60.left_ref, bf16[128,2048]{1,0:T(8,128)(2,1)S(1)} %get-tuple-element.36.near_b_ref.b_ref, f32[1,2048]{1,0:T(1,128)S(1)} %get-tuple-element.37.near_c_ref.c_ref, bf16[128,2048]{1,0:T(8,128)(2,1)S(1)} %get-tuple-element.61.ready_ref, ...), custom_call_target="tpu_custom_call" | custom-call | flops 536870912 | bytes 2000000 | tf_op jit(solution)/shard_map/near_col_lse/pallas_call | solution.py:346
  108.1 0.7 broadcast_in_dim.23
  108.9 3.9 %all-to-all-start.3 = ((f32[32,16,128]{2,1,0:T(8,128)}), f32[32,16,128]{2,1,0:T(8,128)S(1)}, u32[]{:S(2)}, u32[]{:S(2)}) async-start(f32[32,16,128]{2,1,0:T(8,128)} %broadcast_in_dim.23), calls=%async_computation.3 | async-start | bytes 524288 | tf_op jit(solution)/shard_map/all_to_all | solution.py:374
  112.8 9.3 %all-to-all-done.3 = f32[32,16,128]{2,1,0:T(8,128)S(1)} async-done(((f32[32,16,128]{2,1,0:T(8,128)}), f32[32,16,128]{2,1,0:T(8,128)S(1)}, u32[]{:S(2)}, u32[]{:S(2)}) %all-to-all-start.3) | async-done | bytes 262176 | tf_op jit(solution)/shard_map/all_to_all | solution.py:374
  122.1 0.1 exponential_reduce_fusion
  122.2 1.1 collective-permute-start.12
  123.3 1.8 %near_plan.1 = (f32[512,128]{1,0:T(8,128)S(1)}, f32[512,64]{1,0:T(8,128)S(1)}) custom-call(bf16[1024,128]{1,0:T(8,128)(2,1)S(1)} %get-tuple-element.60.left_ref, bf16[128,2048]{1,0:T(8,128)(2,1)S(1)} %get-tuple-element.36.near_b_ref.b_ref, f32[1,2048]{1,0:T(1,128)S(1)} %get-tuple-element.37.near_c_ref.c_ref, ...), custom_call_target="tpu_custom_call" | custom-call | flops 536870912 | bytes 2000000 | tf_op jit(solution)/shard_map/near_plan/pallas_call | solution.py:346
  125.1 1.7 %first_plan.1 = bf16[64,512]{1,0:T(8,128)(2,1)S(1)} custom-call(bf16[64,1024]{1,0:T(8,128)(2,1)S(1)} %copy-done, bf16[1024,128]{1,0:T(8,128)(2,1)S(1)} %get-tuple-element.60.left_ref, bf16[128,2048]{1,0:T(8,128)(2,1)S(1)} %get-tuple-element.43.far_b_ref.b_ref, f32[1,2048]{1,0:T(1,128)S(1)} %get-tuple-element.44.far_c_ref.c_ref, ...), custom_call_target="tpu_custom_call" | custom-call | flops 536870912 | bytes 2000000 | tf_op jit(solution)/shard_map/first_plan/pallas_call | solution.py:346
  126.9 1.3 collective-permute-start.13
  128.1 3.7 %last_plan.1 = bf16[64,512]{1,0:T(8,128)(2,1)S(1)} custom-call(bf16[64,1024]{1,0:T(8,128)(2,1)S(1)} %copy-done, bf16[1024,128]{1,0:T(8,128)(2,1)S(1)} %get-tuple-element.60.left_ref, bf16[128,2048]{1,0:T(8,128)(2,1)S(1)} %get-tuple-element.36.near_b_ref.b_ref, f32[1,2048]{1,0:T(1,128)S(1)} %get-tuple-element.37.near_c_ref.c_ref, ...), custom_call_target="tpu_custom_call" | custom-call | flops 1073741824 | bytes 2000000 | tf_op jit(solution)/shard_map/last_plan/pallas_call | solution.py:346
  131.8 1.3 collective-permute-start.14
  133.1 0.1 collective-permute-done.13
  133.2 1.5 %collective-permute-start.15 = (bf16[64,512]{1,0:T(8,128)(2,1)S(1)}, bf16[64,512]{1,0:T(8,128)(2,1)S(1)}, u32[]{:S(2)}, u32[]{:S(2)}) collective-permute-start(bf16[64,512]{1,0:T(8,128)(2,1)S(1)} %reduce-precision_convert_fusion.1), channel_id=1, source_target_pairs={{0,3},{1,2},{2,1},{3,0},{4,7},{5,6},{6,5},{7,4},{8,11},{9,10},{10,... | collective-permute-start | bytes 196616 | tf_op jit(solution)/shard_map/ppermute | solution.py:362
  134.8 3.4 %collective-permute-done.14 = bf16[64,512]{1,0:T(8,128)(2,1)S(1)} collective-permute-done((bf16[64,512]{1,0:T(8,128)(2,1)S(1)}, bf16[64,512]{1,0:T(8,128)(2,1)S(1)}, u32[]{:S(2)}, u32[]{:S(2)}) %collective-permute-start.14) | collective-permute-done | bytes 65568 | tf_op jit(solution)/shard_map/ppermute | solution.py:362
  138.2 0.1 collective-permute-start.16
  138.3 0.6 dynamic-slice_multiply_fusion
  138.9 0.6 collective-permute-done.15
  139.6 4.0 %collective-permute-done.16 = bf16[64,512]{1,0:T(8,128)(2,1)S(1)} collective-permute-done((bf16[64,512]{1,0:T(8,128)(2,1)S(1)}, bf16[64,512]{1,0:T(8,128)(2,1)S(1)}, u32[]{:S(2)}, u32[]{:S(2)}) %collective-permute-start.16) | collective-permute-done | bytes 65568 | tf_op jit(solution)/shard_map/ppermute | solution.py:362
  143.5 0.7 convert_add_fusion
  (31 shorter events, 0.5 us)
Async XLA Ops:
  0.6 0.7 copy-start.3
  0.6 0.7 copy-start.4
  20.9 2.5 %copy-start = (bf16[64,1024]{1,0:T(8,128)(2,1)S(1)}, bf16[64,1024]{1,0:T(8,128)(2,1)}, u32[]{:S(2)}) copy-start(bf16[64,1024]{1,0:T(8,128)(2,1)} %emb_ref.5) | copy-start | bytes 393220
  20.9 2.5 %copy-start.1 = (f32[2,1024]{1,0:T(2,128)S(1)}, f32[2,1024]{1,0:T(2,128)}, u32[]{:S(2)}) copy-start(f32[2,1024]{1,0:T(2,128)} %pos_ref.1) | copy-start | bytes 24580
  21.3 4.3 %collective-permute-start = (bf16[68,2048]{1,0:T(8,128)(2,1)S(1)}, bf16[68,2048]{1,0:T(8,128)(2,1)S(1)}, u32[]{:S(2)}, u32[]{:S(2)}) collective-permute-start(bf16[68,2048]{1,0:T(8,128)(2,1)S(1)} %reshape.108.pack_ref), channel_id=1, source_target_pairs={{0,4},{4,0},{8,12},{12,8},{16,20},{20,16},{24,28},{28,24},{32,36},... | collective-permute-start | bytes 835592 | tf_op jit(solution)/shard_map/ppermute | solution.py:362
  27.2 4.1 %collective-permute-start.1 = (f32[8,128]{1,0:T(8,128)S(1)}, f32[8,128]{1,0:T(8,128)S(1)}, u32[]{:S(2)}, u32[]{:S(2)}) collective-permute-start(f32[8,128]{1,0:T(8,128)S(1)} %get-tuple-element.42.lse_ref.guess_ref), channel_id=1, source_target_pairs={{0,1},{1,0},{2,3},{3,2},{4,5},{5,4},{6,7},{7,6},{8,9},{9,8},{10,11... | collective-permute-start | bytes 12296 | tf_op jit(solution)/shard_map/ppermute | solution.py:362
  31.3 4.6 %copy-start.2 = (f32[1024]{0:T(1024)S(1)}, f32[1024]{0:T(1024)}, u32[]{:S(2)}) copy-start(f32[1024]{0:T(1024)} %param.8) | copy-start | bytes 12292
  31.3 8.4 %collective-permute-start.2 = (f32[8,128]{1,0:T(8,128)S(1)}, f32[8,128]{1,0:T(8,128)S(1)}, u32[]{:S(2)}, u32[]{:S(2)}) collective-permute-start(f32[8,128]{1,0:T(8,128)S(1)} %log_add_fusion.8.one_ref), channel_id=1, source_target_pairs={{0,3},{1,2},{2,1},{3,0},{4,7},{5,6},{6,5},{7,4},{8,11},{9,10},{10,... | collective-permute-start | bytes 12296 | tf_op jit(solution)/shard_map/ppermute | solution.py:362
  42.1 3.3 %collective-permute-start.3 = (f32[1,2048]{1,0:T(1,128)S(1)}, f32[1,2048]{1,0:T(1,128)S(1)}, u32[]{:S(2)}, u32[]{:S(2)}) collective-permute-start(f32[1,2048]{1,0:T(1,128)S(1)} %get-tuple-element.50.far_guess_ref.guess_ref), channel_id=1, source_target_pairs={{0,4},{4,0},{8,12},{12,8},{16,20},{20,16},{24,28},{28,24},{32,36},... | collective-permute-start | bytes 24584 | tf_op jit(solution)/shard_map/ppermute | solution.py:362
  57.7 3.2 %collective-permute-start.4 = (f32[1,2048]{1,0:T(1,128)S(1)}, f32[1,2048]{1,0:T(1,128)S(1)}, u32[]{:S(2)}, u32[]{:S(2)}) collective-permute-start(f32[1,2048]{1,0:T(1,128)S(1)} %bitcast.11), channel_id=1, source_target_pairs={{0,4},{4,0},{8,12},{12,8},{16,20},{20,16},{24,28},{28,24},{32,36},... | collective-permute-start | bytes 24584 | tf_op jit(solution)/shard_map/ppermute | solution.py:362
  62.4 3.5 %collective-permute-start.5 = (f32[8,128]{1,0:T(8,128)S(1)}, f32[8,128]{1,0:T(8,128)S(1)}, u32[]{:S(2)}, u32[]{:S(2)}) collective-permute-start(f32[8,128]{1,0:T(8,128)S(1)} %row_lse.2.lse_ref.guess_ref), channel_id=1, source_target_pairs={{0,1},{1,0},{2,3},{3,2},{4,5},{5,4},{6,7},{7,6},{8,9},{9,8},{10,11... | collective-permute-start | bytes 12296 | tf_op jit(solution)/shard_map/ppermute | solution.py:362
  65.9 4.7 %collective-permute-start.6 = (f32[8,128]{1,0:T(8,128)S(1)}, f32[8,128]{1,0:T(8,128)S(1)}, u32[]{:S(2)}, u32[]{:S(2)}) collective-permute-start(f32[8,128]{1,0:T(8,128)S(1)} %log_add_fusion.7.one_ref), channel_id=1, source_target_pairs={{0,3},{1,2},{2,1},{3,0},{4,7},{5,6},{6,5},{7,4},{8,11},{9,10},{10,... | collective-permute-start | bytes 12296 | tf_op jit(solution)/shard_map/ppermute | solution.py:362
  72.8 3.9 %collective-permute-start.7 = (f32[1,2048]{1,0:T(1,128)S(1)}, f32[1,2048]{1,0:T(1,128)S(1)}, u32[]{:S(2)}, u32[]{:S(2)}) collective-permute-start(f32[1,2048]{1,0:T(1,128)S(1)} %get-tuple-element.56.far_guess_ref.guess_ref), channel_id=1, source_target_pairs={{0,4},{4,0},{8,12},{12,8},{16,20},{20,16},{24,28},{28,24},{32,36},... | collective-permute-start | bytes 24584 | tf_op jit(solution)/shard_map/ppermute | solution.py:362
  89.0 3.0 %collective-permute-start.8 = (f32[1,2048]{1,0:T(1,128)S(1)}, f32[1,2048]{1,0:T(1,128)S(1)}, u32[]{:S(2)}, u32[]{:S(2)}) collective-permute-start(f32[1,2048]{1,0:T(1,128)S(1)} %bitcast.14), channel_id=1, source_target_pairs={{0,4},{4,0},{8,12},{12,8},{16,20},{20,16},{24,28},{28,24},{32,36},... | collective-permute-start | bytes 24584 | tf_op jit(solution)/shard_map/ppermute | solution.py:362
  93.5 3.5 %collective-permute-start.9 = (f32[8,128]{1,0:T(8,128)S(1)}, f32[8,128]{1,0:T(8,128)S(1)}, u32[]{:S(2)}, u32[]{:S(2)}) collective-permute-start(f32[8,128]{1,0:T(8,128)S(1)} %row_lse.3.lse_ref), channel_id=1, source_target_pairs={{0,1},{1,0},{2,3},{3,2},{4,5},{5,4},{6,7},{7,6},{8,9},{9,8},{10,11... | collective-permute-start | bytes 12296 | tf_op jit(solution)/shard_map/ppermute | solution.py:362
  97.0 4.9 %collective-permute-start.10 = (f32[8,128]{1,0:T(8,128)S(1)}, f32[8,128]{1,0:T(8,128)S(1)}, u32[]{:S(2)}, u32[]{:S(2)}) collective-permute-start(f32[8,128]{1,0:T(8,128)S(1)} %log_add_fusion.6.one_ref), channel_id=1, source_target_pairs={{0,3},{1,2},{2,1},{3,0},{4,7},{5,6},{6,5},{7,4},{8,11},{9,10},{10,... | collective-permute-start | bytes 12296 | tf_op jit(solution)/shard_map/ppermute | solution.py:362
  104.2 3.9 %collective-permute-start.11 = (f32[1,2048]{1,0:T(1,128)S(1)}, f32[1,2048]{1,0:T(1,128)S(1)}, u32[]{:S(2)}, u32[]{:S(2)}) collective-permute-start(f32[1,2048]{1,0:T(1,128)S(1)} %get-tuple-element.62), channel_id=1, source_target_pairs={{0,4},{4,0},{8,12},{12,8},{16,20},{20,16},{24,28},{28,24},{32,36},... | collective-permute-start | bytes 24584 | tf_op jit(solution)/shard_map/ppermute | solution.py:362
  108.9 13.2 %all-to-all-start.3 = ((f32[32,16,128]{2,1,0:T(8,128)}), f32[32,16,128]{2,1,0:T(8,128)S(1)}, u32[]{:S(2)}, u32[]{:S(2)}) async-start(f32[32,16,128]{2,1,0:T(8,128)} %broadcast_in_dim.23), calls=%async_computation.3 | async-start | bytes 524288 | tf_op jit(solution)/shard_map/all_to_all | solution.py:374
  122.2 2.9 %collective-permute-start.12 = (f32[1,2048]{1,0:T(1,128)S(1)}, f32[1,2048]{1,0:T(1,128)S(1)}, u32[]{:S(2)}, u32[]{:S(2)}) collective-permute-start(f32[1,2048]{1,0:T(1,128)S(1)} %bitcast.17), channel_id=1, source_target_pairs={{0,4},{4,0},{8,12},{12,8},{16,20},{20,16},{24,28},{28,24},{32,36},... | collective-permute-start | bytes 24584 | tf_op jit(solution)/shard_map/ppermute | solution.py:362
  126.9 6.4 %collective-permute-start.13 = (bf16[64,512]{1,0:T(8,128)(2,1)S(1)}, bf16[64,512]{1,0:T(8,128)(2,1)S(1)}, u32[]{:S(2)}, u32[]{:S(2)}) collective-permute-start(bf16[64,512]{1,0:T(8,128)(2,1)S(1)} %first_plan.1), channel_id=1, source_target_pairs={{0,1},{1,0},{2,3},{3,2},{4,5},{5,4},{6,7},{7,6},{8,9},{9,8},{10,11... | collective-permute-start | bytes 196616 | tf_op jit(solution)/shard_map/ppermute | solution.py:362
  131.8 6.4 %collective-permute-start.14 = (bf16[64,512]{1,0:T(8,128)(2,1)S(1)}, bf16[64,512]{1,0:T(8,128)(2,1)S(1)}, u32[]{:S(2)}, u32[]{:S(2)}) collective-permute-start(bf16[64,512]{1,0:T(8,128)(2,1)S(1)} %last_plan.1), channel_id=1, source_target_pairs={{0,1},{1,0},{2,3},{3,2},{4,5},{5,4},{6,7},{7,6},{8,9},{9,8},{10,11... | collective-permute-start | bytes 196616 | tf_op jit(solution)/shard_map/ppermute | solution.py:362
  133.2 6.3 %collective-permute-start.15 = (bf16[64,512]{1,0:T(8,128)(2,1)S(1)}, bf16[64,512]{1,0:T(8,128)(2,1)S(1)}, u32[]{:S(2)}, u32[]{:S(2)}) collective-permute-start(bf16[64,512]{1,0:T(8,128)(2,1)S(1)} %reduce-precision_convert_fusion.1), channel_id=1, source_target_pairs={{0,3},{1,2},{2,1},{3,0},{4,7},{5,6},{6,5},{7,4},{8,11},{9,10},{10,... | collective-permute-start | bytes 196616 | tf_op jit(solution)/shard_map/ppermute | solution.py:362
  138.2 5.3 %collective-permute-start.16 = (bf16[64,512]{1,0:T(8,128)(2,1)S(1)}, bf16[64,512]{1,0:T(8,128)(2,1)S(1)}, u32[]{:S(2)}, u32[]{:S(2)}) collective-permute-start(bf16[64,512]{1,0:T(8,128)(2,1)S(1)} %reduce-precision_convert_fusion), channel_id=1, source_target_pairs={{0,3},{1,2},{2,1},{3,0},{4,7},{5,6},{6,5},{7,4},{8,11},{9,10},{10,... | collective-permute-start | bytes 196616 | tf_op jit(solution)/shard_map/ppermute | solution.py:362

commit v4 on v3

--- a/solution.py
+++ b/solution.py
@@ -320,13 +320,26 @@
     plan_finish(emb_ref, 0, mass_s, pull_s, out_ref)
 
 
-def last_plan_kernel(emb_ref, left_ref, near_b_ref, near_c_ref, near_w_ref, near_lse_ref, b_ref, c_ref, w_ref, lse_ref, out_ref, b_s, mass_s, pull_s):
+def own_piece(lse_ref, g_ref):
+    piece = g_ref.shape[1]
+    own = lax.shift_right_logical(lax.axis_index("src"), 1) * piece
+    lane = lax.broadcasted_iota(jnp.int32, lse_ref.shape, 1) - own
+    kept = jnp.where(jnp.logical_and(lane >= 0, lane < piece), lse_ref[...], 0.0)
+    kept = folded(kept, jnp.add)
+    total = kept[:, 0:piece]
+    for at in range(piece, 128, piece):
+        total += kept[:, at : at + piece]
+    g_ref[...] = -LAM * EPS * total
+
+
+def last_plan_kernel(emb_ref, left_ref, near_b_ref, near_c_ref, near_w_ref, near_lse_ref, b_ref, c_ref, w_ref, lse_ref, out_ref, g_ref, b_s, mass_s, pull_s):
+    own_piece(near_lse_ref, g_ref)
     mass_s[...] = jnp.zeros_like(mass_s)
     pull_s[...] = jnp.zeros_like(pull_s)
     begin = emb_ref.shape[1] - out_ref.shape[1]
     left = left_ref.at[begin : emb_ref.shape[1], :]
-    plan_pass(left, near_b_ref, near_c_ref, near_w_ref, near_lse_ref, b_s, mass_s, pull_s, PLAN)
-    plan_pass(left, b_ref, c_ref, w_ref, lse_ref, b_s, mass_s, pull_s, PLAN)
+    plan_pass(left, near_b_ref, near_c_ref, near_w_ref, near_lse_ref, b_s, mass_s, pull_s, 2 * PLAN)
+    plan_pass(left, b_ref, c_ref, w_ref, lse_ref, b_s, mass_s, pull_s, 2 * PLAN)
     plan_finish(emb_ref, begin, mass_s, pull_s, out_ref)
 
 
@@ -442,8 +455,6 @@
         top = jnp.max(col, axis=0)
         col = (top + jnp.log(jnp.sum(jnp.exp(col - top), axis=0))).reshape(1, half)
         far_col = swapped(col, "src", 1)
-    begin = lax.axis_index("src") // 2 * piece
-    g_own = -LAM * EPS * lax.dynamic_slice_in_dim(col[0], begin, piece, 0)
     part = rows // 2
     sums_like = (f32(part, 128), f32(part, EMB))
     sums = call(
@@ -457,14 +468,14 @@
         flops=pass_flops,
     )
     grads = [exchanged(grad, rounded_sum)]
-    grad = call(
-        last_plan_kernel, bf16(EMB, part), (right_like, *sums_like), "last_plan",
+    grad, g_own = call(
+        last_plan_kernel, (bf16(EMB, part), f32(1, piece)), (right_like, *sums_like), "last_plan",
         src_emb, left, *near, col, *far, far_col,
         flops=2 * pass_flops,
     )
     grads.append(exchanged(grad, rounded_sum))
     first, second = (jnp.concatenate(part, axis=1).astype(jnp.float32) for part in zip(*grads))
-    return f.reshape(rows), g_own, first + second
+    return f.reshape(rows), g_own[0], first + second
 
 
 def solution(mesh):

time: 145 us -> 143 us (0.986)
  blocking collectives: 42.4 us -> 54.4 us
  waiting for transfers between devices: 28.6 us -> 20.4 us
  starting transfers between devices: 34.6 us -> 30.5 us
    all_to_all x3 -> x4, blocking collectives: 42.4 us -> 54.4 us  [spread(): lax.all_to_all(block, 'src', 0, 0, axis_index_groups=groups, tiled=True)]
    all_to_all x1 -> x0, waiting for transfers between devices: 9.34 us -> none  [spread(): lax.all_to_all(block, 'src', 0, 0, axis_index_groups=groups, tiled=True)]
    all_to_all x1 -> x0, starting transfers between devices: 3.87 us -> none  [spread(): lax.all_to_all(block, 'src', 0, 0, axis_index_groups=groups, tiled=True)]
  transfers between devices with their start and end apart: 18 -> 17, of which waited for: 10 -> 9; matrix products, arithmetic and copies ran while one was open for 0% -> 0% of each run, Pallas kernels for 14% -> 13%
where the time goes in v4:
time: 143 us; the launch traced here: 142 us
  blocking collectives  54.4 us (38%)
  Pallas kernels  32.3 us (23%)
  starting transfers between devices  30.5 us (21%)
  waiting for transfers between devices  20.4 us (14%)
  other arithmetic  1.98 us (1%)
  local copies, waits for them, and re-layouts  1.75 us (1%)
    all_to_all x4, blocking collectives, spread(): lax.all_to_all(block, 'src', 0, 0, axis_index_groups=groups, tiled=True)  54.4 us
    pallas_call x18, Pallas kernels, call(): pl.pallas_call(kernel, out_shape=out_shape, scratch_shapes=[pltpu.VMEM(li...  32.3 us
    ppermute x17, starting transfers between devices, swapped(): lax.ppermute(value, axis, [(k, k ^ mask) for k in range(lax.axis_size(axi...  30.5 us
    ppermute x17, waiting for transfers between devices, swapped(): lax.ppermute(value, axis, [(k, k ^ mask) for k in range(lax.axis_size(axi...  20.4 us
  transfers between devices with their start and end apart: 17, of which 9 were waited for; matrix products, arithmetic and copies ran while one was open for 0% of the time, Pallas kernels for 13%

profile of v4, /device:TPU:1, one launch (start us, length us, event | category | flops | bytes accessed | tf_op | source)
XLA Modules:
  0.0 142.4 jit_solution(5236901751169194208)
XLA Ops:
  0.7 0.6 copy-done.3
  1.3 0.0 copy-done.4
  1.3 0.7 pad_maximum_fusion
  2.0 0.1 reshape.102
  2.2 18.2 %all_to_all.20 = bf16[32,34,128]{2,1,0:T(8,128)(2,1)S(1)} all-to-all(bf16[32,34,128]{2,1,0:T(8,128)(2,1)S(1)} %broadcast_in_dim.20), channel_id=1, replica_groups={{0,8,16,24,32,40,48,56,64,72,80,88,96,104,112,120,128,136,144,152,160,1..., dimensions={0} | all-to-all | bytes 557056 | tf_op jit(solution)/shard_map/all_to_all | solution.py:387
  20.4 0.4 reshape.103
  20.8 0.1 copy.10
  20.9 0.0 copy-start
  20.9 0.0 copy-start.1
  20.9 0.4 reshape.104.pack_ref
  21.3 2.0 %collective-permute-start = (bf16[68,2048]{1,0:T(8,128)(2,1)S(1)}, bf16[68,2048]{1,0:T(8,128)(2,1)S(1)}, u32[]{:S(2)}, u32[]{:S(2)}) collective-permute-start(bf16[68,2048]{1,0:T(8,128)(2,1)S(1)} %reshape.104.pack_ref), channel_id=1, source_target_pairs={{0,4},{4,0},{8,12},{12,8},{16,20},{20,16},{24,28},{28,24},{32,36},... | collective-permute-start | bytes 835592 | tf_op jit(solution)/shard_map/ppermute | solution.py:375
  23.4 2.2 %static_parts.1 = (bf16[1024,128]{1,0:T(8,128)(2,1)S(1)}, f32[8,128]{1,0:T(8,128)S(1)}, bf16[128,2048]{1,0:T(8,128)(2,1)S(1)}, f32[1,2048]{1,0:T(1,128)S(1)}, f3...) custom-call(bf16[64,1024]{1,0:T(8,128)(2,1)S(1)} %copy-done, ...), custom_call_target="tpu_custom_call" | custom-call | flops 536870912 | bytes 2000000 | tf_op jit(solution)/shard_map/static_parts/pallas_call | solution.py:359
  25.6 0.0 collective-permute-done.pack_ref
  25.6 1.6 %first_row_lse.1 = (f32[8,128]{1,0:T(8,128)S(1)}, bf16[128,2048]{1,0:T(8,128)(2,1)S(1)}, f32[1,2048]{1,0:T(1,128)S(1)}, f32[1,2048]{1,0:T(1,128)S(1)}) custom-call(bf16[1024,128]{1,0:T(8,128)(2,1)S(1)} %get-tuple-element.36.a_ref, f32[8,128]{1,0:T(8,128)S(1)} %get-tuple-element.37.r_ref, bf16[128,2048]{1,0:T(8,128)(2,1)S(1)} %get-tuple-element.38.near_b_ref.b_ref, ...), custom_call_target="tpu_custom_call" | custom-call | flops 536870912 | bytes 2000000 | tf_op jit(solution)/shard_map/first_row_lse/pallas_call | solution.py:359
  27.2 3.1 %collective-permute-start.1 = (f32[8,128]{1,0:T(8,128)S(1)}, f32[8,128]{1,0:T(8,128)S(1)}, u32[]{:S(2)}, u32[]{:S(2)}) collective-permute-start(f32[8,128]{1,0:T(8,128)S(1)} %get-tuple-element.44.lse_ref.guess_ref), channel_id=1, source_target_pairs={{0,1},{1,0},{2,3},{3,2},{4,5},{5,4},{6,7},{7,6},{8,9},{9,8},{10,11... | collective-permute-start | bytes 12296 | tf_op jit(solution)/shard_map/ppermute | solution.py:375
  30.3 1.0 collective-permute-done.1
  31.3 0.0 copy-start.2
  31.3 4.6 %collective-permute-start.2 = (f32[8,128]{1,0:T(8,128)S(1)}, f32[8,128]{1,0:T(8,128)S(1)}, u32[]{:S(2)}, u32[]{:S(2)}) collective-permute-start(f32[8,128]{1,0:T(8,128)S(1)} %log_add_fusion.8.one_ref), channel_id=1, source_target_pairs={{0,3},{1,2},{2,1},{3,0},{4,7},{5,6},{6,5},{7,4},{8,11},{9,10},{10,... | collective-permute-start | bytes 12296 | tf_op jit(solution)/shard_map/ppermute | solution.py:375
  35.9 3.9 %col_guess.1 = (bf16[128,2048]{1,0:T(8,128)(2,1)S(1)}, bf16[128,2048]{1,0:T(8,128)(2,1)S(1)}, bf16[1024,128]{1,0:T(8,128)(2,1)S(1)}, f32[1,2048]{1,0:T(1,128)S(1)}, f32[1,2048]{1,0:T(1,128)S(1)}) custom-call(bf16[1024,128]{1,0:T(8,128)(2,1)S(1)} %get-tuple-element.36.a_ref, f32[8,128]{1,0:T(8,128)S(1)} %get-tuple-element.37.r_ref, ...), custom_call_target="tpu_custom_call" | custom-call | flops 1073741824 | bytes 2000000 | tf_op jit(solution)/shard_map/col_guess/pallas_call | solution.py:359
  39.8 2.3 %far_col_lse.3 = (f32[1,2048]{1,0:T(1,128)S(1)}, f32[8,128]{1,0:T(8,128)}, bf16[1024,128]{1,0:T(8,128)(2,1)S(1)}) custom-call(bf16[1024,128]{1,0:T(8,128)(2,1)S(1)} %get-tuple-element.36.a_ref, f32[8,128]{1,0:T(8,128)S(1)} %get-tuple-element.37.r_ref, f32[8,128]{1,0:T(8,128)S(1)} %bitcast.21, f32[8,128]{1,0:T(8,128)S(1)} %log_add_fusion.8.one_ref, ...), custom_call_target="tpu_custom_call" | custom-call | flops 536870912 | bytes 2000000 | tf_op jit(solution)/shard_map/far_col_lse/pallas_call | solution.py:359
  42.1 1.8 %collective-permute-start.3 = (f32[1,2048]{1,0:T(1,128)S(1)}, f32[1,2048]{1,0:T(1,128)S(1)}, u32[]{:S(2)}, u32[]{:S(2)}) collective-permute-start(f32[1,2048]{1,0:T(1,128)S(1)} %get-tuple-element.52.far_guess_ref.guess_ref), channel_id=1, source_target_pairs={{0,4},{4,0},{8,12},{12,8},{16,20},{20,16},{24,28},{28,24},{32,36},... | collective-permute-start | bytes 24584 | tf_op jit(solution)/shard_map/ppermute | solution.py:375
  43.8 1.6 %near_col_lse.3.near_guess_ref.guess_ref = f32[1,2048]{1,0:T(1,128)S(1)} custom-call(bf16[1024,128]{1,0:T(8,128)(2,1)S(1)} %get-tuple-element.49.left_ref, bf16[128,2048]{1,0:T(8,128)(2,1)S(1)} %get-tuple-element.38.near_b_ref.b_ref, f32[1,2048]{1,0:T(1,128)S(1)} %get-tuple-element.39.near_c_ref.c_ref, bf16[128,2048]{1,0:T(8,128)(2,1)S(1)} %get-tuple-element.50.ready_ref, ...), custom_call_target="tpu_custom_call" | custom-call | flops 536870912 | bytes 2000000 | tf_op jit(solution)/shard_map/near_col_lse/pallas_call | solution.py:359
  45.4 0.0 collective-permute-done.3
  45.5 12.0 %all_to_all.21 = f32[32,16,128]{2,1,0:T(8,128)S(1)} all-to-all(f32[32,16,128]{2,1,0:T(8,128)S(1)} %broadcast_in_dim.21), channel_id=1, replica_groups={{0,8,16,24,32,40,48,56,64,72,80,88,96,104,112,120,128,136,144,152,160,1..., dimensions={0} | all-to-all | bytes 524288 | tf_op jit(solution)/shard_map/all_to_all | solution.py:387
  57.6 0.1 exponential_reduce_fusion.2
  57.7 1.7 %collective-permute-start.4 = (f32[1,2048]{1,0:T(1,128)S(1)}, f32[1,2048]{1,0:T(1,128)S(1)}, u32[]{:S(2)}, u32[]{:S(2)}) collective-permute-start(f32[1,2048]{1,0:T(1,128)S(1)} %bitcast.11), channel_id=1, source_target_pairs={{0,4},{4,0},{8,12},{12,8},{16,20},{20,16},{24,28},{28,24},{32,36},... | collective-permute-start | bytes 24584 | tf_op jit(solution)/shard_map/ppermute | solution.py:375
  59.3 1.5 %near_row_lse.2.acc_ref = f32[1024,128]{1,0:T(8,128)S(1)} custom-call(bf16[128,2048]{1,0:T(8,128)(2,1)S(1)} %get-tuple-element.38.near_b_ref.b_ref, f32[1,2048]{1,0:T(1,128)S(1)} %get-tuple-element.39.near_c_ref.c_ref, f32[1,2048]{1,0:T(1,128)S(1)} %get-tuple-element.40.near_w_ref.w_ref, f32[1,2048]{1,0:T(1,128)S(1)} %bitcast.12, ...), custom_call_target="tpu_custom_call" | custom-call | flops 536870912 | bytes 2000000 | tf_op jit(solution)/shard_map/near_row_lse/pallas_call | solution.py:359
  60.9 1.5 %row_lse.2.lse_ref.guess_ref = f32[8,128]{1,0:T(8,128)S(1)} custom-call(bf16[1024,128]{1,0:T(8,128)(2,1)S(1)} %get-tuple-element.36.a_ref, f32[8,128]{1,0:T(8,128)S(1)} %get-tuple-element.37.r_ref, bf16[128,2048]{1,0:T(8,128)(2,1)S(1)} %get-tuple-element.38.near_b_ref.b_ref, f32[1,2048]{1,0:T(1,128)S(1)} %get-tuple-element.39.near_c_ref.c_ref, ...), custom_call_target="tpu_custom_call" | custom-call | flops 536870912 | bytes 2000000 | tf_op jit(solution)/shard_map/row_lse/pallas_call | solution.py:359
  62.4 1.3 collective-permute-start.5
  63.7 2.2 %collective-permute-done.5 = f32[8,128]{1,0:T(8,128)S(1)} collective-permute-done((f32[8,128]{1,0:T(8,128)S(1)}, f32[8,128]{1,0:T(8,128)S(1)}, u32[]{:S(2)}, u32[]{:S(2)}) %collective-permute-start.5) | collective-permute-done | bytes 4128 | tf_op jit(solution)/shard_map/ppermute | solution.py:375
  65.9 1.6 %collective-permute-start.6 = (f32[8,128]{1,0:T(8,128)S(1)}, f32[8,128]{1,0:T(8,128)S(1)}, u32[]{:S(2)}, u32[]{:S(2)}) collective-permute-start(f32[8,128]{1,0:T(8,128)S(1)} %log_add_fusion.7.one_ref), channel_id=1, source_target_pairs={{0,3},{1,2},{2,1},{3,0},{4,7},{5,6},{6,5},{7,4},{8,11},{9,10},{10,... | collective-permute-start | bytes 12296 | tf_op jit(solution)/shard_map/ppermute | solution.py:375
  67.5 0.2 prepare.2
  67.7 2.8 %collective-permute-done.6.two_ref = f32[8,128]{1,0:T(8,128)S(1)} collective-permute-done((f32[8,128]{1,0:T(8,128)S(1)}, f32[8,128]{1,0:T(8,128)S(1)}, u32[]{:S(2)}, u32[]{:S(2)}) %collective-permute-start.6) | collective-permute-done | bytes 4128 | tf_op jit(solution)/shard_map/ppermute | solution.py:375
  70.5 2.3 %far_col_lse.4 = (f32[1,2048]{1,0:T(1,128)S(1)}, f32[8,128]{1,0:T(8,128)}, bf16[1024,128]{1,0:T(8,128)(2,1)S(1)}) custom-call(bf16[1024,128]{1,0:T(8,128)(2,1)S(1)} %get-tuple-element.36.a_ref, f32[8,128]{1,0:T(8,128)S(1)} %get-tuple-element.37.r_ref, f32[8,128]{1,0:T(8,128)S(1)} %bitcast.22, f32[8,128]{1,0:T(8,128)S(1)} %log_add_fusion.7.one_ref, ...), custom_call_target="tpu_custom_call" | custom-call | flops 536870912 | bytes 2000000 | tf_op jit(solution)/shard_map/far_col_lse/pallas_call | solution.py:359
  72.8 2.3 %collective-permute-start.7 = (f32[1,2048]{1,0:T(1,128)S(1)}, f32[1,2048]{1,0:T(1,128)S(1)}, u32[]{:S(2)}, u32[]{:S(2)}) collective-permute-start(f32[1,2048]{1,0:T(1,128)S(1)} %get-tuple-element.58.far_guess_ref.guess_ref), channel_id=1, source_target_pairs={{0,4},{4,0},{8,12},{12,8},{16,20},{20,16},{24,28},{28,24},{32,36},... | collective-permute-start | bytes 24584 | tf_op jit(solution)/shard_map/ppermute | solution.py:375
  75.1 1.6 %near_col_lse.4.near_guess_ref.guess_ref = f32[1,2048]{1,0:T(1,128)S(1)} custom-call(bf16[1024,128]{1,0:T(8,128)(2,1)S(1)} %get-tuple-element.56.left_ref, bf16[128,2048]{1,0:T(8,128)(2,1)S(1)} %get-tuple-element.38.near_b_ref.b_ref, f32[1,2048]{1,0:T(1,128)S(1)} %get-tuple-element.39.near_c_ref.c_ref, bf16[128,2048]{1,0:T(8,128)(2,1)S(1)} %get-tuple-element.57.ready_ref, ...), custom_call_target="tpu_custom_call" | custom-call | flops 536870912 | bytes 2000000 | tf_op jit(solution)/shard_map/near_col_lse/pallas_call | solution.py:359
  76.8 12.1 %all_to_all.22 = f32[32,16,128]{2,1,0:T(8,128)S(1)} all-to-all(f32[32,16,128]{2,1,0:T(8,128)S(1)} %broadcast_in_dim.22), channel_id=1, replica_groups={{0,8,16,24,32,40,48,56,64,72,80,88,96,104,112,120,128,136,144,152,160,1..., dimensions={0} | all-to-all | bytes 524288 | tf_op jit(solution)/shard_map/all_to_all | solution.py:387
  88.9 0.1 exponential_reduce_fusion.1
  89.0 1.5 %collective-permute-start.8 = (f32[1,2048]{1,0:T(1,128)S(1)}, f32[1,2048]{1,0:T(1,128)S(1)}, u32[]{:S(2)}, u32[]{:S(2)}) collective-permute-start(f32[1,2048]{1,0:T(1,128)S(1)} %bitcast.14), channel_id=1, source_target_pairs={{0,4},{4,0},{8,12},{12,8},{16,20},{20,16},{24,28},{28,24},{32,36},... | collective-permute-start | bytes 24584 | tf_op jit(solution)/shard_map/ppermute | solution.py:375
  90.5 1.5 %near_row_lse.3.acc_ref = f32[1024,128]{1,0:T(8,128)S(1)} custom-call(bf16[128,2048]{1,0:T(8,128)(2,1)S(1)} %get-tuple-element.38.near_b_ref.b_ref, f32[1,2048]{1,0:T(1,128)S(1)} %get-tuple-element.39.near_c_ref.c_ref, f32[1,2048]{1,0:T(1,128)S(1)} %get-tuple-element.40.near_w_ref.w_ref, f32[1,2048]{1,0:T(1,128)S(1)} %bitcast.15, ...), custom_call_target="tpu_custom_call" | custom-call | flops 536870912 | bytes 2000000 | tf_op jit(solution)/shard_map/near_row_lse/pallas_call | solution.py:359
  92.0 1.5 %row_lse.3.lse_ref = f32[8,128]{1,0:T(8,128)S(1)} custom-call(bf16[1024,128]{1,0:T(8,128)(2,1)S(1)} %get-tuple-element.36.a_ref, f32[8,128]{1,0:T(8,128)S(1)} %get-tuple-element.37.r_ref, bf16[128,2048]{1,0:T(8,128)(2,1)S(1)} %get-tuple-element.38.near_b_ref.b_ref, f32[1,2048]{1,0:T(1,128)S(1)} %get-tuple-element.39.near_c_ref.c_ref, ...), custom_call_target="tpu_custom_call" | custom-call | flops 536870912 | bytes 2000000 | tf_op jit(solution)/shard_map/row_lse/pallas_call | solution.py:359
  93.5 1.3 collective-permute-start.9
  94.8 2.2 %collective-permute-done.9 = f32[8,128]{1,0:T(8,128)S(1)} collective-permute-done((f32[8,128]{1,0:T(8,128)S(1)}, f32[8,128]{1,0:T(8,128)S(1)}, u32[]{:S(2)}, u32[]{:S(2)}) %collective-permute-start.9) | collective-permute-done | bytes 4128 | tf_op jit(solution)/shard_map/ppermute | solution.py:375
  97.0 1.9 %collective-permute-start.10 = (f32[8,128]{1,0:T(8,128)S(1)}, f32[8,128]{1,0:T(8,128)S(1)}, u32[]{:S(2)}, u32[]{:S(2)}) collective-permute-start(f32[8,128]{1,0:T(8,128)S(1)} %log_add_fusion.6.one_ref), channel_id=1, source_target_pairs={{0,3},{1,2},{2,1},{3,0},{4,7},{5,6},{6,5},{7,4},{8,11},{9,10},{10,... | collective-permute-start | bytes 12296 | tf_op jit(solution)/shard_map/ppermute | solution.py:375
  98.9 0.1 prepare.3
  99.0 2.9 %collective-permute-done.10.two_ref = f32[8,128]{1,0:T(8,128)S(1)} collective-permute-done((f32[8,128]{1,0:T(8,128)S(1)}, f32[8,128]{1,0:T(8,128)S(1)}, u32[]{:S(2)}, u32[]{:S(2)}) %collective-permute-start.10) | collective-permute-done | bytes 4128 | tf_op jit(solution)/shard_map/ppermute | solution.py:375
  101.9 2.3 %far_col_lse.5 = (f32[1,2048]{1,0:T(1,128)S(1)}, f32[8,128]{1,0:T(8,128)}, bf16[1024,128]{1,0:T(8,128)(2,1)S(1)}) custom-call(bf16[1024,128]{1,0:T(8,128)(2,1)S(1)} %get-tuple-element.36.a_ref, f32[8,128]{1,0:T(8,128)S(1)} %get-tuple-element.37.r_ref, f32[8,128]{1,0:T(8,128)S(1)} %bitcast.23, f32[8,128]{1,0:T(8,128)S(1)} %log_add_fusion.6.one_ref, ...), custom_call_target="tpu_custom_call" | custom-call | flops 536870912 | bytes 2000000 | tf_op jit(solution)/shard_map/far_col_lse/pallas_call | solution.py:359
  104.2 2.3 %collective-permute-start.11 = (f32[1,2048]{1,0:T(1,128)S(1)}, f32[1,2048]{1,0:T(1,128)S(1)}, u32[]{:S(2)}, u32[]{:S(2)}) collective-permute-start(f32[1,2048]{1,0:T(1,128)S(1)} %get-tuple-element.64), channel_id=1, source_target_pairs={{0,4},{4,0},{8,12},{12,8},{16,20},{20,16},{24,28},{28,24},{32,36},... | collective-permute-start | bytes 24584 | tf_op jit(solution)/shard_map/ppermute | solution.py:375
  106.5 1.6 %near_col_lse.5 = f32[1,2048]{1,0:T(1,128)S(1)} custom-call(bf16[1024,128]{1,0:T(8,128)(2,1)S(1)} %get-tuple-element.62.left_ref, bf16[128,2048]{1,0:T(8,128)(2,1)S(1)} %get-tuple-element.38.near_b_ref.b_ref, f32[1,2048]{1,0:T(1,128)S(1)} %get-tuple-element.39.near_c_ref.c_ref, bf16[128,2048]{1,0:T(8,128)(2,1)S(1)} %get-tuple-element.63.ready_ref, ...), custom_call_target="tpu_custom_call" | custom-call | flops 536870912 | bytes 2000000 | tf_op jit(solution)/shard_map/near_col_lse/pallas_call | solution.py:359
  108.2 12.1 %all_to_all.23 = f32[32,16,128]{2,1,0:T(8,128)S(1)} all-to-all(f32[32,16,128]{2,1,0:T(8,128)S(1)} %broadcast_in_dim.23), channel_id=1, replica_groups={{0,8,16,24,32,40,48,56,64,72,80,88,96,104,112,120,128,136,144,152,160,1..., dimensions={0} | all-to-all | bytes 524288 | tf_op jit(solution)/shard_map/all_to_all | solution.py:387
  120.3 0.1 exponential_reduce_fusion
  120.4 1.5 %collective-permute-start.12 = (f32[1,2048]{1,0:T(1,128)S(1)}, f32[1,2048]{1,0:T(1,128)S(1)}, u32[]{:S(2)}, u32[]{:S(2)}) collective-permute-start(f32[1,2048]{1,0:T(1,128)S(1)} %bitcast.17), channel_id=1, source_target_pairs={{0,4},{4,0},{8,12},{12,8},{16,20},{20,16},{24,28},{28,24},{32,36},... | collective-permute-start | bytes 24584 | tf_op jit(solution)/shard_map/ppermute | solution.py:375
  121.9 1.8 %near_plan.1 = (f32[512,128]{1,0:T(8,128)S(1)}, f32[512,64]{1,0:T(8,128)S(1)}) custom-call(bf16[1024,128]{1,0:T(8,128)(2,1)S(1)} %get-tuple-element.62.left_ref, bf16[128,2048]{1,0:T(8,128)(2,1)S(1)} %get-tuple-element.38.near_b_ref.b_ref, f32[1,2048]{1,0:T(1,128)S(1)} %get-tuple-element.39.near_c_ref.c_ref, ...), custom_call_target="tpu_custom_call" | custom-call | flops 536870912 | bytes 2000000 | tf_op jit(solution)/shard_map/near_plan/pallas_call | solution.py:359
  123.7 1.7 %first_plan.1 = bf16[64,512]{1,0:T(8,128)(2,1)S(1)} custom-call(bf16[64,1024]{1,0:T(8,128)(2,1)S(1)} %copy-done, bf16[1024,128]{1,0:T(8,128)(2,1)S(1)} %get-tuple-element.62.left_ref, bf16[128,2048]{1,0:T(8,128)(2,1)S(1)} %get-tuple-element.45.far_b_ref.b_ref, f32[1,2048]{1,0:T(1,128)S(1)} %get-tuple-element.46.far_c_ref.c_ref, ...), custom_call_target="tpu_custom_call" | custom-call | flops 536870912 | bytes 2000000 | tf_op jit(solution)/shard_map/first_plan/pallas_call | solution.py:359
  125.4 1.3 collective-permute-start.13
  126.7 3.2 %last_plan.1 = (bf16[64,512]{1,0:T(8,128)(2,1)S(1)}, f32[1,64]{1,0:T(1,128)}) custom-call(bf16[64,1024]{1,0:T(8,128)(2,1)S(1)} %copy-done, bf16[1024,128]{1,0:T(8,128)(2,1)S(1)} %get-tuple-element.62.left_ref, bf16[128,2048]{1,0:T(8,128)(2,1)S(1)} %get-tuple-element.38.near_b_ref.b_ref, f32[1,2048]{1,0:T(1,128)S(1)} %get-tuple-element.39.near_c_ref.c_ref, ...), custom_call_target="tpu_custom_call" | custom-call | flops 1073741824 | bytes 2000000 | tf_op jit(solution)/shard_map/last_plan/pallas_call | solution.py:359
  129.9 1.2 collective-permute-start.14
  131.1 0.6 collective-permute-done.13
  131.8 1.0 collective-permute-start.15
  132.8 3.5 %collective-permute-done.14 = bf16[64,512]{1,0:T(8,128)(2,1)S(1)} collective-permute-done((bf16[64,512]{1,0:T(8,128)(2,1)S(1)}, bf16[64,512]{1,0:T(8,128)(2,1)S(1)}, u32[]{:S(2)}, u32[]{:S(2)}) %collective-permute-start.14) | collective-permute-done | bytes 65568 | tf_op jit(solution)/shard_map/ppermute | solution.py:375
  136.3 0.1 collective-permute-start.16
  136.4 0.9 collective-permute-done.15
  137.3 4.3 %collective-permute-done.16 = bf16[64,512]{1,0:T(8,128)(2,1)S(1)} collective-permute-done((bf16[64,512]{1,0:T(8,128)(2,1)S(1)}, bf16[64,512]{1,0:T(8,128)(2,1)S(1)}, u32[]{:S(2)}, u32[]{:S(2)}) %collective-permute-start.16) | collective-permute-done | bytes 65568 | tf_op jit(solution)/shard_map/ppermute | solution.py:375
  141.6 0.7 convert_add_fusion
  (29 shorter events, 0.5 us)
Async XLA Ops:
  0.6 0.7 copy-start.3
  0.6 0.7 copy-start.4
  20.9 2.5 %copy-start = (bf16[64,1024]{1,0:T(8,128)(2,1)S(1)}, bf16[64,1024]{1,0:T(8,128)(2,1)}, u32[]{:S(2)}) copy-start(bf16[64,1024]{1,0:T(8,128)(2,1)} %emb_ref.5) | copy-start | bytes 393220
  20.9 2.5 %copy-start.1 = (f32[2,1024]{1,0:T(2,128)S(1)}, f32[2,1024]{1,0:T(2,128)}, u32[]{:S(2)}) copy-start(f32[2,1024]{1,0:T(2,128)} %pos_ref.1) | copy-start | bytes 24580
  21.3 4.3 %collective-permute-start = (bf16[68,2048]{1,0:T(8,128)(2,1)S(1)}, bf16[68,2048]{1,0:T(8,128)(2,1)S(1)}, u32[]{:S(2)}, u32[]{:S(2)}) collective-permute-start(bf16[68,2048]{1,0:T(8,128)(2,1)S(1)} %reshape.104.pack_ref), channel_id=1, source_target_pairs={{0,4},{4,0},{8,12},{12,8},{16,20},{20,16},{24,28},{28,24},{32,36},... | collective-permute-start | bytes 835592 | tf_op jit(solution)/shard_map/ppermute | solution.py:375
  27.2 4.1 %collective-permute-start.1 = (f32[8,128]{1,0:T(8,128)S(1)}, f32[8,128]{1,0:T(8,128)S(1)}, u32[]{:S(2)}, u32[]{:S(2)}) collective-permute-start(f32[8,128]{1,0:T(8,128)S(1)} %get-tuple-element.44.lse_ref.guess_ref), channel_id=1, source_target_pairs={{0,1},{1,0},{2,3},{3,2},{4,5},{5,4},{6,7},{7,6},{8,9},{9,8},{10,11... | collective-permute-start | bytes 12296 | tf_op jit(solution)/shard_map/ppermute | solution.py:375
  31.3 4.6 %copy-start.2 = (f32[1024]{0:T(1024)S(1)}, f32[1024]{0:T(1024)}, u32[]{:S(2)}) copy-start(f32[1024]{0:T(1024)} %param.8) | copy-start | bytes 12292
  31.3 8.4 %collective-permute-start.2 = (f32[8,128]{1,0:T(8,128)S(1)}, f32[8,128]{1,0:T(8,128)S(1)}, u32[]{:S(2)}, u32[]{:S(2)}) collective-permute-start(f32[8,128]{1,0:T(8,128)S(1)} %log_add_fusion.8.one_ref), channel_id=1, source_target_pairs={{0,3},{1,2},{2,1},{3,0},{4,7},{5,6},{6,5},{7,4},{8,11},{9,10},{10,... | collective-permute-start | bytes 12296 | tf_op jit(solution)/shard_map/ppermute | solution.py:375
  42.1 3.3 %collective-permute-start.3 = (f32[1,2048]{1,0:T(1,128)S(1)}, f32[1,2048]{1,0:T(1,128)S(1)}, u32[]{:S(2)}, u32[]{:S(2)}) collective-permute-start(f32[1,2048]{1,0:T(1,128)S(1)} %get-tuple-element.52.far_guess_ref.guess_ref), channel_id=1, source_target_pairs={{0,4},{4,0},{8,12},{12,8},{16,20},{20,16},{24,28},{28,24},{32,36},... | collective-permute-start | bytes 24584 | tf_op jit(solution)/shard_map/ppermute | solution.py:375
  57.7 3.2 %collective-permute-start.4 = (f32[1,2048]{1,0:T(1,128)S(1)}, f32[1,2048]{1,0:T(1,128)S(1)}, u32[]{:S(2)}, u32[]{:S(2)}) collective-permute-start(f32[1,2048]{1,0:T(1,128)S(1)} %bitcast.11), channel_id=1, source_target_pairs={{0,4},{4,0},{8,12},{12,8},{16,20},{20,16},{24,28},{28,24},{32,36},... | collective-permute-start | bytes 24584 | tf_op jit(solution)/shard_map/ppermute | solution.py:375
  62.4 3.5 %collective-permute-start.5 = (f32[8,128]{1,0:T(8,128)S(1)}, f32[8,128]{1,0:T(8,128)S(1)}, u32[]{:S(2)}, u32[]{:S(2)}) collective-permute-start(f32[8,128]{1,0:T(8,128)S(1)} %row_lse.2.lse_ref.guess_ref), channel_id=1, source_target_pairs={{0,1},{1,0},{2,3},{3,2},{4,5},{5,4},{6,7},{7,6},{8,9},{9,8},{10,11... | collective-permute-start | bytes 12296 | tf_op jit(solution)/shard_map/ppermute | solution.py:375
  65.9 4.7 %collective-permute-start.6 = (f32[8,128]{1,0:T(8,128)S(1)}, f32[8,128]{1,0:T(8,128)S(1)}, u32[]{:S(2)}, u32[]{:S(2)}) collective-permute-start(f32[8,128]{1,0:T(8,128)S(1)} %log_add_fusion.7.one_ref), channel_id=1, source_target_pairs={{0,3},{1,2},{2,1},{3,0},{4,7},{5,6},{6,5},{7,4},{8,11},{9,10},{10,... | collective-permute-start | bytes 12296 | tf_op jit(solution)/shard_map/ppermute | solution.py:375
  72.8 3.9 %collective-permute-start.7 = (f32[1,2048]{1,0:T(1,128)S(1)}, f32[1,2048]{1,0:T(1,128)S(1)}, u32[]{:S(2)}, u32[]{:S(2)}) collective-permute-start(f32[1,2048]{1,0:T(1,128)S(1)} %get-tuple-element.58.far_guess_ref.guess_ref), channel_id=1, source_target_pairs={{0,4},{4,0},{8,12},{12,8},{16,20},{20,16},{24,28},{28,24},{32,36},... | collective-permute-start | bytes 24584 | tf_op jit(solution)/shard_map/ppermute | solution.py:375
  89.0 3.0 %collective-permute-start.8 = (f32[1,2048]{1,0:T(1,128)S(1)}, f32[1,2048]{1,0:T(1,128)S(1)}, u32[]{:S(2)}, u32[]{:S(2)}) collective-permute-start(f32[1,2048]{1,0:T(1,128)S(1)} %bitcast.14), channel_id=1, source_target_pairs={{0,4},{4,0},{8,12},{12,8},{16,20},{20,16},{24,28},{28,24},{32,36},... | collective-permute-start | bytes 24584 | tf_op jit(solution)/shard_map/ppermute | solution.py:375
  93.5 3.5 %collective-permute-start.9 = (f32[8,128]{1,0:T(8,128)S(1)}, f32[8,128]{1,0:T(8,128)S(1)}, u32[]{:S(2)}, u32[]{:S(2)}) collective-permute-start(f32[8,128]{1,0:T(8,128)S(1)} %row_lse.3.lse_ref), channel_id=1, source_target_pairs={{0,1},{1,0},{2,3},{3,2},{4,5},{5,4},{6,7},{7,6},{8,9},{9,8},{10,11... | collective-permute-start | bytes 12296 | tf_op jit(solution)/shard_map/ppermute | solution.py:375
  97.0 4.9 %collective-permute-start.10 = (f32[8,128]{1,0:T(8,128)S(1)}, f32[8,128]{1,0:T(8,128)S(1)}, u32[]{:S(2)}, u32[]{:S(2)}) collective-permute-start(f32[8,128]{1,0:T(8,128)S(1)} %log_add_fusion.6.one_ref), channel_id=1, source_target_pairs={{0,3},{1,2},{2,1},{3,0},{4,7},{5,6},{6,5},{7,4},{8,11},{9,10},{10,... | collective-permute-start | bytes 12296 | tf_op jit(solution)/shard_map/ppermute | solution.py:375
  104.2 3.9 %collective-permute-start.11 = (f32[1,2048]{1,0:T(1,128)S(1)}, f32[1,2048]{1,0:T(1,128)S(1)}, u32[]{:S(2)}, u32[]{:S(2)}) collective-permute-start(f32[1,2048]{1,0:T(1,128)S(1)} %get-tuple-element.64), channel_id=1, source_target_pairs={{0,4},{4,0},{8,12},{12,8},{16,20},{20,16},{24,28},{28,24},{32,36},... | collective-permute-start | bytes 24584 | tf_op jit(solution)/shard_map/ppermute | solution.py:375
  120.4 3.3 %collective-permute-start.12 = (f32[1,2048]{1,0:T(1,128)S(1)}, f32[1,2048]{1,0:T(1,128)S(1)}, u32[]{:S(2)}, u32[]{:S(2)}) collective-permute-start(f32[1,2048]{1,0:T(1,128)S(1)} %bitcast.17), channel_id=1, source_target_pairs={{0,4},{4,0},{8,12},{12,8},{16,20},{20,16},{24,28},{28,24},{32,36},... | collective-permute-start | bytes 24584 | tf_op jit(solution)/shard_map/ppermute | solution.py:375
  125.4 6.4 %collective-permute-start.13 = (bf16[64,512]{1,0:T(8,128)(2,1)S(1)}, bf16[64,512]{1,0:T(8,128)(2,1)S(1)}, u32[]{:S(2)}, u32[]{:S(2)}) collective-permute-start(bf16[64,512]{1,0:T(8,128)(2,1)S(1)} %first_plan.1), channel_id=1, source_target_pairs={{0,1},{1,0},{2,3},{3,2},{4,5},{5,4},{6,7},{7,6},{8,9},{9,8},{10,11... | collective-permute-start | bytes 196616 | tf_op jit(solution)/shard_map/ppermute | solution.py:375
  129.9 6.4 %collective-permute-start.14 = (bf16[64,512]{1,0:T(8,128)(2,1)S(1)}, bf16[64,512]{1,0:T(8,128)(2,1)S(1)}, u32[]{:S(2)}, u32[]{:S(2)}) collective-permute-start(bf16[64,512]{1,0:T(8,128)(2,1)S(1)} %get-tuple-element.68), channel_id=1, source_target_pairs={{0,1},{1,0},{2,3},{3,2},{4,5},{5,4},{6,7},{7,6},{8,9},{9,8},{10,11... | collective-permute-start | bytes 196616 | tf_op jit(solution)/shard_map/ppermute | solution.py:375
  131.8 5.5 %collective-permute-start.15 = (bf16[64,512]{1,0:T(8,128)(2,1)S(1)}, bf16[64,512]{1,0:T(8,128)(2,1)S(1)}, u32[]{:S(2)}, u32[]{:S(2)}) collective-permute-start(bf16[64,512]{1,0:T(8,128)(2,1)S(1)} %reduce-precision_convert_fusion.1), channel_id=1, source_target_pairs={{0,3},{1,2},{2,1},{3,0},{4,7},{5,6},{6,5},{7,4},{8,11},{9,10},{10,... | collective-permute-start | bytes 196616 | tf_op jit(solution)/shard_map/ppermute | solution.py:375
  136.3 5.3 %collective-permute-start.16 = (bf16[64,512]{1,0:T(8,128)(2,1)S(1)}, bf16[64,512]{1,0:T(8,128)(2,1)S(1)}, u32[]{:S(2)}, u32[]{:S(2)}) collective-permute-start(bf16[64,512]{1,0:T(8,128)(2,1)S(1)} %reduce-precision_convert_fusion), channel_id=1, source_target_pairs={{0,3},{1,2},{2,1},{3,0},{4,7},{5,6},{6,5},{7,4},{8,11},{9,10},{10,... | collective-permute-start | bytes 196616 | tf_op jit(solution)/shard_map/ppermute | solution.py:375

commit v5 on v4

--- a/solution.py
+++ b/solution.py
@@ -52,19 +52,25 @@
         shift_ref[at // 128 : at // 128 + 1, :] = shift[:, at : at + 128]
 
 
-def target_static(pack_ref, at, out_ref):
-    width = pack_ref.shape[1]
-    pack = pack_ref[...].astype(jnp.float32)
-    emb, geo = pack[0:EMB], pack[EMB : EMB + 4]
-    sq = jnp.sum(emb * emb, axis=0, keepdims=True)
-    x, y = geo[0:1], geo[1:2]
-    shift = -(sq * (1.0 / EMB) + x * x + y * y) * (1.0 / EPS)
-    cut = slice(at, at + width)
-    out_ref[0:EMB, cut] = pack_ref[0:EMB, :]
-    out_ref[EMB:PACK, cut] = stacked([x, x, x, y, y, y], 16, width).astype(jnp.bfloat16)
-    depth = lax.broadcasted_iota(jnp.int32, (DEPTH - PACK, width), 0)
-    out_ref[PACK:DEPTH, cut] = jnp.where(depth < 24, 1.0, 0.0).astype(jnp.bfloat16)
-    return shift, geo[2:3]
+def target_static(pack_ref, b_ref, c_ref, w_ref):
+    count, _, width = pack_ref.shape
+    piece = width // 2
+    for index in range(0, count, 2):
+        blocks = [pack_ref[index + k].astype(jnp.float32) for k in range(2)]
+        low, high = (
+            jnp.concatenate([block[:, at : at + piece] for block in blocks], axis=1) for at in (0, piece)
+        )
+        cut = slice(index * piece, index * piece + width)
+        upper, lower = low[0 : EMB // 2], high[0 : EMB // 2]
+        x, y, w = low[EMB // 2 : EMB // 2 + 1], low[EMB // 2 + 1 : EMB // 2 + 2], high[EMB // 2 : EMB // 2 + 1]
+        sq = jnp.sum(upper * upper + lower * lower, axis=0, keepdims=True)
+        c_ref[:, cut] = -(sq * (1.0 / EMB) + x * x + y * y) * (1.0 / EPS)
+        w_ref[:, cut] = w
+        b_ref[0 : EMB // 2, cut] = upper.astype(jnp.bfloat16)
+        b_ref[EMB // 2 : EMB, cut] = lower.astype(jnp.bfloat16)
+        b_ref[EMB:PACK, cut] = stacked([x, x, x, y, y, y], PACK - EMB, width).astype(jnp.bfloat16)
+    depth = lax.broadcasted_iota(jnp.int32, (DEPTH - PACK, b_ref.shape[1]), 0)
+    b_ref[PACK:DEPTH, :] = jnp.where(depth < 24, 1.0, 0.0).astype(jnp.bfloat16)
 
 
 def set_source(a_ref, shift, a_s):
@@ -177,7 +183,7 @@
 
 def static_kernel(emb_ref, pos_ref, pack_ref, a_ref, r_ref, b_ref, c_ref, w_ref, ready_ref, guess_ref, acc_ref, b_s):
     source_static(emb_ref, pos_ref, a_ref, r_ref)
-    c_ref[...], w_ref[...] = target_static(pack_ref, 0, b_ref)
+    target_static(pack_ref, b_ref, c_ref, w_ref)
     set_target(b_ref, c_ref[...] + w_ref[...], b_s)
     set_source(a_ref, r_ref[...], ready_ref)
     acc_ref[...] = jnp.full(acc_ref.shape, -jnp.inf, jnp.float32)
@@ -212,7 +218,7 @@
 
 
 def first_kernel(a_ref, r_ref, near_b_ref, near_c_ref, near_w_ref, pack_ref, ready_ref, guess_ref, acc_ref, out_ref, b_ref, c_ref, w_ref, a_s, near_s, far_s, *rest):
-    c_ref[...], w_ref[...] = target_static(pack_ref, 0, b_ref)
+    target_static(pack_ref, b_ref, c_ref, w_ref)
     set_target(b_ref, c_ref[...] + w_ref[...], far_s)
     near_of = lambda cut: near_c_ref[:, cut] + near_w_ref[:, cut]
     row_finish(a_ref, r_ref, near_b_ref, near_of, ready_ref, guess_ref, acc_ref, out_ref, a_s, near_s, far_s, *rest)
@@ -255,8 +261,8 @@
     set_source(a_ref, r_ref[...] - lse_ref[...], ready_ref)
 
 
-def col_finish(left, b_ref, c_ref, ready_ref, guess_ref, out_ref, b_s, guess_s, total_s):
-    col_sums(left, ready_ref, total_s, COLS)
+def col_finish(tile, left, b_ref, c_ref, ready_ref, guess_ref, out_ref, b_s, guess_s, total_s):
+    col_sums(left, ready_ref, total_s, tile)
     guess_s[...] = guess_ref[...]
 
     @pl.when(jnp.logical_not(in_range(total_s[...])))
@@ -273,11 +279,11 @@
     lse = joined(one_ref[...], two_ref[...])
     f_ref[...] = -LAM * EPS * lse
     set_source(a_ref, r_ref[...] + logw_ref[...] - LAM * lse, left_ref)
-    col_finish(left_ref, b_ref, c_ref, ready_ref, guess_ref, out_ref, *rest)
+    col_finish(NEAR, left_ref, b_ref, c_ref, ready_ref, guess_ref, out_ref, *rest)
 
 
 def near_col_kernel(left_ref, b_ref, c_ref, ready_ref, guess_ref, out_ref, *rest):
-    col_finish(left_ref, b_ref, c_ref, ready_ref, guess_ref, out_ref, *rest)
+    col_finish(NEAR, left_ref, b_ref, c_ref, ready_ref, guess_ref, out_ref, *rest)
 
 
 def plan_sums(left, b_s, mass_s, pull_s, tile):
@@ -343,7 +349,7 @@
     plan_finish(emb_ref, begin, mass_s, pull_s, out_ref)
 
 
-NEAR, FAR, COLS, PLAN = 1024, 2048, 1024, 512
+NEAR, FAR, PLAN = 1024, 2048, 512
 SMALL = 128
 
 
@@ -398,9 +404,15 @@
     row_scratch = (left_like, right_like, right_like, acc_like, row_line, row_line)
     col_scratch = (right_like, half_line, half_line)
 
-    count = EMB + 4
-    own = jnp.concatenate([tgt_emb, tgt_pos, tgt_logw[None, :], tgt_logw[None, :]], 0).reshape(count * piece // 128, 128)
-    own = spread(own).reshape(-1, count, piece).transpose(1, 0, 2).reshape(count, half)
+    line = tgt_logw[None, :]
+    own = jnp.concatenate(
+        [
+            jnp.concatenate([tgt_emb[0 : EMB // 2], tgt_pos], 0),
+            jnp.concatenate([tgt_emb[EMB // 2 :], line, line], 0),
+        ],
+        1,
+    )
+    own = spread(own)
     other = swapped(own, "src", 1)
     a, r, near_b, near_c, near_w, ready, guess, acc = call(
         static_kernel,

time: 143 us -> 142 us (level)
  transfers between devices with their start and end apart: 17 -> 17, of which waited for: 9 -> 9; matrix products, arithmetic and copies ran while one was open for 0% -> 0% of each run, Pallas kernels for 13% -> 14%
where the time goes in v5:
time: 142 us; the launch traced here: 141 us
  blocking collectives  54.6 us (38%)
  Pallas kernels  32.6 us (23%)
  starting transfers between devices  29.9 us (21%)
  waiting for transfers between devices  20.6 us (15%)
  local copies, waits for them, and re-layouts  1.51 us (1%)
    all_to_all x4, blocking collectives, spread(): lax.all_to_all(block, 'src', 0, 0, axis_index_groups=groups, tiled=True)  54.6 us
    pallas_call x18, Pallas kernels, call(): pl.pallas_call(kernel, out_shape=out_shape, scratch_shapes=[pltpu.VMEM(li...  32.6 us
    ppermute x17, starting transfers between devices, swapped(): lax.ppermute(value, axis, [(k, k ^ mask) for k in range(lax.axis_size(axi...  29.9 us
    ppermute x17, waiting for transfers between devices, swapped(): lax.ppermute(value, axis, [(k, k ^ mask) for k in range(lax.axis_size(axi...  20.6 us
  transfers between devices with their start and end apart: 17, of which 9 were waited for; matrix products, arithmetic and copies ran while one was open for 0% of the time, Pallas kernels for 14%

profile of v5, /device:TPU:1, one launch (start us, length us, event | category | flops | bytes accessed | tf_op | source)
XLA Modules:
  0.0 141.5 jit_solution(13172056685364498485)
XLA Ops:
  0.6 0.7 fusion.6
  1.4 0.7 copy-done.3
  2.0 0.0 copy-done.4
  2.0 0.1 maximum_maximum_fusion
  2.2 0.0 copy-start
  2.2 0.0 copy-start.1
  2.2 18.4 %all_to_all.20.pack_ref = bf16[32,34,128]{2,1,0:T(8,128)(2,1)S(1)} all-to-all(bf16[32,34,128]{2,1,0:T(8,128)(2,1)S(1)} %broadcast_in_dim.19), channel_id=1, replica_groups={{0,8,16,24,32,40,48,56,64,72,80,88,96,104,112,120,128,136,144,152,160,1..., dimensions={0} | all-to-all | bytes 557056 | tf_op jit(solution)/shard_map/all_to_all | solution.py:393
  20.5 2.0 %collective-permute-start = (bf16[32,34,128]{2,1,0:T(8,128)(2,1)S(1)}, bf16[32,34,128]{2,1,0:T(8,128)(2,1)S(1)}, u32[]{:S(2)}, u32[]{:S(2)}) collective-permute-start(bf16[32,34,128]{2,1,0:T(8,128)(2,1)S(1)} %all_to_all.20.pack_ref), channel_id=1, source_target_pairs={{0,4},{4,0},{8,12},{12,8},{16,20},{20,16},{24,28},{28,24},{32,36},... | collective-permute-start | bytes 835592 | tf_op jit(solution)/shard_map/ppermute | solution.py:381
  22.5 2.4 %static_parts.1 = (bf16[1024,128]{1,0:T(8,128)(2,1)S(1)}, f32[8,128]{1,0:T(8,128)S(1)}, bf16[128,2048]{1,0:T(8,128)(2,1)S(1)}, f32[1,2048]{1,0:T(1,128)S(1)}, f3...) custom-call(bf16[64,1024]{1,0:T(8,128)(2,1)S(1)} %copy-done, ...), custom_call_target="tpu_custom_call" | custom-call | flops 536870912 | bytes 2000000 | tf_op jit(solution)/shard_map/static_parts/pallas_call | solution.py:365
  24.9 0.0 collective-permute-done.pack_ref
  24.9 1.8 %first_row_lse.1 = (f32[8,128]{1,0:T(8,128)S(1)}, bf16[128,2048]{1,0:T(8,128)(2,1)S(1)}, f32[1,2048]{1,0:T(1,128)S(1)}, f32[1,2048]{1,0:T(1,128)S(1)}) custom-call(bf16[1024,128]{1,0:T(8,128)(2,1)S(1)} %get-tuple-element.36.a_ref, f32[8,128]{1,0:T(8,128)S(1)} %get-tuple-element.37.r_ref, bf16[128,2048]{1,0:T(8,128)(2,1)S(1)} %get-tuple-element.38.near_b_ref.b_ref, ...), custom_call_target="tpu_custom_call" | custom-call | flops 536870912 | bytes 2000000 | tf_op jit(solution)/shard_map/first_row_lse/pallas_call | solution.py:365
  26.7 3.1 %collective-permute-start.1 = (f32[8,128]{1,0:T(8,128)S(1)}, f32[8,128]{1,0:T(8,128)S(1)}, u32[]{:S(2)}, u32[]{:S(2)}) collective-permute-start(f32[8,128]{1,0:T(8,128)S(1)} %get-tuple-element.44.lse_ref.guess_ref), channel_id=1, source_target_pairs={{0,1},{1,0},{2,3},{3,2},{4,5},{5,4},{6,7},{7,6},{8,9},{9,8},{10,11... | collective-permute-start | bytes 12296 | tf_op jit(solution)/shard_map/ppermute | solution.py:381
  29.8 1.0 collective-permute-done.1
  30.8 0.0 copy-start.2
  30.8 4.6 %collective-permute-start.2 = (f32[8,128]{1,0:T(8,128)S(1)}, f32[8,128]{1,0:T(8,128)S(1)}, u32[]{:S(2)}, u32[]{:S(2)}) collective-permute-start(f32[8,128]{1,0:T(8,128)S(1)} %log_add_fusion.8.one_ref), channel_id=1, source_target_pairs={{0,3},{1,2},{2,1},{3,0},{4,7},{5,6},{6,5},{7,4},{8,11},{9,10},{10,... | collective-permute-start | bytes 12296 | tf_op jit(solution)/shard_map/ppermute | solution.py:381
  35.4 3.9 %col_guess.1 = (bf16[128,2048]{1,0:T(8,128)(2,1)S(1)}, bf16[128,2048]{1,0:T(8,128)(2,1)S(1)}, bf16[1024,128]{1,0:T(8,128)(2,1)S(1)}, f32[1,2048]{1,0:T(1,128)S(1)}, f32[1,2048]{1,0:T(1,128)S(1)}) custom-call(bf16[1024,128]{1,0:T(8,128)(2,1)S(1)} %get-tuple-element.36.a_ref, f32[8,128]{1,0:T(8,128)S(1)} %get-tuple-element.37.r_ref, ...), custom_call_target="tpu_custom_call" | custom-call | flops 1073741824 | bytes 2000000 | tf_op jit(solution)/shard_map/col_guess/pallas_call | solution.py:365
  39.2 0.0 collective-permute-done.2.two_ref
  39.2 2.3 %far_col_lse.3 = (f32[1,2048]{1,0:T(1,128)S(1)}, f32[8,128]{1,0:T(8,128)}, bf16[1024,128]{1,0:T(8,128)(2,1)S(1)}) custom-call(bf16[1024,128]{1,0:T(8,128)(2,1)S(1)} %get-tuple-element.36.a_ref, f32[8,128]{1,0:T(8,128)S(1)} %get-tuple-element.37.r_ref, f32[8,128]{1,0:T(8,128)S(1)} %bitcast.20, f32[8,128]{1,0:T(8,128)S(1)} %log_add_fusion.8.one_ref, ...), custom_call_target="tpu_custom_call" | custom-call | flops 536870912 | bytes 2000000 | tf_op jit(solution)/shard_map/far_col_lse/pallas_call | solution.py:365
  41.5 1.5 %collective-permute-start.3 = (f32[1,2048]{1,0:T(1,128)S(1)}, f32[1,2048]{1,0:T(1,128)S(1)}, u32[]{:S(2)}, u32[]{:S(2)}) collective-permute-start(f32[1,2048]{1,0:T(1,128)S(1)} %get-tuple-element.52.far_guess_ref.guess_ref), channel_id=1, source_target_pairs={{0,4},{4,0},{8,12},{12,8},{16,20},{20,16},{24,28},{28,24},{32,36},... | collective-permute-start | bytes 24584 | tf_op jit(solution)/shard_map/ppermute | solution.py:381
  43.0 1.6 %near_col_lse.3.near_guess_ref.guess_ref = f32[1,2048]{1,0:T(1,128)S(1)} custom-call(bf16[1024,128]{1,0:T(8,128)(2,1)S(1)} %get-tuple-element.49.left_ref, bf16[128,2048]{1,0:T(8,128)(2,1)S(1)} %get-tuple-element.38.near_b_ref.b_ref, f32[1,2048]{1,0:T(1,128)S(1)} %get-tuple-element.39.near_c_ref.c_ref, bf16[128,2048]{1,0:T(8,128)(2,1)S(1)} %get-tuple-element.50.ready_ref, ...), custom_call_target="tpu_custom_call" | custom-call | flops 536870912 | bytes 2000000 | tf_op jit(solution)/shard_map/near_col_lse/pallas_call | solution.py:365
  44.6 12.0 %all_to_all.21 = f32[32,16,128]{2,1,0:T(8,128)S(1)} all-to-all(f32[32,16,128]{2,1,0:T(8,128)S(1)} %broadcast_in_dim.20), channel_id=1, replica_groups={{0,8,16,24,32,40,48,56,64,72,80,88,96,104,112,120,128,136,144,152,160,1..., dimensions={0} | all-to-all | bytes 524288 | tf_op jit(solution)/shard_map/all_to_all | solution.py:393
  56.7 0.1 exponential_reduce_fusion.2
  56.8 1.7 %collective-permute-start.4 = (f32[1,2048]{1,0:T(1,128)S(1)}, f32[1,2048]{1,0:T(1,128)S(1)}, u32[]{:S(2)}, u32[]{:S(2)}) collective-permute-start(f32[1,2048]{1,0:T(1,128)S(1)} %bitcast.10), channel_id=1, source_target_pairs={{0,4},{4,0},{8,12},{12,8},{16,20},{20,16},{24,28},{28,24},{32,36},... | collective-permute-start | bytes 24584 | tf_op jit(solution)/shard_map/ppermute | solution.py:381
  58.5 1.5 %near_row_lse.2.acc_ref = f32[1024,128]{1,0:T(8,128)S(1)} custom-call(bf16[128,2048]{1,0:T(8,128)(2,1)S(1)} %get-tuple-element.38.near_b_ref.b_ref, f32[1,2048]{1,0:T(1,128)S(1)} %get-tuple-element.39.near_c_ref.c_ref, f32[1,2048]{1,0:T(1,128)S(1)} %get-tuple-element.40.near_w_ref.w_ref, f32[1,2048]{1,0:T(1,128)S(1)} %bitcast.11, ...), custom_call_target="tpu_custom_call" | custom-call | flops 536870912 | bytes 2000000 | tf_op jit(solution)/shard_map/near_row_lse/pallas_call | solution.py:365
  60.0 0.0 collective-permute-done.4.lse_ref
  60.0 1.5 %row_lse.2.lse_ref.guess_ref = f32[8,128]{1,0:T(8,128)S(1)} custom-call(bf16[1024,128]{1,0:T(8,128)(2,1)S(1)} %get-tuple-element.36.a_ref, f32[8,128]{1,0:T(8,128)S(1)} %get-tuple-element.37.r_ref, bf16[128,2048]{1,0:T(8,128)(2,1)S(1)} %get-tuple-element.38.near_b_ref.b_ref, f32[1,2048]{1,0:T(1,128)S(1)} %get-tuple-element.39.near_c_ref.c_ref, ...), custom_call_target="tpu_custom_call" | custom-call | flops 536870912 | bytes 2000000 | tf_op jit(solution)/shard_map/row_lse/pallas_call | solution.py:365
  61.5 1.2 collective-permute-start.5
  62.8 2.2 %collective-permute-done.5 = f32[8,128]{1,0:T(8,128)S(1)} collective-permute-done((f32[8,128]{1,0:T(8,128)S(1)}, f32[8,128]{1,0:T(8,128)S(1)}, u32[]{:S(2)}, u32[]{:S(2)}) %collective-permute-start.5) | collective-permute-done | bytes 4128 | tf_op jit(solution)/shard_map/ppermute | solution.py:381
  65.0 1.6 %collective-permute-start.6 = (f32[8,128]{1,0:T(8,128)S(1)}, f32[8,128]{1,0:T(8,128)S(1)}, u32[]{:S(2)}, u32[]{:S(2)}) collective-permute-start(f32[8,128]{1,0:T(8,128)S(1)} %log_add_fusion.7.one_ref), channel_id=1, source_target_pairs={{0,3},{1,2},{2,1},{3,0},{4,7},{5,6},{6,5},{7,4},{8,11},{9,10},{10,... | collective-permute-start | bytes 12296 | tf_op jit(solution)/shard_map/ppermute | solution.py:381
  66.6 0.2 prepare.2
  66.8 2.9 %collective-permute-done.6.two_ref = f32[8,128]{1,0:T(8,128)S(1)} collective-permute-done((f32[8,128]{1,0:T(8,128)S(1)}, f32[8,128]{1,0:T(8,128)S(1)}, u32[]{:S(2)}, u32[]{:S(2)}) %collective-permute-start.6) | collective-permute-done | bytes 4128 | tf_op jit(solution)/shard_map/ppermute | solution.py:381
  69.7 2.3 %far_col_lse.4 = (f32[1,2048]{1,0:T(1,128)S(1)}, f32[8,128]{1,0:T(8,128)}, bf16[1024,128]{1,0:T(8,128)(2,1)S(1)}) custom-call(bf16[1024,128]{1,0:T(8,128)(2,1)S(1)} %get-tuple-element.36.a_ref, f32[8,128]{1,0:T(8,128)S(1)} %get-tuple-element.37.r_ref, f32[8,128]{1,0:T(8,128)S(1)} %bitcast.21, f32[8,128]{1,0:T(8,128)S(1)} %log_add_fusion.7.one_ref, ...), custom_call_target="tpu_custom_call" | custom-call | flops 536870912 | bytes 2000000 | tf_op jit(solution)/shard_map/far_col_lse/pallas_call | solution.py:365
  71.9 2.3 %collective-permute-start.7 = (f32[1,2048]{1,0:T(1,128)S(1)}, f32[1,2048]{1,0:T(1,128)S(1)}, u32[]{:S(2)}, u32[]{:S(2)}) collective-permute-start(f32[1,2048]{1,0:T(1,128)S(1)} %get-tuple-element.58.far_guess_ref.guess_ref), channel_id=1, source_target_pairs={{0,4},{4,0},{8,12},{12,8},{16,20},{20,16},{24,28},{28,24},{32,36},... | collective-permute-start | bytes 24584 | tf_op jit(solution)/shard_map/ppermute | solution.py:381
  74.3 1.6 %near_col_lse.4.near_guess_ref.guess_ref = f32[1,2048]{1,0:T(1,128)S(1)} custom-call(bf16[1024,128]{1,0:T(8,128)(2,1)S(1)} %get-tuple-element.56.left_ref, bf16[128,2048]{1,0:T(8,128)(2,1)S(1)} %get-tuple-element.38.near_b_ref.b_ref, f32[1,2048]{1,0:T(1,128)S(1)} %get-tuple-element.39.near_c_ref.c_ref, bf16[128,2048]{1,0:T(8,128)(2,1)S(1)} %get-tuple-element.57.ready_ref, ...), custom_call_target="tpu_custom_call" | custom-call | flops 536870912 | bytes 2000000 | tf_op jit(solution)/shard_map/near_col_lse/pallas_call | solution.py:365
  75.9 0.0 collective-permute-done.7
  75.9 12.1 %all_to_all.22 = f32[32,16,128]{2,1,0:T(8,128)S(1)} all-to-all(f32[32,16,128]{2,1,0:T(8,128)S(1)} %broadcast_in_dim.21), channel_id=1, replica_groups={{0,8,16,24,32,40,48,56,64,72,80,88,96,104,112,120,128,136,144,152,160,1..., dimensions={0} | all-to-all | bytes 524288 | tf_op jit(solution)/shard_map/all_to_all | solution.py:393
  88.1 0.1 exponential_reduce_fusion.1
  88.1 1.5 %collective-permute-start.8 = (f32[1,2048]{1,0:T(1,128)S(1)}, f32[1,2048]{1,0:T(1,128)S(1)}, u32[]{:S(2)}, u32[]{:S(2)}) collective-permute-start(f32[1,2048]{1,0:T(1,128)S(1)} %bitcast.13), channel_id=1, source_target_pairs={{0,4},{4,0},{8,12},{12,8},{16,20},{20,16},{24,28},{28,24},{32,36},... | collective-permute-start | bytes 24584 | tf_op jit(solution)/shard_map/ppermute | solution.py:381
  89.6 1.5 %near_row_lse.3.acc_ref = f32[1024,128]{1,0:T(8,128)S(1)} custom-call(bf16[128,2048]{1,0:T(8,128)(2,1)S(1)} %get-tuple-element.38.near_b_ref.b_ref, f32[1,2048]{1,0:T(1,128)S(1)} %get-tuple-element.39.near_c_ref.c_ref, f32[1,2048]{1,0:T(1,128)S(1)} %get-tuple-element.40.near_w_ref.w_ref, f32[1,2048]{1,0:T(1,128)S(1)} %bitcast.14, ...), custom_call_target="tpu_custom_call" | custom-call | flops 536870912 | bytes 2000000 | tf_op jit(solution)/shard_map/near_row_lse/pallas_call | solution.py:365
  91.2 1.5 %row_lse.3.lse_ref = f32[8,128]{1,0:T(8,128)S(1)} custom-call(bf16[1024,128]{1,0:T(8,128)(2,1)S(1)} %get-tuple-element.36.a_ref, f32[8,128]{1,0:T(8,128)S(1)} %get-tuple-element.37.r_ref, bf16[128,2048]{1,0:T(8,128)(2,1)S(1)} %get-tuple-element.38.near_b_ref.b_ref, f32[1,2048]{1,0:T(1,128)S(1)} %get-tuple-element.39.near_c_ref.c_ref, ...), custom_call_target="tpu_custom_call" | custom-call | flops 536870912 | bytes 2000000 | tf_op jit(solution)/shard_map/row_lse/pallas_call | solution.py:365
  92.7 1.2 collective-permute-start.9
  93.9 2.2 %collective-permute-done.9 = f32[8,128]{1,0:T(8,128)S(1)} collective-permute-done((f32[8,128]{1,0:T(8,128)S(1)}, f32[8,128]{1,0:T(8,128)S(1)}, u32[]{:S(2)}, u32[]{:S(2)}) %collective-permute-start.9) | collective-permute-done | bytes 4128 | tf_op jit(solution)/shard_map/ppermute | solution.py:381
  96.1 1.8 %collective-permute-start.10 = (f32[8,128]{1,0:T(8,128)S(1)}, f32[8,128]{1,0:T(8,128)S(1)}, u32[]{:S(2)}, u32[]{:S(2)}) collective-permute-start(f32[8,128]{1,0:T(8,128)S(1)} %log_add_fusion.6.one_ref), channel_id=1, source_target_pairs={{0,3},{1,2},{2,1},{3,0},{4,7},{5,6},{6,5},{7,4},{8,11},{9,10},{10,... | collective-permute-start | bytes 12296 | tf_op jit(solution)/shard_map/ppermute | solution.py:381
  98.0 0.1 prepare.3
  98.1 2.9 %collective-permute-done.10.two_ref = f32[8,128]{1,0:T(8,128)S(1)} collective-permute-done((f32[8,128]{1,0:T(8,128)S(1)}, f32[8,128]{1,0:T(8,128)S(1)}, u32[]{:S(2)}, u32[]{:S(2)}) %collective-permute-start.10) | collective-permute-done | bytes 4128 | tf_op jit(solution)/shard_map/ppermute | solution.py:381
  101.0 2.3 %far_col_lse.5 = (f32[1,2048]{1,0:T(1,128)S(1)}, f32[8,128]{1,0:T(8,128)}, bf16[1024,128]{1,0:T(8,128)(2,1)S(1)}) custom-call(bf16[1024,128]{1,0:T(8,128)(2,1)S(1)} %get-tuple-element.36.a_ref, f32[8,128]{1,0:T(8,128)S(1)} %get-tuple-element.37.r_ref, f32[8,128]{1,0:T(8,128)S(1)} %bitcast.22, f32[8,128]{1,0:T(8,128)S(1)} %log_add_fusion.6.one_ref, ...), custom_call_target="tpu_custom_call" | custom-call | flops 536870912 | bytes 2000000 | tf_op jit(solution)/shard_map/far_col_lse/pallas_call | solution.py:365
  103.3 2.3 %collective-permute-start.11 = (f32[1,2048]{1,0:T(1,128)S(1)}, f32[1,2048]{1,0:T(1,128)S(1)}, u32[]{:S(2)}, u32[]{:S(2)}) collective-permute-start(f32[1,2048]{1,0:T(1,128)S(1)} %get-tuple-element.64), channel_id=1, source_target_pairs={{0,4},{4,0},{8,12},{12,8},{16,20},{20,16},{24,28},{28,24},{32,36},... | collective-permute-start | bytes 24584 | tf_op jit(solution)/shard_map/ppermute | solution.py:381
  105.7 1.6 %near_col_lse.5 = f32[1,2048]{1,0:T(1,128)S(1)} custom-call(bf16[1024,128]{1,0:T(8,128)(2,1)S(1)} %get-tuple-element.62.left_ref, bf16[128,2048]{1,0:T(8,128)(2,1)S(1)} %get-tuple-element.38.near_b_ref.b_ref, f32[1,2048]{1,0:T(1,128)S(1)} %get-tuple-element.39.near_c_ref.c_ref, bf16[128,2048]{1,0:T(8,128)(2,1)S(1)} %get-tuple-element.63.ready_ref, ...), custom_call_target="tpu_custom_call" | custom-call | flops 536870912 | bytes 2000000 | tf_op jit(solution)/shard_map/near_col_lse/pallas_call | solution.py:365
  107.3 12.1 %all_to_all.23 = f32[32,16,128]{2,1,0:T(8,128)S(1)} all-to-all(f32[32,16,128]{2,1,0:T(8,128)S(1)} %broadcast_in_dim.22), channel_id=1, replica_groups={{0,8,16,24,32,40,48,56,64,72,80,88,96,104,112,120,128,136,144,152,160,1..., dimensions={0} | all-to-all | bytes 524288 | tf_op jit(solution)/shard_map/all_to_all | solution.py:393
  119.4 0.1 exponential_reduce_fusion
  119.5 1.5 %collective-permute-start.12 = (f32[1,2048]{1,0:T(1,128)S(1)}, f32[1,2048]{1,0:T(1,128)S(1)}, u32[]{:S(2)}, u32[]{:S(2)}) collective-permute-start(f32[1,2048]{1,0:T(1,128)S(1)} %bitcast.16), channel_id=1, source_target_pairs={{0,4},{4,0},{8,12},{12,8},{16,20},{20,16},{24,28},{28,24},{32,36},... | collective-permute-start | bytes 24584 | tf_op jit(solution)/shard_map/ppermute | solution.py:381
  121.0 1.8 %near_plan.1 = (f32[512,128]{1,0:T(8,128)S(1)}, f32[512,64]{1,0:T(8,128)S(1)}) custom-call(bf16[1024,128]{1,0:T(8,128)(2,1)S(1)} %get-tuple-element.62.left_ref, bf16[128,2048]{1,0:T(8,128)(2,1)S(1)} %get-tuple-element.38.near_b_ref.b_ref, f32[1,2048]{1,0:T(1,128)S(1)} %get-tuple-element.39.near_c_ref.c_ref, ...), custom_call_target="tpu_custom_call" | custom-call | flops 536870912 | bytes 2000000 | tf_op jit(solution)/shard_map/near_plan/pallas_call | solution.py:365
  122.8 0.0 collective-permute-done.12.lse_ref
  122.8 1.7 %first_plan.1 = bf16[64,512]{1,0:T(8,128)(2,1)S(1)} custom-call(bf16[64,1024]{1,0:T(8,128)(2,1)S(1)} %copy-done, bf16[1024,128]{1,0:T(8,128)(2,1)S(1)} %get-tuple-element.62.left_ref, bf16[128,2048]{1,0:T(8,128)(2,1)S(1)} %get-tuple-element.45.far_b_ref.b_ref, f32[1,2048]{1,0:T(1,128)S(1)} %get-tuple-element.46.far_c_ref.c_ref, ...), custom_call_target="tpu_custom_call" | custom-call | flops 536870912 | bytes 2000000 | tf_op jit(solution)/shard_map/first_plan/pallas_call | solution.py:365
  124.5 1.2 collective-permute-start.13
  125.8 3.2 %last_plan.1 = (bf16[64,512]{1,0:T(8,128)(2,1)S(1)}, f32[1,64]{1,0:T(1,128)}) custom-call(bf16[64,1024]{1,0:T(8,128)(2,1)S(1)} %copy-done, bf16[1024,128]{1,0:T(8,128)(2,1)S(1)} %get-tuple-element.62.left_ref, bf16[128,2048]{1,0:T(8,128)(2,1)S(1)} %get-tuple-element.38.near_b_ref.b_ref, f32[1,2048]{1,0:T(1,128)S(1)} %get-tuple-element.39.near_c_ref.c_ref, ...), custom_call_target="tpu_custom_call" | custom-call | flops 1073741824 | bytes 2000000 | tf_op jit(solution)/shard_map/last_plan/pallas_call | solution.py:365
  129.0 1.3 collective-permute-start.14
  130.3 0.6 collective-permute-done.13
  130.9 1.0 collective-permute-start.15
  131.9 3.5 %collective-permute-done.14 = bf16[64,512]{1,0:T(8,128)(2,1)S(1)} collective-permute-done((bf16[64,512]{1,0:T(8,128)(2,1)S(1)}, bf16[64,512]{1,0:T(8,128)(2,1)S(1)}, u32[]{:S(2)}, u32[]{:S(2)}) %collective-permute-start.14) | collective-permute-done | bytes 65568 | tf_op jit(solution)/shard_map/ppermute | solution.py:381
  135.4 0.1 collective-permute-start.16
  135.5 0.9 collective-permute-done.15
  136.4 4.3 %collective-permute-done.16 = bf16[64,512]{1,0:T(8,128)(2,1)S(1)} collective-permute-done((bf16[64,512]{1,0:T(8,128)(2,1)S(1)}, bf16[64,512]{1,0:T(8,128)(2,1)S(1)}, u32[]{:S(2)}, u32[]{:S(2)}) %collective-permute-start.16) | collective-permute-done | bytes 65568 | tf_op jit(solution)/shard_map/ppermute | solution.py:381
  140.7 0.7 convert_add_fusion
  (26 shorter events, 0.5 us)
Async XLA Ops:
  1.3 0.7 copy-start.3
  1.3 0.7 copy-start.4
  2.2 20.3 %copy-start = (bf16[64,1024]{1,0:T(8,128)(2,1)S(1)}, bf16[64,1024]{1,0:T(8,128)(2,1)}, u32[]{:S(2)}) copy-start(bf16[64,1024]{1,0:T(8,128)(2,1)} %emb_ref.5) | copy-start | bytes 393220
  2.2 20.3 %copy-start.1 = (f32[2,1024]{1,0:T(2,128)S(1)}, f32[2,1024]{1,0:T(2,128)}, u32[]{:S(2)}) copy-start(f32[2,1024]{1,0:T(2,128)} %pos_ref.1) | copy-start | bytes 24580
  20.5 4.4 %collective-permute-start = (bf16[32,34,128]{2,1,0:T(8,128)(2,1)S(1)}, bf16[32,34,128]{2,1,0:T(8,128)(2,1)S(1)}, u32[]{:S(2)}, u32[]{:S(2)}) collective-permute-start(bf16[32,34,128]{2,1,0:T(8,128)(2,1)S(1)} %all_to_all.20.pack_ref), channel_id=1, source_target_pairs={{0,4},{4,0},{8,12},{12,8},{16,20},{20,16},{24,28},{28,24},{32,36},... | collective-permute-start | bytes 835592 | tf_op jit(solution)/shard_map/ppermute | solution.py:381
  26.7 4.1 %collective-permute-start.1 = (f32[8,128]{1,0:T(8,128)S(1)}, f32[8,128]{1,0:T(8,128)S(1)}, u32[]{:S(2)}, u32[]{:S(2)}) collective-permute-start(f32[8,128]{1,0:T(8,128)S(1)} %get-tuple-element.44.lse_ref.guess_ref), channel_id=1, source_target_pairs={{0,1},{1,0},{2,3},{3,2},{4,5},{5,4},{6,7},{7,6},{8,9},{9,8},{10,11... | collective-permute-start | bytes 12296 | tf_op jit(solution)/shard_map/ppermute | solution.py:381
  30.8 4.6 %copy-start.2 = (f32[1024]{0:T(1024)S(1)}, f32[1024]{0:T(1024)}, u32[]{:S(2)}) copy-start(f32[1024]{0:T(1024)} %param.8) | copy-start | bytes 12292
  30.8 8.4 %collective-permute-start.2 = (f32[8,128]{1,0:T(8,128)S(1)}, f32[8,128]{1,0:T(8,128)S(1)}, u32[]{:S(2)}, u32[]{:S(2)}) collective-permute-start(f32[8,128]{1,0:T(8,128)S(1)} %log_add_fusion.8.one_ref), channel_id=1, source_target_pairs={{0,3},{1,2},{2,1},{3,0},{4,7},{5,6},{6,5},{7,4},{8,11},{9,10},{10,... | collective-permute-start | bytes 12296 | tf_op jit(solution)/shard_map/ppermute | solution.py:381
  41.5 3.0 %collective-permute-start.3 = (f32[1,2048]{1,0:T(1,128)S(1)}, f32[1,2048]{1,0:T(1,128)S(1)}, u32[]{:S(2)}, u32[]{:S(2)}) collective-permute-start(f32[1,2048]{1,0:T(1,128)S(1)} %get-tuple-element.52.far_guess_ref.guess_ref), channel_id=1, source_target_pairs={{0,4},{4,0},{8,12},{12,8},{16,20},{20,16},{24,28},{28,24},{32,36},... | collective-permute-start | bytes 24584 | tf_op jit(solution)/shard_map/ppermute | solution.py:381
  56.8 3.2 %collective-permute-start.4 = (f32[1,2048]{1,0:T(1,128)S(1)}, f32[1,2048]{1,0:T(1,128)S(1)}, u32[]{:S(2)}, u32[]{:S(2)}) collective-permute-start(f32[1,2048]{1,0:T(1,128)S(1)} %bitcast.10), channel_id=1, source_target_pairs={{0,4},{4,0},{8,12},{12,8},{16,20},{20,16},{24,28},{28,24},{32,36},... | collective-permute-start | bytes 24584 | tf_op jit(solution)/shard_map/ppermute | solution.py:381
  61.5 3.5 %collective-permute-start.5 = (f32[8,128]{1,0:T(8,128)S(1)}, f32[8,128]{1,0:T(8,128)S(1)}, u32[]{:S(2)}, u32[]{:S(2)}) collective-permute-start(f32[8,128]{1,0:T(8,128)S(1)} %row_lse.2.lse_ref.guess_ref), channel_id=1, source_target_pairs={{0,1},{1,0},{2,3},{3,2},{4,5},{5,4},{6,7},{7,6},{8,9},{9,8},{10,11... | collective-permute-start | bytes 12296 | tf_op jit(solution)/shard_map/ppermute | solution.py:381
  65.0 4.7 %collective-permute-start.6 = (f32[8,128]{1,0:T(8,128)S(1)}, f32[8,128]{1,0:T(8,128)S(1)}, u32[]{:S(2)}, u32[]{:S(2)}) collective-permute-start(f32[8,128]{1,0:T(8,128)S(1)} %log_add_fusion.7.one_ref), channel_id=1, source_target_pairs={{0,3},{1,2},{2,1},{3,0},{4,7},{5,6},{6,5},{7,4},{8,11},{9,10},{10,... | collective-permute-start | bytes 12296 | tf_op jit(solution)/shard_map/ppermute | solution.py:381
  71.9 3.9 %collective-permute-start.7 = (f32[1,2048]{1,0:T(1,128)S(1)}, f32[1,2048]{1,0:T(1,128)S(1)}, u32[]{:S(2)}, u32[]{:S(2)}) collective-permute-start(f32[1,2048]{1,0:T(1,128)S(1)} %get-tuple-element.58.far_guess_ref.guess_ref), channel_id=1, source_target_pairs={{0,4},{4,0},{8,12},{12,8},{16,20},{20,16},{24,28},{28,24},{32,36},... | collective-permute-start | bytes 24584 | tf_op jit(solution)/shard_map/ppermute | solution.py:381
  88.1 3.0 %collective-permute-start.8 = (f32[1,2048]{1,0:T(1,128)S(1)}, f32[1,2048]{1,0:T(1,128)S(1)}, u32[]{:S(2)}, u32[]{:S(2)}) collective-permute-start(f32[1,2048]{1,0:T(1,128)S(1)} %bitcast.13), channel_id=1, source_target_pairs={{0,4},{4,0},{8,12},{12,8},{16,20},{20,16},{24,28},{28,24},{32,36},... | collective-permute-start | bytes 24584 | tf_op jit(solution)/shard_map/ppermute | solution.py:381
  92.7 3.5 %collective-permute-start.9 = (f32[8,128]{1,0:T(8,128)S(1)}, f32[8,128]{1,0:T(8,128)S(1)}, u32[]{:S(2)}, u32[]{:S(2)}) collective-permute-start(f32[8,128]{1,0:T(8,128)S(1)} %row_lse.3.lse_ref), channel_id=1, source_target_pairs={{0,1},{1,0},{2,3},{3,2},{4,5},{5,4},{6,7},{7,6},{8,9},{9,8},{10,11... | collective-permute-start | bytes 12296 | tf_op jit(solution)/shard_map/ppermute | solution.py:381
  96.1 4.9 %collective-permute-start.10 = (f32[8,128]{1,0:T(8,128)S(1)}, f32[8,128]{1,0:T(8,128)S(1)}, u32[]{:S(2)}, u32[]{:S(2)}) collective-permute-start(f32[8,128]{1,0:T(8,128)S(1)} %log_add_fusion.6.one_ref), channel_id=1, source_target_pairs={{0,3},{1,2},{2,1},{3,0},{4,7},{5,6},{6,5},{7,4},{8,11},{9,10},{10,... | collective-permute-start | bytes 12296 | tf_op jit(solution)/shard_map/ppermute | solution.py:381
  103.3 3.9 %collective-permute-start.11 = (f32[1,2048]{1,0:T(1,128)S(1)}, f32[1,2048]{1,0:T(1,128)S(1)}, u32[]{:S(2)}, u32[]{:S(2)}) collective-permute-start(f32[1,2048]{1,0:T(1,128)S(1)} %get-tuple-element.64), channel_id=1, source_target_pairs={{0,4},{4,0},{8,12},{12,8},{16,20},{20,16},{24,28},{28,24},{32,36},... | collective-permute-start | bytes 24584 | tf_op jit(solution)/shard_map/ppermute | solution.py:381
  119.5 3.3 %collective-permute-start.12 = (f32[1,2048]{1,0:T(1,128)S(1)}, f32[1,2048]{1,0:T(1,128)S(1)}, u32[]{:S(2)}, u32[]{:S(2)}) collective-permute-start(f32[1,2048]{1,0:T(1,128)S(1)} %bitcast.16), channel_id=1, source_target_pairs={{0,4},{4,0},{8,12},{12,8},{16,20},{20,16},{24,28},{28,24},{32,36},... | collective-permute-start | bytes 24584 | tf_op jit(solution)/shard_map/ppermute | solution.py:381
  124.5 6.4 %collective-permute-start.13 = (bf16[64,512]{1,0:T(8,128)(2,1)S(1)}, bf16[64,512]{1,0:T(8,128)(2,1)S(1)}, u32[]{:S(2)}, u32[]{:S(2)}) collective-permute-start(bf16[64,512]{1,0:T(8,128)(2,1)S(1)} %first_plan.1), channel_id=1, source_target_pairs={{0,1},{1,0},{2,3},{3,2},{4,5},{5,4},{6,7},{7,6},{8,9},{9,8},{10,11... | collective-permute-start | bytes 196616 | tf_op jit(solution)/shard_map/ppermute | solution.py:381
  129.0 6.4 %collective-permute-start.14 = (bf16[64,512]{1,0:T(8,128)(2,1)S(1)}, bf16[64,512]{1,0:T(8,128)(2,1)S(1)}, u32[]{:S(2)}, u32[]{:S(2)}) collective-permute-start(bf16[64,512]{1,0:T(8,128)(2,1)S(1)} %get-tuple-element.68), channel_id=1, source_target_pairs={{0,1},{1,0},{2,3},{3,2},{4,5},{5,4},{6,7},{7,6},{8,9},{9,8},{10,11... | collective-permute-start | bytes 196616 | tf_op jit(solution)/shard_map/ppermute | solution.py:381
  130.9 5.5 %collective-permute-start.15 = (bf16[64,512]{1,0:T(8,128)(2,1)S(1)}, bf16[64,512]{1,0:T(8,128)(2,1)S(1)}, u32[]{:S(2)}, u32[]{:S(2)}) collective-permute-start(bf16[64,512]{1,0:T(8,128)(2,1)S(1)} %reduce-precision_convert_fusion.1), channel_id=1, source_target_pairs={{0,3},{1,2},{2,1},{3,0},{4,7},{5,6},{6,5},{7,4},{8,11},{9,10},{10,... | collective-permute-start | bytes 196616 | tf_op jit(solution)/shard_map/ppermute | solution.py:381
  135.4 5.3 %collective-permute-start.16 = (bf16[64,512]{1,0:T(8,128)(2,1)S(1)}, bf16[64,512]{1,0:T(8,128)(2,1)S(1)}, u32[]{:S(2)}, u32[]{:S(2)}) collective-permute-start(bf16[64,512]{1,0:T(8,128)(2,1)S(1)} %reduce-precision_convert_fusion), channel_id=1, source_target_pairs={{0,3},{1,2},{2,1},{3,0},{4,7},{5,6},{6,5},{7,4},{8,11},{9,10},{10,... | collective-permute-start | bytes 196616 | tf_op jit(solution)/shard_map/ppermute | solution.py:381

commit v6 on v5

--- a/solution.py
+++ b/solution.py
@@ -187,7 +187,7 @@
     set_target(b_ref, c_ref[...] + w_ref[...], b_s)
     set_source(a_ref, r_ref[...], ready_ref)
     acc_ref[...] = jnp.full(acc_ref.shape, -jnp.inf, jnp.float32)
-    row_tops(ready_ref, b_s, acc_ref, 512, min(512, b_s.shape[1]))
+    row_tops(ready_ref, b_s, acc_ref, 256, min(256, b_s.shape[1]))
     over_lanes(acc_ref, guess_ref, jnp.max)
     set_source(a_ref, r_ref[...] - guess_ref[...], ready_ref)
     acc_ref[...] = jnp.zeros_like(acc_ref)
@@ -256,7 +256,7 @@
         (far_b_ref, far_c_ref, far_ref, far_guess_ref),
     ):
         set_target(b_ref, c_ref[...], out_ref)
-        col_tops(ready_ref, out_ref, top_ref, 512)
+        col_tops(ready_ref.at[0 : ready_ref.shape[0] // 2, :], out_ref, top_ref, 1024)
         out_ref[EMB:PACK, :] = target_parts(b_ref[EMB:PACK, :], c_ref[...] - top_ref[...])
     set_source(a_ref, r_ref[...] - lse_ref[...], ready_ref)
 

time: 142 us -> 140 us (0.986)
  starting transfers between devices: 29.9 us -> 36.6 us
  waiting for transfers between devices: 20.6 us -> 14 us
  Pallas kernels: 32.6 us -> 30.8 us
    ppermute x17, starting transfers between devices: 29.9 us -> 36.6 us  [swapped(): lax.ppermute(value, axis, [(k, k ^ mask) for k in range(lax.axis_size(axi...]
    ppermute x17, waiting for transfers between devices: 20.6 us -> 14 us  [swapped(): lax.ppermute(value, axis, [(k, k ^ mask) for k in range(lax.axis_size(axi...]
    pallas_call x18, Pallas kernels: 32.6 us -> 30.8 us  [call(): pl.pallas_call(kernel, out_shape=out_shape, scratch_shapes=[pltpu.VMEM(li...]
  transfers between devices with their start and end apart: 17 -> 17, of which waited for: 9 -> 8; matrix products, arithmetic and copies ran while one was open for 0% -> 0% of each run, Pallas kernels for 14% -> 12%
where the time goes in v6:
time: 140 us
  blocking collectives  54.6 us (39%)
  starting transfers between devices  36.6 us (26%)
  Pallas kernels  30.8 us (22%)
  waiting for transfers between devices  14 us (10%)
  local copies, waits for them, and re-layouts  1.51 us (1%)
    all_to_all x4, blocking collectives, spread(): lax.all_to_all(block, 'src', 0, 0, axis_index_groups=groups, tiled=True)  54.6 us
    ppermute x17, starting transfers between devices, swapped(): lax.ppermute(value, axis, [(k, k ^ mask) for k in range(lax.axis_size(axi...  36.6 us
    pallas_call x18, Pallas kernels, call(): pl.pallas_call(kernel, out_shape=out_shape, scratch_shapes=[pltpu.VMEM(li...  30.8 us
    ppermute x17, waiting for transfers between devices, swapped(): lax.ppermute(value, axis, [(k, k ^ mask) for k in range(lax.axis_size(axi...  14 us
  transfers between devices with their start and end apart: 17, of which 8 were waited for; matrix products, arithmetic and copies ran while one was open for 0% of the time, Pallas kernels for 12%

profile of v6, /device:TPU:1, one launch (start us, length us, event | category | flops | bytes accessed | tf_op | source)
XLA Modules:
  0.0 139.7 jit_solution(6760813301964013326)
XLA Ops:
  0.6 0.7 fusion.6
  1.4 0.7 copy-done.3
  2.0 0.0 copy-done.4
  2.0 0.1 maximum_maximum_fusion
  2.2 0.0 copy-start
  2.2 0.0 copy-start.1
  2.2 18.4 %all_to_all.20.pack_ref = bf16[32,34,128]{2,1,0:T(8,128)(2,1)S(1)} all-to-all(bf16[32,34,128]{2,1,0:T(8,128)(2,1)S(1)} %broadcast_in_dim.19), channel_id=1, replica_groups={{0,8,16,24,32,40,48,56,64,72,80,88,96,104,112,120,128,136,144,152,160,1..., dimensions={0} | all-to-all | bytes 557056 | tf_op jit(solution)/shard_map/all_to_all | solution.py:393
  20.5 2.0 %collective-permute-start = (bf16[32,34,128]{2,1,0:T(8,128)(2,1)S(1)}, bf16[32,34,128]{2,1,0:T(8,128)(2,1)S(1)}, u32[]{:S(2)}, u32[]{:S(2)}) collective-permute-start(bf16[32,34,128]{2,1,0:T(8,128)(2,1)S(1)} %all_to_all.20.pack_ref), channel_id=1, source_target_pairs={{0,4},{4,0},{8,12},{12,8},{16,20},{20,16},{24,28},{28,24},{32,36},... | collective-permute-start | bytes 835592 | tf_op jit(solution)/shard_map/ppermute | solution.py:381
  22.5 2.3 %static_parts.1 = (bf16[1024,128]{1,0:T(8,128)(2,1)S(1)}, f32[8,128]{1,0:T(8,128)S(1)}, bf16[128,2048]{1,0:T(8,128)(2,1)S(1)}, f32[1,2048]{1,0:T(1,128)S(1)}, f3...) custom-call(bf16[64,1024]{1,0:T(8,128)(2,1)S(1)} %copy-done, ...), custom_call_target="tpu_custom_call" | custom-call | flops 536870912 | bytes 2000000 | tf_op jit(solution)/shard_map/static_parts/pallas_call | solution.py:365
  24.8 0.0 collective-permute-done.pack_ref
  24.8 1.8 %first_row_lse.1 = (f32[8,128]{1,0:T(8,128)S(1)}, bf16[128,2048]{1,0:T(8,128)(2,1)S(1)}, f32[1,2048]{1,0:T(1,128)S(1)}, f32[1,2048]{1,0:T(1,128)S(1)}) custom-call(bf16[1024,128]{1,0:T(8,128)(2,1)S(1)} %get-tuple-element.36.a_ref, f32[8,128]{1,0:T(8,128)S(1)} %get-tuple-element.37.r_ref, bf16[128,2048]{1,0:T(8,128)(2,1)S(1)} %get-tuple-element.38.near_b_ref.b_ref, ...), custom_call_target="tpu_custom_call" | custom-call | flops 536870912 | bytes 2000000 | tf_op jit(solution)/shard_map/first_row_lse/pallas_call | solution.py:365
  26.6 3.1 %collective-permute-start.1 = (f32[8,128]{1,0:T(8,128)S(1)}, f32[8,128]{1,0:T(8,128)S(1)}, u32[]{:S(2)}, u32[]{:S(2)}) collective-permute-start(f32[8,128]{1,0:T(8,128)S(1)} %get-tuple-element.44.lse_ref.guess_ref), channel_id=1, source_target_pairs={{0,1},{1,0},{2,3},{3,2},{4,5},{5,4},{6,7},{7,6},{8,9},{9,8},{10,11... | collective-permute-start | bytes 12296 | tf_op jit(solution)/shard_map/ppermute | solution.py:381
  29.7 1.0 collective-permute-done.1
  30.7 0.0 copy-start.2
  30.7 4.6 %collective-permute-start.2 = (f32[8,128]{1,0:T(8,128)S(1)}, f32[8,128]{1,0:T(8,128)S(1)}, u32[]{:S(2)}, u32[]{:S(2)}) collective-permute-start(f32[8,128]{1,0:T(8,128)S(1)} %log_add_fusion.8.one_ref), channel_id=1, source_target_pairs={{0,3},{1,2},{2,1},{3,0},{4,7},{5,6},{6,5},{7,4},{8,11},{9,10},{10,... | collective-permute-start | bytes 12296 | tf_op jit(solution)/shard_map/ppermute | solution.py:381
  35.3 2.1 %col_guess.1 = (bf16[128,2048]{1,0:T(8,128)(2,1)S(1)}, bf16[128,2048]{1,0:T(8,128)(2,1)S(1)}, bf16[1024,128]{1,0:T(8,128)(2,1)S(1)}, f32[1,2048]{1,0:T(1,128)S(1)}, f32[1,2048]{1,0:T(1,128)S(1)}) custom-call(bf16[1024,128]{1,0:T(8,128)(2,1)S(1)} %get-tuple-element.36.a_ref, f32[8,128]{1,0:T(8,128)S(1)} %get-tuple-element.37.r_ref, ...), custom_call_target="tpu_custom_call" | custom-call | flops 1073741824 | bytes 2000000 | tf_op jit(solution)/shard_map/col_guess/pallas_call | solution.py:365
  37.4 0.0 collective-permute-done.2.two_ref
  37.4 2.3 %far_col_lse.3 = (f32[1,2048]{1,0:T(1,128)S(1)}, f32[8,128]{1,0:T(8,128)}, bf16[1024,128]{1,0:T(8,128)(2,1)S(1)}) custom-call(bf16[1024,128]{1,0:T(8,128)(2,1)S(1)} %get-tuple-element.36.a_ref, f32[8,128]{1,0:T(8,128)S(1)} %get-tuple-element.37.r_ref, f32[8,128]{1,0:T(8,128)S(1)} %bitcast.20, f32[8,128]{1,0:T(8,128)S(1)} %log_add_fusion.8.one_ref, ...), custom_call_target="tpu_custom_call" | custom-call | flops 536870912 | bytes 2000000 | tf_op jit(solution)/shard_map/far_col_lse/pallas_call | solution.py:365
  39.7 1.4 %collective-permute-start.3 = (f32[1,2048]{1,0:T(1,128)S(1)}, f32[1,2048]{1,0:T(1,128)S(1)}, u32[]{:S(2)}, u32[]{:S(2)}) collective-permute-start(f32[1,2048]{1,0:T(1,128)S(1)} %get-tuple-element.52.far_guess_ref.guess_ref), channel_id=1, source_target_pairs={{0,4},{4,0},{8,12},{12,8},{16,20},{20,16},{24,28},{28,24},{32,36},... | collective-permute-start | bytes 24584 | tf_op jit(solution)/shard_map/ppermute | solution.py:381
  41.1 1.6 %near_col_lse.3.near_guess_ref.guess_ref = f32[1,2048]{1,0:T(1,128)S(1)} custom-call(bf16[1024,128]{1,0:T(8,128)(2,1)S(1)} %get-tuple-element.49.left_ref, bf16[128,2048]{1,0:T(8,128)(2,1)S(1)} %get-tuple-element.38.near_b_ref.b_ref, f32[1,2048]{1,0:T(1,128)S(1)} %get-tuple-element.39.near_c_ref.c_ref, bf16[128,2048]{1,0:T(8,128)(2,1)S(1)} %get-tuple-element.50.ready_ref, ...), custom_call_target="tpu_custom_call" | custom-call | flops 536870912 | bytes 2000000 | tf_op jit(solution)/shard_map/near_col_lse/pallas_call | solution.py:365
  42.8 12.0 %all_to_all.21 = f32[32,16,128]{2,1,0:T(8,128)S(1)} all-to-all(f32[32,16,128]{2,1,0:T(8,128)S(1)} %broadcast_in_dim.20), channel_id=1, replica_groups={{0,8,16,24,32,40,48,56,64,72,80,88,96,104,112,120,128,136,144,152,160,1..., dimensions={0} | all-to-all | bytes 524288 | tf_op jit(solution)/shard_map/all_to_all | solution.py:393
  54.9 0.1 exponential_reduce_fusion.2
  55.0 1.7 %collective-permute-start.4 = (f32[1,2048]{1,0:T(1,128)S(1)}, f32[1,2048]{1,0:T(1,128)S(1)}, u32[]{:S(2)}, u32[]{:S(2)}) collective-permute-start(f32[1,2048]{1,0:T(1,128)S(1)} %bitcast.10), channel_id=1, source_target_pairs={{0,4},{4,0},{8,12},{12,8},{16,20},{20,16},{24,28},{28,24},{32,36},... | collective-permute-start | bytes 24584 | tf_op jit(solution)/shard_map/ppermute | solution.py:381
  56.6 1.5 %near_row_lse.2.acc_ref = f32[1024,128]{1,0:T(8,128)S(1)} custom-call(bf16[128,2048]{1,0:T(8,128)(2,1)S(1)} %get-tuple-element.38.near_b_ref.b_ref, f32[1,2048]{1,0:T(1,128)S(1)} %get-tuple-element.39.near_c_ref.c_ref, f32[1,2048]{1,0:T(1,128)S(1)} %get-tuple-element.40.near_w_ref.w_ref, f32[1,2048]{1,0:T(1,128)S(1)} %bitcast.11, ...), custom_call_target="tpu_custom_call" | custom-call | flops 536870912 | bytes 2000000 | tf_op jit(solution)/shard_map/near_row_lse/pallas_call | solution.py:365
  58.2 0.0 collective-permute-done.4.lse_ref
  58.2 1.5 %row_lse.2.lse_ref.guess_ref = f32[8,128]{1,0:T(8,128)S(1)} custom-call(bf16[1024,128]{1,0:T(8,128)(2,1)S(1)} %get-tuple-element.36.a_ref, f32[8,128]{1,0:T(8,128)S(1)} %get-tuple-element.37.r_ref, bf16[128,2048]{1,0:T(8,128)(2,1)S(1)} %get-tuple-element.38.near_b_ref.b_ref, f32[1,2048]{1,0:T(1,128)S(1)} %get-tuple-element.39.near_c_ref.c_ref, ...), custom_call_target="tpu_custom_call" | custom-call | flops 536870912 | bytes 2000000 | tf_op jit(solution)/shard_map/row_lse/pallas_call | solution.py:365
  59.7 1.3 collective-permute-start.5
  61.0 2.2 %collective-permute-done.5 = f32[8,128]{1,0:T(8,128)S(1)} collective-permute-done((f32[8,128]{1,0:T(8,128)S(1)}, f32[8,128]{1,0:T(8,128)S(1)}, u32[]{:S(2)}, u32[]{:S(2)}) %collective-permute-start.5) | collective-permute-done | bytes 4128 | tf_op jit(solution)/shard_map/ppermute | solution.py:381
  63.2 3.4 %collective-permute-start.6 = (f32[8,128]{1,0:T(8,128)S(1)}, f32[8,128]{1,0:T(8,128)S(1)}, u32[]{:S(2)}, u32[]{:S(2)}) collective-permute-start(f32[8,128]{1,0:T(8,128)S(1)} %log_add_fusion.7.one_ref), channel_id=1, source_target_pairs={{0,3},{1,2},{2,1},{3,0},{4,7},{5,6},{6,5},{7,4},{8,11},{9,10},{10,... | collective-permute-start | bytes 12296 | tf_op jit(solution)/shard_map/ppermute | solution.py:381
  66.5 0.2 prepare.2
  66.7 1.1 collective-permute-done.6.two_ref
  67.8 2.3 %far_col_lse.4 = (f32[1,2048]{1,0:T(1,128)S(1)}, f32[8,128]{1,0:T(8,128)}, bf16[1024,128]{1,0:T(8,128)(2,1)S(1)}) custom-call(bf16[1024,128]{1,0:T(8,128)(2,1)S(1)} %get-tuple-element.36.a_ref, f32[8,128]{1,0:T(8,128)S(1)} %get-tuple-element.37.r_ref, f32[8,128]{1,0:T(8,128)S(1)} %bitcast.21, f32[8,128]{1,0:T(8,128)S(1)} %log_add_fusion.7.one_ref, ...), custom_call_target="tpu_custom_call" | custom-call | flops 536870912 | bytes 2000000 | tf_op jit(solution)/shard_map/far_col_lse/pallas_call | solution.py:365
  70.1 2.3 %collective-permute-start.7 = (f32[1,2048]{1,0:T(1,128)S(1)}, f32[1,2048]{1,0:T(1,128)S(1)}, u32[]{:S(2)}, u32[]{:S(2)}) collective-permute-start(f32[1,2048]{1,0:T(1,128)S(1)} %get-tuple-element.58.far_guess_ref.guess_ref), channel_id=1, source_target_pairs={{0,4},{4,0},{8,12},{12,8},{16,20},{20,16},{24,28},{28,24},{32,36},... | collective-permute-start | bytes 24584 | tf_op jit(solution)/shard_map/ppermute | solution.py:381
  72.4 1.6 %near_col_lse.4.near_guess_ref.guess_ref = f32[1,2048]{1,0:T(1,128)S(1)} custom-call(bf16[1024,128]{1,0:T(8,128)(2,1)S(1)} %get-tuple-element.56.left_ref, bf16[128,2048]{1,0:T(8,128)(2,1)S(1)} %get-tuple-element.38.near_b_ref.b_ref, f32[1,2048]{1,0:T(1,128)S(1)} %get-tuple-element.39.near_c_ref.c_ref, bf16[128,2048]{1,0:T(8,128)(2,1)S(1)} %get-tuple-element.57.ready_ref, ...), custom_call_target="tpu_custom_call" | custom-call | flops 536870912 | bytes 2000000 | tf_op jit(solution)/shard_map/near_col_lse/pallas_call | solution.py:365
  74.0 0.0 collective-permute-done.7
  74.1 12.1 %all_to_all.22 = f32[32,16,128]{2,1,0:T(8,128)S(1)} all-to-all(f32[32,16,128]{2,1,0:T(8,128)S(1)} %broadcast_in_dim.21), channel_id=1, replica_groups={{0,8,16,24,32,40,48,56,64,72,80,88,96,104,112,120,128,136,144,152,160,1..., dimensions={0} | all-to-all | bytes 524288 | tf_op jit(solution)/shard_map/all_to_all | solution.py:393
  86.2 0.1 exponential_reduce_fusion.1
  86.3 1.5 %collective-permute-start.8 = (f32[1,2048]{1,0:T(1,128)S(1)}, f32[1,2048]{1,0:T(1,128)S(1)}, u32[]{:S(2)}, u32[]{:S(2)}) collective-permute-start(f32[1,2048]{1,0:T(1,128)S(1)} %bitcast.13), channel_id=1, source_target_pairs={{0,4},{4,0},{8,12},{12,8},{16,20},{20,16},{24,28},{28,24},{32,36},... | collective-permute-start | bytes 24584 | tf_op jit(solution)/shard_map/ppermute | solution.py:381
  87.8 1.5 %near_row_lse.3.acc_ref = f32[1024,128]{1,0:T(8,128)S(1)} custom-call(bf16[128,2048]{1,0:T(8,128)(2,1)S(1)} %get-tuple-element.38.near_b_ref.b_ref, f32[1,2048]{1,0:T(1,128)S(1)} %get-tuple-element.39.near_c_ref.c_ref, f32[1,2048]{1,0:T(1,128)S(1)} %get-tuple-element.40.near_w_ref.w_ref, f32[1,2048]{1,0:T(1,128)S(1)} %bitcast.14, ...), custom_call_target="tpu_custom_call" | custom-call | flops 536870912 | bytes 2000000 | tf_op jit(solution)/shard_map/near_row_lse/pallas_call | solution.py:365
  89.3 1.5 %row_lse.3.lse_ref = f32[8,128]{1,0:T(8,128)S(1)} custom-call(bf16[1024,128]{1,0:T(8,128)(2,1)S(1)} %get-tuple-element.36.a_ref, f32[8,128]{1,0:T(8,128)S(1)} %get-tuple-element.37.r_ref, bf16[128,2048]{1,0:T(8,128)(2,1)S(1)} %get-tuple-element.38.near_b_ref.b_ref, f32[1,2048]{1,0:T(1,128)S(1)} %get-tuple-element.39.near_c_ref.c_ref, ...), custom_call_target="tpu_custom_call" | custom-call | flops 536870912 | bytes 2000000 | tf_op jit(solution)/shard_map/row_lse/pallas_call | solution.py:365
  90.8 1.3 collective-permute-start.9
  92.1 2.2 %collective-permute-done.9 = f32[8,128]{1,0:T(8,128)S(1)} collective-permute-done((f32[8,128]{1,0:T(8,128)S(1)}, f32[8,128]{1,0:T(8,128)S(1)}, u32[]{:S(2)}, u32[]{:S(2)}) %collective-permute-start.9) | collective-permute-done | bytes 4128 | tf_op jit(solution)/shard_map/ppermute | solution.py:381
  94.3 3.6 %collective-permute-start.10 = (f32[8,128]{1,0:T(8,128)S(1)}, f32[8,128]{1,0:T(8,128)S(1)}, u32[]{:S(2)}, u32[]{:S(2)}) collective-permute-start(f32[8,128]{1,0:T(8,128)S(1)} %log_add_fusion.6.one_ref), channel_id=1, source_target_pairs={{0,3},{1,2},{2,1},{3,0},{4,7},{5,6},{6,5},{7,4},{8,11},{9,10},{10,... | collective-permute-start | bytes 12296 | tf_op jit(solution)/shard_map/ppermute | solution.py:381
  97.9 0.1 prepare.3
  98.0 1.2 collective-permute-done.10.two_ref
  99.2 2.3 %far_col_lse.5 = (f32[1,2048]{1,0:T(1,128)S(1)}, f32[8,128]{1,0:T(8,128)}, bf16[1024,128]{1,0:T(8,128)(2,1)S(1)}) custom-call(bf16[1024,128]{1,0:T(8,128)(2,1)S(1)} %get-tuple-element.36.a_ref, f32[8,128]{1,0:T(8,128)S(1)} %get-tuple-element.37.r_ref, f32[8,128]{1,0:T(8,128)S(1)} %bitcast.22, f32[8,128]{1,0:T(8,128)S(1)} %log_add_fusion.6.one_ref, ...), custom_call_target="tpu_custom_call" | custom-call | flops 536870912 | bytes 2000000 | tf_op jit(solution)/shard_map/far_col_lse/pallas_call | solution.py:365
  101.5 2.3 %collective-permute-start.11 = (f32[1,2048]{1,0:T(1,128)S(1)}, f32[1,2048]{1,0:T(1,128)S(1)}, u32[]{:S(2)}, u32[]{:S(2)}) collective-permute-start(f32[1,2048]{1,0:T(1,128)S(1)} %get-tuple-element.64), channel_id=1, source_target_pairs={{0,4},{4,0},{8,12},{12,8},{16,20},{20,16},{24,28},{28,24},{32,36},... | collective-permute-start | bytes 24584 | tf_op jit(solution)/shard_map/ppermute | solution.py:381
  103.8 1.6 %near_col_lse.5 = f32[1,2048]{1,0:T(1,128)S(1)} custom-call(bf16[1024,128]{1,0:T(8,128)(2,1)S(1)} %get-tuple-element.62.left_ref, bf16[128,2048]{1,0:T(8,128)(2,1)S(1)} %get-tuple-element.38.near_b_ref.b_ref, f32[1,2048]{1,0:T(1,128)S(1)} %get-tuple-element.39.near_c_ref.c_ref, bf16[128,2048]{1,0:T(8,128)(2,1)S(1)} %get-tuple-element.63.ready_ref, ...), custom_call_target="tpu_custom_call" | custom-call | flops 536870912 | bytes 2000000 | tf_op jit(solution)/shard_map/near_col_lse/pallas_call | solution.py:365
  105.4 0.0 collective-permute-done.11
  105.5 12.1 %all_to_all.23 = f32[32,16,128]{2,1,0:T(8,128)S(1)} all-to-all(f32[32,16,128]{2,1,0:T(8,128)S(1)} %broadcast_in_dim.22), channel_id=1, replica_groups={{0,8,16,24,32,40,48,56,64,72,80,88,96,104,112,120,128,136,144,152,160,1..., dimensions={0} | all-to-all | bytes 524288 | tf_op jit(solution)/shard_map/all_to_all | solution.py:393
  117.6 0.1 exponential_reduce_fusion
  117.7 1.5 %collective-permute-start.12 = (f32[1,2048]{1,0:T(1,128)S(1)}, f32[1,2048]{1,0:T(1,128)S(1)}, u32[]{:S(2)}, u32[]{:S(2)}) collective-permute-start(f32[1,2048]{1,0:T(1,128)S(1)} %bitcast.16), channel_id=1, source_target_pairs={{0,4},{4,0},{8,12},{12,8},{16,20},{20,16},{24,28},{28,24},{32,36},... | collective-permute-start | bytes 24584 | tf_op jit(solution)/shard_map/ppermute | solution.py:381
  119.2 1.8 %near_plan.1 = (f32[512,128]{1,0:T(8,128)S(1)}, f32[512,64]{1,0:T(8,128)S(1)}) custom-call(bf16[1024,128]{1,0:T(8,128)(2,1)S(1)} %get-tuple-element.62.left_ref, bf16[128,2048]{1,0:T(8,128)(2,1)S(1)} %get-tuple-element.38.near_b_ref.b_ref, f32[1,2048]{1,0:T(1,128)S(1)} %get-tuple-element.39.near_c_ref.c_ref, ...), custom_call_target="tpu_custom_call" | custom-call | flops 536870912 | bytes 2000000 | tf_op jit(solution)/shard_map/near_plan/pallas_call | solution.py:365
  121.0 0.0 collective-permute-done.12.lse_ref
  121.0 1.7 %first_plan.1 = bf16[64,512]{1,0:T(8,128)(2,1)S(1)} custom-call(bf16[64,1024]{1,0:T(8,128)(2,1)S(1)} %copy-done, bf16[1024,128]{1,0:T(8,128)(2,1)S(1)} %get-tuple-element.62.left_ref, bf16[128,2048]{1,0:T(8,128)(2,1)S(1)} %get-tuple-element.45.far_b_ref.b_ref, f32[1,2048]{1,0:T(1,128)S(1)} %get-tuple-element.46.far_c_ref.c_ref, ...), custom_call_target="tpu_custom_call" | custom-call | flops 536870912 | bytes 2000000 | tf_op jit(solution)/shard_map/first_plan/pallas_call | solution.py:365
  122.7 1.3 collective-permute-start.13
  124.0 3.2 %last_plan.1 = (bf16[64,512]{1,0:T(8,128)(2,1)S(1)}, f32[1,64]{1,0:T(1,128)}) custom-call(bf16[64,1024]{1,0:T(8,128)(2,1)S(1)} %copy-done, bf16[1024,128]{1,0:T(8,128)(2,1)S(1)} %get-tuple-element.62.left_ref, bf16[128,2048]{1,0:T(8,128)(2,1)S(1)} %get-tuple-element.38.near_b_ref.b_ref, f32[1,2048]{1,0:T(1,128)S(1)} %get-tuple-element.39.near_c_ref.c_ref, ...), custom_call_target="tpu_custom_call" | custom-call | flops 1073741824 | bytes 2000000 | tf_op jit(solution)/shard_map/last_plan/pallas_call | solution.py:365
  127.2 1.3 collective-permute-start.14
  128.4 0.6 collective-permute-done.13
  129.1 2.7 %collective-permute-start.15 = (bf16[64,512]{1,0:T(8,128)(2,1)S(1)}, bf16[64,512]{1,0:T(8,128)(2,1)S(1)}, u32[]{:S(2)}, u32[]{:S(2)}) collective-permute-start(bf16[64,512]{1,0:T(8,128)(2,1)S(1)} %reduce-precision_convert_fusion.1), channel_id=1, source_target_pairs={{0,3},{1,2},{2,1},{3,0},{4,7},{5,6},{6,5},{7,4},{8,11},{9,10},{10,... | collective-permute-start | bytes 196616 | tf_op jit(solution)/shard_map/ppermute | solution.py:381
  131.8 1.7 %collective-permute-done.14 = bf16[64,512]{1,0:T(8,128)(2,1)S(1)} collective-permute-done((bf16[64,512]{1,0:T(8,128)(2,1)S(1)}, bf16[64,512]{1,0:T(8,128)(2,1)S(1)}, u32[]{:S(2)}, u32[]{:S(2)}) %collective-permute-start.14) | collective-permute-done | bytes 65568 | tf_op jit(solution)/shard_map/ppermute | solution.py:381
  133.5 1.4 %collective-permute-start.16 = (bf16[64,512]{1,0:T(8,128)(2,1)S(1)}, bf16[64,512]{1,0:T(8,128)(2,1)S(1)}, u32[]{:S(2)}, u32[]{:S(2)}) collective-permute-start(bf16[64,512]{1,0:T(8,128)(2,1)S(1)} %reduce-precision_convert_fusion), channel_id=1, source_target_pairs={{0,3},{1,2},{2,1},{3,0},{4,7},{5,6},{6,5},{7,4},{8,11},{9,10},{10,... | collective-permute-start | bytes 196616 | tf_op jit(solution)/shard_map/ppermute | solution.py:381
  135.0 4.0 %collective-permute-done.16 = bf16[64,512]{1,0:T(8,128)(2,1)S(1)} collective-permute-done((bf16[64,512]{1,0:T(8,128)(2,1)S(1)}, bf16[64,512]{1,0:T(8,128)(2,1)S(1)}, u32[]{:S(2)}, u32[]{:S(2)}) %collective-permute-start.16) | collective-permute-done | bytes 65568 | tf_op jit(solution)/shard_map/ppermute | solution.py:381
  139.0 0.7 convert_add_fusion
  (26 shorter events, 0.5 us)
Async XLA Ops:
  1.3 0.7 copy-start.3
  1.3 0.7 copy-start.4
  2.2 20.3 %copy-start = (bf16[64,1024]{1,0:T(8,128)(2,1)S(1)}, bf16[64,1024]{1,0:T(8,128)(2,1)}, u32[]{:S(2)}) copy-start(bf16[64,1024]{1,0:T(8,128)(2,1)} %emb_ref.5) | copy-start | bytes 393220
  2.2 20.3 %copy-start.1 = (f32[2,1024]{1,0:T(2,128)S(1)}, f32[2,1024]{1,0:T(2,128)}, u32[]{:S(2)}) copy-start(f32[2,1024]{1,0:T(2,128)} %pos_ref.1) | copy-start | bytes 24580
  20.5 4.3 %collective-permute-start = (bf16[32,34,128]{2,1,0:T(8,128)(2,1)S(1)}, bf16[32,34,128]{2,1,0:T(8,128)(2,1)S(1)}, u32[]{:S(2)}, u32[]{:S(2)}) collective-permute-start(bf16[32,34,128]{2,1,0:T(8,128)(2,1)S(1)} %all_to_all.20.pack_ref), channel_id=1, source_target_pairs={{0,4},{4,0},{8,12},{12,8},{16,20},{20,16},{24,28},{28,24},{32,36},... | collective-permute-start | bytes 835592 | tf_op jit(solution)/shard_map/ppermute | solution.py:381
  26.6 4.1 %collective-permute-start.1 = (f32[8,128]{1,0:T(8,128)S(1)}, f32[8,128]{1,0:T(8,128)S(1)}, u32[]{:S(2)}, u32[]{:S(2)}) collective-permute-start(f32[8,128]{1,0:T(8,128)S(1)} %get-tuple-element.44.lse_ref.guess_ref), channel_id=1, source_target_pairs={{0,1},{1,0},{2,3},{3,2},{4,5},{5,4},{6,7},{7,6},{8,9},{9,8},{10,11... | collective-permute-start | bytes 12296 | tf_op jit(solution)/shard_map/ppermute | solution.py:381
  30.7 4.6 %copy-start.2 = (f32[1024]{0:T(1024)S(1)}, f32[1024]{0:T(1024)}, u32[]{:S(2)}) copy-start(f32[1024]{0:T(1024)} %param.8) | copy-start | bytes 12292
  30.7 6.7 %collective-permute-start.2 = (f32[8,128]{1,0:T(8,128)S(1)}, f32[8,128]{1,0:T(8,128)S(1)}, u32[]{:S(2)}, u32[]{:S(2)}) collective-permute-start(f32[8,128]{1,0:T(8,128)S(1)} %log_add_fusion.8.one_ref), channel_id=1, source_target_pairs={{0,3},{1,2},{2,1},{3,0},{4,7},{5,6},{6,5},{7,4},{8,11},{9,10},{10,... | collective-permute-start | bytes 12296 | tf_op jit(solution)/shard_map/ppermute | solution.py:381
  39.7 3.0 %collective-permute-start.3 = (f32[1,2048]{1,0:T(1,128)S(1)}, f32[1,2048]{1,0:T(1,128)S(1)}, u32[]{:S(2)}, u32[]{:S(2)}) collective-permute-start(f32[1,2048]{1,0:T(1,128)S(1)} %get-tuple-element.52.far_guess_ref.guess_ref), channel_id=1, source_target_pairs={{0,4},{4,0},{8,12},{12,8},{16,20},{20,16},{24,28},{28,24},{32,36},... | collective-permute-start | bytes 24584 | tf_op jit(solution)/shard_map/ppermute | solution.py:381
  55.0 3.2 %collective-permute-start.4 = (f32[1,2048]{1,0:T(1,128)S(1)}, f32[1,2048]{1,0:T(1,128)S(1)}, u32[]{:S(2)}, u32[]{:S(2)}) collective-permute-start(f32[1,2048]{1,0:T(1,128)S(1)} %bitcast.10), channel_id=1, source_target_pairs={{0,4},{4,0},{8,12},{12,8},{16,20},{20,16},{24,28},{28,24},{32,36},... | collective-permute-start | bytes 24584 | tf_op jit(solution)/shard_map/ppermute | solution.py:381
  59.7 3.5 %collective-permute-start.5 = (f32[8,128]{1,0:T(8,128)S(1)}, f32[8,128]{1,0:T(8,128)S(1)}, u32[]{:S(2)}, u32[]{:S(2)}) collective-permute-start(f32[8,128]{1,0:T(8,128)S(1)} %row_lse.2.lse_ref.guess_ref), channel_id=1, source_target_pairs={{0,1},{1,0},{2,3},{3,2},{4,5},{5,4},{6,7},{7,6},{8,9},{9,8},{10,11... | collective-permute-start | bytes 12296 | tf_op jit(solution)/shard_map/ppermute | solution.py:381
  63.2 4.7 %collective-permute-start.6 = (f32[8,128]{1,0:T(8,128)S(1)}, f32[8,128]{1,0:T(8,128)S(1)}, u32[]{:S(2)}, u32[]{:S(2)}) collective-permute-start(f32[8,128]{1,0:T(8,128)S(1)} %log_add_fusion.7.one_ref), channel_id=1, source_target_pairs={{0,3},{1,2},{2,1},{3,0},{4,7},{5,6},{6,5},{7,4},{8,11},{9,10},{10,... | collective-permute-start | bytes 12296 | tf_op jit(solution)/shard_map/ppermute | solution.py:381
  70.1 3.9 %collective-permute-start.7 = (f32[1,2048]{1,0:T(1,128)S(1)}, f32[1,2048]{1,0:T(1,128)S(1)}, u32[]{:S(2)}, u32[]{:S(2)}) collective-permute-start(f32[1,2048]{1,0:T(1,128)S(1)} %get-tuple-element.58.far_guess_ref.guess_ref), channel_id=1, source_target_pairs={{0,4},{4,0},{8,12},{12,8},{16,20},{20,16},{24,28},{28,24},{32,36},... | collective-permute-start | bytes 24584 | tf_op jit(solution)/shard_map/ppermute | solution.py:381
  86.3 3.0 %collective-permute-start.8 = (f32[1,2048]{1,0:T(1,128)S(1)}, f32[1,2048]{1,0:T(1,128)S(1)}, u32[]{:S(2)}, u32[]{:S(2)}) collective-permute-start(f32[1,2048]{1,0:T(1,128)S(1)} %bitcast.13), channel_id=1, source_target_pairs={{0,4},{4,0},{8,12},{12,8},{16,20},{20,16},{24,28},{28,24},{32,36},... | collective-permute-start | bytes 24584 | tf_op jit(solution)/shard_map/ppermute | solution.py:381
  90.8 3.5 %collective-permute-start.9 = (f32[8,128]{1,0:T(8,128)S(1)}, f32[8,128]{1,0:T(8,128)S(1)}, u32[]{:S(2)}, u32[]{:S(2)}) collective-permute-start(f32[8,128]{1,0:T(8,128)S(1)} %row_lse.3.lse_ref), channel_id=1, source_target_pairs={{0,1},{1,0},{2,3},{3,2},{4,5},{5,4},{6,7},{7,6},{8,9},{9,8},{10,11... | collective-permute-start | bytes 12296 | tf_op jit(solution)/shard_map/ppermute | solution.py:381
  94.3 4.9 %collective-permute-start.10 = (f32[8,128]{1,0:T(8,128)S(1)}, f32[8,128]{1,0:T(8,128)S(1)}, u32[]{:S(2)}, u32[]{:S(2)}) collective-permute-start(f32[8,128]{1,0:T(8,128)S(1)} %log_add_fusion.6.one_ref), channel_id=1, source_target_pairs={{0,3},{1,2},{2,1},{3,0},{4,7},{5,6},{6,5},{7,4},{8,11},{9,10},{10,... | collective-permute-start | bytes 12296 | tf_op jit(solution)/shard_map/ppermute | solution.py:381
  101.5 3.9 %collective-permute-start.11 = (f32[1,2048]{1,0:T(1,128)S(1)}, f32[1,2048]{1,0:T(1,128)S(1)}, u32[]{:S(2)}, u32[]{:S(2)}) collective-permute-start(f32[1,2048]{1,0:T(1,128)S(1)} %get-tuple-element.64), channel_id=1, source_target_pairs={{0,4},{4,0},{8,12},{12,8},{16,20},{20,16},{24,28},{28,24},{32,36},... | collective-permute-start | bytes 24584 | tf_op jit(solution)/shard_map/ppermute | solution.py:381
  117.7 3.3 %collective-permute-start.12 = (f32[1,2048]{1,0:T(1,128)S(1)}, f32[1,2048]{1,0:T(1,128)S(1)}, u32[]{:S(2)}, u32[]{:S(2)}) collective-permute-start(f32[1,2048]{1,0:T(1,128)S(1)} %bitcast.16), channel_id=1, source_target_pairs={{0,4},{4,0},{8,12},{12,8},{16,20},{20,16},{24,28},{28,24},{32,36},... | collective-permute-start | bytes 24584 | tf_op jit(solution)/shard_map/ppermute | solution.py:381
  122.7 6.4 %collective-permute-start.13 = (bf16[64,512]{1,0:T(8,128)(2,1)S(1)}, bf16[64,512]{1,0:T(8,128)(2,1)S(1)}, u32[]{:S(2)}, u32[]{:S(2)}) collective-permute-start(bf16[64,512]{1,0:T(8,128)(2,1)S(1)} %first_plan.1), channel_id=1, source_target_pairs={{0,1},{1,0},{2,3},{3,2},{4,5},{5,4},{6,7},{7,6},{8,9},{9,8},{10,11... | collective-permute-start | bytes 196616 | tf_op jit(solution)/shard_map/ppermute | solution.py:381
  127.2 6.4 %collective-permute-start.14 = (bf16[64,512]{1,0:T(8,128)(2,1)S(1)}, bf16[64,512]{1,0:T(8,128)(2,1)S(1)}, u32[]{:S(2)}, u32[]{:S(2)}) collective-permute-start(bf16[64,512]{1,0:T(8,128)(2,1)S(1)} %get-tuple-element.68), channel_id=1, source_target_pairs={{0,1},{1,0},{2,3},{3,2},{4,5},{5,4},{6,7},{7,6},{8,9},{9,8},{10,11... | collective-permute-start | bytes 196616 | tf_op jit(solution)/shard_map/ppermute | solution.py:381
  129.1 5.9 %collective-permute-start.15 = (bf16[64,512]{1,0:T(8,128)(2,1)S(1)}, bf16[64,512]{1,0:T(8,128)(2,1)S(1)}, u32[]{:S(2)}, u32[]{:S(2)}) collective-permute-start(bf16[64,512]{1,0:T(8,128)(2,1)S(1)} %reduce-precision_convert_fusion.1), channel_id=1, source_target_pairs={{0,3},{1,2},{2,1},{3,0},{4,7},{5,6},{6,5},{7,4},{8,11},{9,10},{10,... | collective-permute-start | bytes 196616 | tf_op jit(solution)/shard_map/ppermute | solution.py:381
  133.5 5.4 %collective-permute-start.16 = (bf16[64,512]{1,0:T(8,128)(2,1)S(1)}, bf16[64,512]{1,0:T(8,128)(2,1)S(1)}, u32[]{:S(2)}, u32[]{:S(2)}) collective-permute-start(bf16[64,512]{1,0:T(8,128)(2,1)S(1)} %reduce-precision_convert_fusion), channel_id=1, source_target_pairs={{0,3},{1,2},{2,1},{3,0},{4,7},{5,6},{6,5},{7,4},{8,11},{9,10},{10,... | collective-permute-start | bytes 196616 | tf_op jit(solution)/shard_map/ppermute | solution.py:381

commit v7 on v6

--- a/solution.py
+++ b/solution.py
@@ -279,7 +279,7 @@
     lse = joined(one_ref[...], two_ref[...])
     f_ref[...] = -LAM * EPS * lse
     set_source(a_ref, r_ref[...] + logw_ref[...] - LAM * lse, left_ref)
-    col_finish(NEAR, left_ref, b_ref, c_ref, ready_ref, guess_ref, out_ref, *rest)
+    col_finish(FAR, left_ref, b_ref, c_ref, ready_ref, guess_ref, out_ref, *rest)
 
 
 def near_col_kernel(left_ref, b_ref, c_ref, ready_ref, guess_ref, out_ref, *rest):
@@ -308,7 +308,7 @@
 def near_plan_kernel(left_ref, b_ref, c_ref, w_ref, lse_ref, mass_ref, pull_ref, b_s):
     mass_ref[...] = jnp.zeros_like(mass_ref)
     pull_ref[...] = jnp.zeros_like(pull_ref)
-    plan_pass(left_ref.at[0 : mass_ref.shape[0], :], b_ref, c_ref, w_ref, lse_ref, b_s, mass_ref, pull_ref, PLAN)
+    plan_pass(left_ref.at[0 : mass_ref.shape[0], :], b_ref, c_ref, w_ref, lse_ref, b_s, mass_ref, pull_ref, 2 * PLAN)
 
 
 def plan_finish(emb_ref, begin, mass_s, pull_s, out_ref):

time: 140 us -> 139 us (level)
  no operation moved by 1% of the time
where the time goes in v7:
time: 139 us
  blocking collectives  54.6 us (39%)
  starting transfers between devices  36.6 us (26%)
  Pallas kernels  29.9 us (22%)
  waiting for transfers between devices  14 us (10%)
  local copies, waits for them, and re-layouts  1.51 us (1%)
    all_to_all x4, blocking collectives, spread(): lax.all_to_all(block, 'src', 0, 0, axis_index_groups=groups, tiled=True)  54.6 us
    ppermute x17, starting transfers between devices, swapped(): lax.ppermute(value, axis, [(k, k ^ mask) for k in range(lax.axis_size(axi...  36.6 us
    pallas_call x18, Pallas kernels, call(): pl.pallas_call(kernel, out_shape=out_shape, scratch_shapes=[pltpu.VMEM(li...  29.9 us
    ppermute x17, waiting for transfers between devices, swapped(): lax.ppermute(value, axis, [(k, k ^ mask) for k in range(lax.axis_size(axi...  14 us
  transfers between devices with their start and end apart: 17, of which 8 were waited for; matrix products, arithmetic and copies ran while one was open for 0% of the time, Pallas kernels for 12%

profile of v7, /device:TPU:1, one launch (start us, length us, event | category | flops | bytes accessed | tf_op | source)
XLA Modules:
  0.0 138.7 jit_solution(16462757537797263585)
XLA Ops:
  0.6 0.7 fusion.6
  1.4 0.7 copy-done.3
  2.0 0.0 copy-done.4
  2.0 0.1 maximum_maximum_fusion
  2.2 0.0 copy-start
  2.2 0.0 copy-start.1
  2.2 18.4 %all_to_all.20.pack_ref = bf16[32,34,128]{2,1,0:T(8,128)(2,1)S(1)} all-to-all(bf16[32,34,128]{2,1,0:T(8,128)(2,1)S(1)} %broadcast_in_dim.19), channel_id=1, replica_groups={{0,8,16,24,32,40,48,56,64,72,80,88,96,104,112,120,128,136,144,152,160,1..., dimensions={0} | all-to-all | bytes 557056 | tf_op jit(solution)/shard_map/all_to_all | solution.py:393
  20.5 2.0 %collective-permute-start = (bf16[32,34,128]{2,1,0:T(8,128)(2,1)S(1)}, bf16[32,34,128]{2,1,0:T(8,128)(2,1)S(1)}, u32[]{:S(2)}, u32[]{:S(2)}) collective-permute-start(bf16[32,34,128]{2,1,0:T(8,128)(2,1)S(1)} %all_to_all.20.pack_ref), channel_id=1, source_target_pairs={{0,4},{4,0},{8,12},{12,8},{16,20},{20,16},{24,28},{28,24},{32,36},... | collective-permute-start | bytes 835592 | tf_op jit(solution)/shard_map/ppermute | solution.py:381
  22.5 2.3 %static_parts.1 = (bf16[1024,128]{1,0:T(8,128)(2,1)S(1)}, f32[8,128]{1,0:T(8,128)S(1)}, bf16[128,2048]{1,0:T(8,128)(2,1)S(1)}, f32[1,2048]{1,0:T(1,128)S(1)}, f3...) custom-call(bf16[64,1024]{1,0:T(8,128)(2,1)S(1)} %copy-done, ...), custom_call_target="tpu_custom_call" | custom-call | flops 536870912 | bytes 2000000 | tf_op jit(solution)/shard_map/static_parts/pallas_call | solution.py:365
  24.8 0.0 collective-permute-done.pack_ref
  24.8 1.8 %first_row_lse.1 = (f32[8,128]{1,0:T(8,128)S(1)}, bf16[128,2048]{1,0:T(8,128)(2,1)S(1)}, f32[1,2048]{1,0:T(1,128)S(1)}, f32[1,2048]{1,0:T(1,128)S(1)}) custom-call(bf16[1024,128]{1,0:T(8,128)(2,1)S(1)} %get-tuple-element.36.a_ref, f32[8,128]{1,0:T(8,128)S(1)} %get-tuple-element.37.r_ref, bf16[128,2048]{1,0:T(8,128)(2,1)S(1)} %get-tuple-element.38.near_b_ref.b_ref, ...), custom_call_target="tpu_custom_call" | custom-call | flops 536870912 | bytes 2000000 | tf_op jit(solution)/shard_map/first_row_lse/pallas_call | solution.py:365
  26.6 3.1 %collective-permute-start.1 = (f32[8,128]{1,0:T(8,128)S(1)}, f32[8,128]{1,0:T(8,128)S(1)}, u32[]{:S(2)}, u32[]{:S(2)}) collective-permute-start(f32[8,128]{1,0:T(8,128)S(1)} %get-tuple-element.44.lse_ref.guess_ref), channel_id=1, source_target_pairs={{0,1},{1,0},{2,3},{3,2},{4,5},{5,4},{6,7},{7,6},{8,9},{9,8},{10,11... | collective-permute-start | bytes 12296 | tf_op jit(solution)/shard_map/ppermute | solution.py:381
  29.7 1.0 collective-permute-done.1
  30.7 0.0 copy-start.2
  30.7 4.6 %collective-permute-start.2 = (f32[8,128]{1,0:T(8,128)S(1)}, f32[8,128]{1,0:T(8,128)S(1)}, u32[]{:S(2)}, u32[]{:S(2)}) collective-permute-start(f32[8,128]{1,0:T(8,128)S(1)} %log_add_fusion.8.one_ref), channel_id=1, source_target_pairs={{0,3},{1,2},{2,1},{3,0},{4,7},{5,6},{6,5},{7,4},{8,11},{9,10},{10,... | collective-permute-start | bytes 12296 | tf_op jit(solution)/shard_map/ppermute | solution.py:381
  35.3 2.1 %col_guess.1 = (bf16[128,2048]{1,0:T(8,128)(2,1)S(1)}, bf16[128,2048]{1,0:T(8,128)(2,1)S(1)}, bf16[1024,128]{1,0:T(8,128)(2,1)S(1)}, f32[1,2048]{1,0:T(1,128)S(1)}, f32[1,2048]{1,0:T(1,128)S(1)}) custom-call(bf16[1024,128]{1,0:T(8,128)(2,1)S(1)} %get-tuple-element.36.a_ref, f32[8,128]{1,0:T(8,128)S(1)} %get-tuple-element.37.r_ref, ...), custom_call_target="tpu_custom_call" | custom-call | flops 1073741824 | bytes 2000000 | tf_op jit(solution)/shard_map/col_guess/pallas_call | solution.py:365
  37.4 0.0 collective-permute-done.2.two_ref
  37.4 2.1 %far_col_lse.3 = (f32[1,2048]{1,0:T(1,128)S(1)}, f32[8,128]{1,0:T(8,128)}, bf16[1024,128]{1,0:T(8,128)(2,1)S(1)}) custom-call(bf16[1024,128]{1,0:T(8,128)(2,1)S(1)} %get-tuple-element.36.a_ref, f32[8,128]{1,0:T(8,128)S(1)} %get-tuple-element.37.r_ref, f32[8,128]{1,0:T(8,128)S(1)} %bitcast.20, f32[8,128]{1,0:T(8,128)S(1)} %log_add_fusion.8.one_ref, ...), custom_call_target="tpu_custom_call" | custom-call | flops 536870912 | bytes 2000000 | tf_op jit(solution)/shard_map/far_col_lse/pallas_call | solution.py:365
  39.5 1.4 %collective-permute-start.3 = (f32[1,2048]{1,0:T(1,128)S(1)}, f32[1,2048]{1,0:T(1,128)S(1)}, u32[]{:S(2)}, u32[]{:S(2)}) collective-permute-start(f32[1,2048]{1,0:T(1,128)S(1)} %get-tuple-element.52.far_guess_ref.guess_ref), channel_id=1, source_target_pairs={{0,4},{4,0},{8,12},{12,8},{16,20},{20,16},{24,28},{28,24},{32,36},... | collective-permute-start | bytes 24584 | tf_op jit(solution)/shard_map/ppermute | solution.py:381
  40.9 1.6 %near_col_lse.3.near_guess_ref.guess_ref = f32[1,2048]{1,0:T(1,128)S(1)} custom-call(bf16[1024,128]{1,0:T(8,128)(2,1)S(1)} %get-tuple-element.49.left_ref, bf16[128,2048]{1,0:T(8,128)(2,1)S(1)} %get-tuple-element.38.near_b_ref.b_ref, f32[1,2048]{1,0:T(1,128)S(1)} %get-tuple-element.39.near_c_ref.c_ref, bf16[128,2048]{1,0:T(8,128)(2,1)S(1)} %get-tuple-element.50.ready_ref, ...), custom_call_target="tpu_custom_call" | custom-call | flops 536870912 | bytes 2000000 | tf_op jit(solution)/shard_map/near_col_lse/pallas_call | solution.py:365
  42.5 0.0 collective-permute-done.3
  42.6 12.0 %all_to_all.21 = f32[32,16,128]{2,1,0:T(8,128)S(1)} all-to-all(f32[32,16,128]{2,1,0:T(8,128)S(1)} %broadcast_in_dim.20), channel_id=1, replica_groups={{0,8,16,24,32,40,48,56,64,72,80,88,96,104,112,120,128,136,144,152,160,1..., dimensions={0} | all-to-all | bytes 524288 | tf_op jit(solution)/shard_map/all_to_all | solution.py:393
  54.7 0.1 exponential_reduce_fusion.2
  54.7 1.7 %collective-permute-start.4 = (f32[1,2048]{1,0:T(1,128)S(1)}, f32[1,2048]{1,0:T(1,128)S(1)}, u32[]{:S(2)}, u32[]{:S(2)}) collective-permute-start(f32[1,2048]{1,0:T(1,128)S(1)} %bitcast.10), channel_id=1, source_target_pairs={{0,4},{4,0},{8,12},{12,8},{16,20},{20,16},{24,28},{28,24},{32,36},... | collective-permute-start | bytes 24584 | tf_op jit(solution)/shard_map/ppermute | solution.py:381
  56.4 1.5 %near_row_lse.2.acc_ref = f32[1024,128]{1,0:T(8,128)S(1)} custom-call(bf16[128,2048]{1,0:T(8,128)(2,1)S(1)} %get-tuple-element.38.near_b_ref.b_ref, f32[1,2048]{1,0:T(1,128)S(1)} %get-tuple-element.39.near_c_ref.c_ref, f32[1,2048]{1,0:T(1,128)S(1)} %get-tuple-element.40.near_w_ref.w_ref, f32[1,2048]{1,0:T(1,128)S(1)} %bitcast.11, ...), custom_call_target="tpu_custom_call" | custom-call | flops 536870912 | bytes 2000000 | tf_op jit(solution)/shard_map/near_row_lse/pallas_call | solution.py:365
  57.9 0.0 collective-permute-done.4.lse_ref
  58.0 1.5 %row_lse.2.lse_ref.guess_ref = f32[8,128]{1,0:T(8,128)S(1)} custom-call(bf16[1024,128]{1,0:T(8,128)(2,1)S(1)} %get-tuple-element.36.a_ref, f32[8,128]{1,0:T(8,128)S(1)} %get-tuple-element.37.r_ref, bf16[128,2048]{1,0:T(8,128)(2,1)S(1)} %get-tuple-element.38.near_b_ref.b_ref, f32[1,2048]{1,0:T(1,128)S(1)} %get-tuple-element.39.near_c_ref.c_ref, ...), custom_call_target="tpu_custom_call" | custom-call | flops 536870912 | bytes 2000000 | tf_op jit(solution)/shard_map/row_lse/pallas_call | solution.py:365
  59.5 1.3 collective-permute-start.5
  60.7 2.2 %collective-permute-done.5 = f32[8,128]{1,0:T(8,128)S(1)} collective-permute-done((f32[8,128]{1,0:T(8,128)S(1)}, f32[8,128]{1,0:T(8,128)S(1)}, u32[]{:S(2)}, u32[]{:S(2)}) %collective-permute-start.5) | collective-permute-done | bytes 4128 | tf_op jit(solution)/shard_map/ppermute | solution.py:381
  62.9 3.4 %collective-permute-start.6 = (f32[8,128]{1,0:T(8,128)S(1)}, f32[8,128]{1,0:T(8,128)S(1)}, u32[]{:S(2)}, u32[]{:S(2)}) collective-permute-start(f32[8,128]{1,0:T(8,128)S(1)} %log_add_fusion.7.one_ref), channel_id=1, source_target_pairs={{0,3},{1,2},{2,1},{3,0},{4,7},{5,6},{6,5},{7,4},{8,11},{9,10},{10,... | collective-permute-start | bytes 12296 | tf_op jit(solution)/shard_map/ppermute | solution.py:381
  66.3 0.2 prepare.2
  66.5 1.1 collective-permute-done.6.two_ref
  67.6 2.1 %far_col_lse.4 = (f32[1,2048]{1,0:T(1,128)S(1)}, f32[8,128]{1,0:T(8,128)}, bf16[1024,128]{1,0:T(8,128)(2,1)S(1)}) custom-call(bf16[1024,128]{1,0:T(8,128)(2,1)S(1)} %get-tuple-element.36.a_ref, f32[8,128]{1,0:T(8,128)S(1)} %get-tuple-element.37.r_ref, f32[8,128]{1,0:T(8,128)S(1)} %bitcast.21, f32[8,128]{1,0:T(8,128)S(1)} %log_add_fusion.7.one_ref, ...), custom_call_target="tpu_custom_call" | custom-call | flops 536870912 | bytes 2000000 | tf_op jit(solution)/shard_map/far_col_lse/pallas_call | solution.py:365
  69.7 2.3 %collective-permute-start.7 = (f32[1,2048]{1,0:T(1,128)S(1)}, f32[1,2048]{1,0:T(1,128)S(1)}, u32[]{:S(2)}, u32[]{:S(2)}) collective-permute-start(f32[1,2048]{1,0:T(1,128)S(1)} %get-tuple-element.58.far_guess_ref.guess_ref), channel_id=1, source_target_pairs={{0,4},{4,0},{8,12},{12,8},{16,20},{20,16},{24,28},{28,24},{32,36},... | collective-permute-start | bytes 24584 | tf_op jit(solution)/shard_map/ppermute | solution.py:381
  72.0 1.6 %near_col_lse.4.near_guess_ref.guess_ref = f32[1,2048]{1,0:T(1,128)S(1)} custom-call(bf16[1024,128]{1,0:T(8,128)(2,1)S(1)} %get-tuple-element.56.left_ref, bf16[128,2048]{1,0:T(8,128)(2,1)S(1)} %get-tuple-element.38.near_b_ref.b_ref, f32[1,2048]{1,0:T(1,128)S(1)} %get-tuple-element.39.near_c_ref.c_ref, bf16[128,2048]{1,0:T(8,128)(2,1)S(1)} %get-tuple-element.57.ready_ref, ...), custom_call_target="tpu_custom_call" | custom-call | flops 536870912 | bytes 2000000 | tf_op jit(solution)/shard_map/near_col_lse/pallas_call | solution.py:365
  73.6 0.0 collective-permute-done.7
  73.7 12.1 %all_to_all.22 = f32[32,16,128]{2,1,0:T(8,128)S(1)} all-to-all(f32[32,16,128]{2,1,0:T(8,128)S(1)} %broadcast_in_dim.21), channel_id=1, replica_groups={{0,8,16,24,32,40,48,56,64,72,80,88,96,104,112,120,128,136,144,152,160,1..., dimensions={0} | all-to-all | bytes 524288 | tf_op jit(solution)/shard_map/all_to_all | solution.py:393
  85.8 0.1 exponential_reduce_fusion.1
  85.9 1.5 %collective-permute-start.8 = (f32[1,2048]{1,0:T(1,128)S(1)}, f32[1,2048]{1,0:T(1,128)S(1)}, u32[]{:S(2)}, u32[]{:S(2)}) collective-permute-start(f32[1,2048]{1,0:T(1,128)S(1)} %bitcast.13), channel_id=1, source_target_pairs={{0,4},{4,0},{8,12},{12,8},{16,20},{20,16},{24,28},{28,24},{32,36},... | collective-permute-start | bytes 24584 | tf_op jit(solution)/shard_map/ppermute | solution.py:381
  87.4 1.5 %near_row_lse.3.acc_ref = f32[1024,128]{1,0:T(8,128)S(1)} custom-call(bf16[128,2048]{1,0:T(8,128)(2,1)S(1)} %get-tuple-element.38.near_b_ref.b_ref, f32[1,2048]{1,0:T(1,128)S(1)} %get-tuple-element.39.near_c_ref.c_ref, f32[1,2048]{1,0:T(1,128)S(1)} %get-tuple-element.40.near_w_ref.w_ref, f32[1,2048]{1,0:T(1,128)S(1)} %bitcast.14, ...), custom_call_target="tpu_custom_call" | custom-call | flops 536870912 | bytes 2000000 | tf_op jit(solution)/shard_map/near_row_lse/pallas_call | solution.py:365
  88.9 0.0 collective-permute-done.8.lse_ref
  88.9 1.5 %row_lse.3.lse_ref = f32[8,128]{1,0:T(8,128)S(1)} custom-call(bf16[1024,128]{1,0:T(8,128)(2,1)S(1)} %get-tuple-element.36.a_ref, f32[8,128]{1,0:T(8,128)S(1)} %get-tuple-element.37.r_ref, bf16[128,2048]{1,0:T(8,128)(2,1)S(1)} %get-tuple-element.38.near_b_ref.b_ref, f32[1,2048]{1,0:T(1,128)S(1)} %get-tuple-element.39.near_c_ref.c_ref, ...), custom_call_target="tpu_custom_call" | custom-call | flops 536870912 | bytes 2000000 | tf_op jit(solution)/shard_map/row_lse/pallas_call | solution.py:365
  90.4 1.3 collective-permute-start.9
  91.7 2.2 %collective-permute-done.9 = f32[8,128]{1,0:T(8,128)S(1)} collective-permute-done((f32[8,128]{1,0:T(8,128)S(1)}, f32[8,128]{1,0:T(8,128)S(1)}, u32[]{:S(2)}, u32[]{:S(2)}) %collective-permute-start.9) | collective-permute-done | bytes 4128 | tf_op jit(solution)/shard_map/ppermute | solution.py:381
  93.9 3.6 %collective-permute-start.10 = (f32[8,128]{1,0:T(8,128)S(1)}, f32[8,128]{1,0:T(8,128)S(1)}, u32[]{:S(2)}, u32[]{:S(2)}) collective-permute-start(f32[8,128]{1,0:T(8,128)S(1)} %log_add_fusion.6.one_ref), channel_id=1, source_target_pairs={{0,3},{1,2},{2,1},{3,0},{4,7},{5,6},{6,5},{7,4},{8,11},{9,10},{10,... | collective-permute-start | bytes 12296 | tf_op jit(solution)/shard_map/ppermute | solution.py:381
  97.4 0.1 prepare.3
  97.6 1.2 collective-permute-done.10.two_ref
  98.7 2.1 %far_col_lse.5 = (f32[1,2048]{1,0:T(1,128)S(1)}, f32[8,128]{1,0:T(8,128)}, bf16[1024,128]{1,0:T(8,128)(2,1)S(1)}) custom-call(bf16[1024,128]{1,0:T(8,128)(2,1)S(1)} %get-tuple-element.36.a_ref, f32[8,128]{1,0:T(8,128)S(1)} %get-tuple-element.37.r_ref, f32[8,128]{1,0:T(8,128)S(1)} %bitcast.22, f32[8,128]{1,0:T(8,128)S(1)} %log_add_fusion.6.one_ref, ...), custom_call_target="tpu_custom_call" | custom-call | flops 536870912 | bytes 2000000 | tf_op jit(solution)/shard_map/far_col_lse/pallas_call | solution.py:365
  100.8 2.3 %collective-permute-start.11 = (f32[1,2048]{1,0:T(1,128)S(1)}, f32[1,2048]{1,0:T(1,128)S(1)}, u32[]{:S(2)}, u32[]{:S(2)}) collective-permute-start(f32[1,2048]{1,0:T(1,128)S(1)} %get-tuple-element.64), channel_id=1, source_target_pairs={{0,4},{4,0},{8,12},{12,8},{16,20},{20,16},{24,28},{28,24},{32,36},... | collective-permute-start | bytes 24584 | tf_op jit(solution)/shard_map/ppermute | solution.py:381
  103.2 1.6 %near_col_lse.5 = f32[1,2048]{1,0:T(1,128)S(1)} custom-call(bf16[1024,128]{1,0:T(8,128)(2,1)S(1)} %get-tuple-element.62.left_ref, bf16[128,2048]{1,0:T(8,128)(2,1)S(1)} %get-tuple-element.38.near_b_ref.b_ref, f32[1,2048]{1,0:T(1,128)S(1)} %get-tuple-element.39.near_c_ref.c_ref, bf16[128,2048]{1,0:T(8,128)(2,1)S(1)} %get-tuple-element.63.ready_ref, ...), custom_call_target="tpu_custom_call" | custom-call | flops 536870912 | bytes 2000000 | tf_op jit(solution)/shard_map/near_col_lse/pallas_call | solution.py:365
  104.8 12.1 %all_to_all.23 = f32[32,16,128]{2,1,0:T(8,128)S(1)} all-to-all(f32[32,16,128]{2,1,0:T(8,128)S(1)} %broadcast_in_dim.22), channel_id=1, replica_groups={{0,8,16,24,32,40,48,56,64,72,80,88,96,104,112,120,128,136,144,152,160,1..., dimensions={0} | all-to-all | bytes 524288 | tf_op jit(solution)/shard_map/all_to_all | solution.py:393
  116.9 0.1 exponential_reduce_fusion
  117.0 1.5 %collective-permute-start.12 = (f32[1,2048]{1,0:T(1,128)S(1)}, f32[1,2048]{1,0:T(1,128)S(1)}, u32[]{:S(2)}, u32[]{:S(2)}) collective-permute-start(f32[1,2048]{1,0:T(1,128)S(1)} %bitcast.16), channel_id=1, source_target_pairs={{0,4},{4,0},{8,12},{12,8},{16,20},{20,16},{24,28},{28,24},{32,36},... | collective-permute-start | bytes 24584 | tf_op jit(solution)/shard_map/ppermute | solution.py:381
  118.5 1.5 %near_plan.1 = (f32[512,128]{1,0:T(8,128)S(1)}, f32[512,64]{1,0:T(8,128)S(1)}) custom-call(bf16[1024,128]{1,0:T(8,128)(2,1)S(1)} %get-tuple-element.62.left_ref, bf16[128,2048]{1,0:T(8,128)(2,1)S(1)} %get-tuple-element.38.near_b_ref.b_ref, f32[1,2048]{1,0:T(1,128)S(1)} %get-tuple-element.39.near_c_ref.c_ref, ...), custom_call_target="tpu_custom_call" | custom-call | flops 536870912 | bytes 2000000 | tf_op jit(solution)/shard_map/near_plan/pallas_call | solution.py:365
  120.0 1.7 %first_plan.1 = bf16[64,512]{1,0:T(8,128)(2,1)S(1)} custom-call(bf16[64,1024]{1,0:T(8,128)(2,1)S(1)} %copy-done, bf16[1024,128]{1,0:T(8,128)(2,1)S(1)} %get-tuple-element.62.left_ref, bf16[128,2048]{1,0:T(8,128)(2,1)S(1)} %get-tuple-element.45.far_b_ref.b_ref, f32[1,2048]{1,0:T(1,128)S(1)} %get-tuple-element.46.far_c_ref.c_ref, ...), custom_call_target="tpu_custom_call" | custom-call | flops 536870912 | bytes 2000000 | tf_op jit(solution)/shard_map/first_plan/pallas_call | solution.py:365
  121.8 1.3 collective-permute-start.13
  123.0 3.2 %last_plan.1 = (bf16[64,512]{1,0:T(8,128)(2,1)S(1)}, f32[1,64]{1,0:T(1,128)}) custom-call(bf16[64,1024]{1,0:T(8,128)(2,1)S(1)} %copy-done, bf16[1024,128]{1,0:T(8,128)(2,1)S(1)} %get-tuple-element.62.left_ref, bf16[128,2048]{1,0:T(8,128)(2,1)S(1)} %get-tuple-element.38.near_b_ref.b_ref, f32[1,2048]{1,0:T(1,128)S(1)} %get-tuple-element.39.near_c_ref.c_ref, ...), custom_call_target="tpu_custom_call" | custom-call | flops 1073741824 | bytes 2000000 | tf_op jit(solution)/shard_map/last_plan/pallas_call | solution.py:365
  126.2 1.3 collective-permute-start.14
  127.5 0.6 collective-permute-done.13
  128.1 2.7 %collective-permute-start.15 = (bf16[64,512]{1,0:T(8,128)(2,1)S(1)}, bf16[64,512]{1,0:T(8,128)(2,1)S(1)}, u32[]{:S(2)}, u32[]{:S(2)}) collective-permute-start(bf16[64,512]{1,0:T(8,128)(2,1)S(1)} %reduce-precision_convert_fusion.1), channel_id=1, source_target_pairs={{0,3},{1,2},{2,1},{3,0},{4,7},{5,6},{6,5},{7,4},{8,11},{9,10},{10,... | collective-permute-start | bytes 196616 | tf_op jit(solution)/shard_map/ppermute | solution.py:381
  130.9 1.7 %collective-permute-done.14 = bf16[64,512]{1,0:T(8,128)(2,1)S(1)} collective-permute-done((bf16[64,512]{1,0:T(8,128)(2,1)S(1)}, bf16[64,512]{1,0:T(8,128)(2,1)S(1)}, u32[]{:S(2)}, u32[]{:S(2)}) %collective-permute-start.14) | collective-permute-done | bytes 65568 | tf_op jit(solution)/shard_map/ppermute | solution.py:381
  132.6 1.5 %collective-permute-start.16 = (bf16[64,512]{1,0:T(8,128)(2,1)S(1)}, bf16[64,512]{1,0:T(8,128)(2,1)S(1)}, u32[]{:S(2)}, u32[]{:S(2)}) collective-permute-start(bf16[64,512]{1,0:T(8,128)(2,1)S(1)} %reduce-precision_convert_fusion), channel_id=1, source_target_pairs={{0,3},{1,2},{2,1},{3,0},{4,7},{5,6},{6,5},{7,4},{8,11},{9,10},{10,... | collective-permute-start | bytes 196616 | tf_op jit(solution)/shard_map/ppermute | solution.py:381
  134.1 4.0 %collective-permute-done.16 = bf16[64,512]{1,0:T(8,128)(2,1)S(1)} collective-permute-done((bf16[64,512]{1,0:T(8,128)(2,1)S(1)}, bf16[64,512]{1,0:T(8,128)(2,1)S(1)}, u32[]{:S(2)}, u32[]{:S(2)}) %collective-permute-start.16) | collective-permute-done | bytes 65568 | tf_op jit(solution)/shard_map/ppermute | solution.py:381
  138.0 0.7 convert_add_fusion
  (26 shorter events, 0.5 us)
Async XLA Ops:
  1.3 0.7 copy-start.3
  1.3 0.7 copy-start.4
  2.2 20.3 %copy-start = (bf16[64,1024]{1,0:T(8,128)(2,1)S(1)}, bf16[64,1024]{1,0:T(8,128)(2,1)}, u32[]{:S(2)}) copy-start(bf16[64,1024]{1,0:T(8,128)(2,1)} %emb_ref.5) | copy-start | bytes 393220
  2.2 20.3 %copy-start.1 = (f32[2,1024]{1,0:T(2,128)S(1)}, f32[2,1024]{1,0:T(2,128)}, u32[]{:S(2)}) copy-start(f32[2,1024]{1,0:T(2,128)} %pos_ref.1) | copy-start | bytes 24580
  20.5 4.3 %collective-permute-start = (bf16[32,34,128]{2,1,0:T(8,128)(2,1)S(1)}, bf16[32,34,128]{2,1,0:T(8,128)(2,1)S(1)}, u32[]{:S(2)}, u32[]{:S(2)}) collective-permute-start(bf16[32,34,128]{2,1,0:T(8,128)(2,1)S(1)} %all_to_all.20.pack_ref), channel_id=1, source_target_pairs={{0,4},{4,0},{8,12},{12,8},{16,20},{20,16},{24,28},{28,24},{32,36},... | collective-permute-start | bytes 835592 | tf_op jit(solution)/shard_map/ppermute | solution.py:381
  26.6 4.1 %collective-permute-start.1 = (f32[8,128]{1,0:T(8,128)S(1)}, f32[8,128]{1,0:T(8,128)S(1)}, u32[]{:S(2)}, u32[]{:S(2)}) collective-permute-start(f32[8,128]{1,0:T(8,128)S(1)} %get-tuple-element.44.lse_ref.guess_ref), channel_id=1, source_target_pairs={{0,1},{1,0},{2,3},{3,2},{4,5},{5,4},{6,7},{7,6},{8,9},{9,8},{10,11... | collective-permute-start | bytes 12296 | tf_op jit(solution)/shard_map/ppermute | solution.py:381
  30.7 4.6 %copy-start.2 = (f32[1024]{0:T(1024)S(1)}, f32[1024]{0:T(1024)}, u32[]{:S(2)}) copy-start(f32[1024]{0:T(1024)} %param.8) | copy-start | bytes 12292
  30.7 6.7 %collective-permute-start.2 = (f32[8,128]{1,0:T(8,128)S(1)}, f32[8,128]{1,0:T(8,128)S(1)}, u32[]{:S(2)}, u32[]{:S(2)}) collective-permute-start(f32[8,128]{1,0:T(8,128)S(1)} %log_add_fusion.8.one_ref), channel_id=1, source_target_pairs={{0,3},{1,2},{2,1},{3,0},{4,7},{5,6},{6,5},{7,4},{8,11},{9,10},{10,... | collective-permute-start | bytes 12296 | tf_op jit(solution)/shard_map/ppermute | solution.py:381
  39.5 3.0 %collective-permute-start.3 = (f32[1,2048]{1,0:T(1,128)S(1)}, f32[1,2048]{1,0:T(1,128)S(1)}, u32[]{:S(2)}, u32[]{:S(2)}) collective-permute-start(f32[1,2048]{1,0:T(1,128)S(1)} %get-tuple-element.52.far_guess_ref.guess_ref), channel_id=1, source_target_pairs={{0,4},{4,0},{8,12},{12,8},{16,20},{20,16},{24,28},{28,24},{32,36},... | collective-permute-start | bytes 24584 | tf_op jit(solution)/shard_map/ppermute | solution.py:381
  54.7 3.2 %collective-permute-start.4 = (f32[1,2048]{1,0:T(1,128)S(1)}, f32[1,2048]{1,0:T(1,128)S(1)}, u32[]{:S(2)}, u32[]{:S(2)}) collective-permute-start(f32[1,2048]{1,0:T(1,128)S(1)} %bitcast.10), channel_id=1, source_target_pairs={{0,4},{4,0},{8,12},{12,8},{16,20},{20,16},{24,28},{28,24},{32,36},... | collective-permute-start | bytes 24584 | tf_op jit(solution)/shard_map/ppermute | solution.py:381
  59.5 3.5 %collective-permute-start.5 = (f32[8,128]{1,0:T(8,128)S(1)}, f32[8,128]{1,0:T(8,128)S(1)}, u32[]{:S(2)}, u32[]{:S(2)}) collective-permute-start(f32[8,128]{1,0:T(8,128)S(1)} %row_lse.2.lse_ref.guess_ref), channel_id=1, source_target_pairs={{0,1},{1,0},{2,3},{3,2},{4,5},{5,4},{6,7},{7,6},{8,9},{9,8},{10,11... | collective-permute-start | bytes 12296 | tf_op jit(solution)/shard_map/ppermute | solution.py:381
  62.9 4.7 %collective-permute-start.6 = (f32[8,128]{1,0:T(8,128)S(1)}, f32[8,128]{1,0:T(8,128)S(1)}, u32[]{:S(2)}, u32[]{:S(2)}) collective-permute-start(f32[8,128]{1,0:T(8,128)S(1)} %log_add_fusion.7.one_ref), channel_id=1, source_target_pairs={{0,3},{1,2},{2,1},{3,0},{4,7},{5,6},{6,5},{7,4},{8,11},{9,10},{10,... | collective-permute-start | bytes 12296 | tf_op jit(solution)/shard_map/ppermute | solution.py:381
  69.7 3.9 %collective-permute-start.7 = (f32[1,2048]{1,0:T(1,128)S(1)}, f32[1,2048]{1,0:T(1,128)S(1)}, u32[]{:S(2)}, u32[]{:S(2)}) collective-permute-start(f32[1,2048]{1,0:T(1,128)S(1)} %get-tuple-element.58.far_guess_ref.guess_ref), channel_id=1, source_target_pairs={{0,4},{4,0},{8,12},{12,8},{16,20},{20,16},{24,28},{28,24},{32,36},... | collective-permute-start | bytes 24584 | tf_op jit(solution)/shard_map/ppermute | solution.py:381
  85.9 3.0 %collective-permute-start.8 = (f32[1,2048]{1,0:T(1,128)S(1)}, f32[1,2048]{1,0:T(1,128)S(1)}, u32[]{:S(2)}, u32[]{:S(2)}) collective-permute-start(f32[1,2048]{1,0:T(1,128)S(1)} %bitcast.13), channel_id=1, source_target_pairs={{0,4},{4,0},{8,12},{12,8},{16,20},{20,16},{24,28},{28,24},{32,36},... | collective-permute-start | bytes 24584 | tf_op jit(solution)/shard_map/ppermute | solution.py:381
  90.4 3.5 %collective-permute-start.9 = (f32[8,128]{1,0:T(8,128)S(1)}, f32[8,128]{1,0:T(8,128)S(1)}, u32[]{:S(2)}, u32[]{:S(2)}) collective-permute-start(f32[8,128]{1,0:T(8,128)S(1)} %row_lse.3.lse_ref), channel_id=1, source_target_pairs={{0,1},{1,0},{2,3},{3,2},{4,5},{5,4},{6,7},{7,6},{8,9},{9,8},{10,11... | collective-permute-start | bytes 12296 | tf_op jit(solution)/shard_map/ppermute | solution.py:381
  93.9 4.9 %collective-permute-start.10 = (f32[8,128]{1,0:T(8,128)S(1)}, f32[8,128]{1,0:T(8,128)S(1)}, u32[]{:S(2)}, u32[]{:S(2)}) collective-permute-start(f32[8,128]{1,0:T(8,128)S(1)} %log_add_fusion.6.one_ref), channel_id=1, source_target_pairs={{0,3},{1,2},{2,1},{3,0},{4,7},{5,6},{6,5},{7,4},{8,11},{9,10},{10,... | collective-permute-start | bytes 12296 | tf_op jit(solution)/shard_map/ppermute | solution.py:381
  100.8 3.9 %collective-permute-start.11 = (f32[1,2048]{1,0:T(1,128)S(1)}, f32[1,2048]{1,0:T(1,128)S(1)}, u32[]{:S(2)}, u32[]{:S(2)}) collective-permute-start(f32[1,2048]{1,0:T(1,128)S(1)} %get-tuple-element.64), channel_id=1, source_target_pairs={{0,4},{4,0},{8,12},{12,8},{16,20},{20,16},{24,28},{28,24},{32,36},... | collective-permute-start | bytes 24584 | tf_op jit(solution)/shard_map/ppermute | solution.py:381
  117.0 3.0 %collective-permute-start.12 = (f32[1,2048]{1,0:T(1,128)S(1)}, f32[1,2048]{1,0:T(1,128)S(1)}, u32[]{:S(2)}, u32[]{:S(2)}) collective-permute-start(f32[1,2048]{1,0:T(1,128)S(1)} %bitcast.16), channel_id=1, source_target_pairs={{0,4},{4,0},{8,12},{12,8},{16,20},{20,16},{24,28},{28,24},{32,36},... | collective-permute-start | bytes 24584 | tf_op jit(solution)/shard_map/ppermute | solution.py:381
  121.8 6.4 %collective-permute-start.13 = (bf16[64,512]{1,0:T(8,128)(2,1)S(1)}, bf16[64,512]{1,0:T(8,128)(2,1)S(1)}, u32[]{:S(2)}, u32[]{:S(2)}) collective-permute-start(bf16[64,512]{1,0:T(8,128)(2,1)S(1)} %first_plan.1), channel_id=1, source_target_pairs={{0,1},{1,0},{2,3},{3,2},{4,5},{5,4},{6,7},{7,6},{8,9},{9,8},{10,11... | collective-permute-start | bytes 196616 | tf_op jit(solution)/shard_map/ppermute | solution.py:381
  126.2 6.4 %collective-permute-start.14 = (bf16[64,512]{1,0:T(8,128)(2,1)S(1)}, bf16[64,512]{1,0:T(8,128)(2,1)S(1)}, u32[]{:S(2)}, u32[]{:S(2)}) collective-permute-start(bf16[64,512]{1,0:T(8,128)(2,1)S(1)} %get-tuple-element.68), channel_id=1, source_target_pairs={{0,1},{1,0},{2,3},{3,2},{4,5},{5,4},{6,7},{7,6},{8,9},{9,8},{10,11... | collective-permute-start | bytes 196616 | tf_op jit(solution)/shard_map/ppermute | solution.py:381
  128.1 5.9 %collective-permute-start.15 = (bf16[64,512]{1,0:T(8,128)(2,1)S(1)}, bf16[64,512]{1,0:T(8,128)(2,1)S(1)}, u32[]{:S(2)}, u32[]{:S(2)}) collective-permute-start(bf16[64,512]{1,0:T(8,128)(2,1)S(1)} %reduce-precision_convert_fusion.1), channel_id=1, source_target_pairs={{0,3},{1,2},{2,1},{3,0},{4,7},{5,6},{6,5},{7,4},{8,11},{9,10},{10,... | collective-permute-start | bytes 196616 | tf_op jit(solution)/shard_map/ppermute | solution.py:381
  132.6 5.4 %collective-permute-start.16 = (bf16[64,512]{1,0:T(8,128)(2,1)S(1)}, bf16[64,512]{1,0:T(8,128)(2,1)S(1)}, u32[]{:S(2)}, u32[]{:S(2)}) collective-permute-start(bf16[64,512]{1,0:T(8,128)(2,1)S(1)} %reduce-precision_convert_fusion), channel_id=1, source_target_pairs={{0,3},{1,2},{2,1},{3,0},{4,7},{5,6},{6,5},{7,4},{8,11},{9,10},{10,... | collective-permute-start | bytes 196616 | tf_op jit(solution)/shard_map/ppermute | solution.py:381

commit v8 on v7

--- a/solution.py
+++ b/solution.py
@@ -322,7 +322,7 @@
 def first_plan_kernel(emb_ref, left_ref, b_ref, c_ref, w_ref, lse_ref, mass_ref, pull_ref, out_ref, b_s, mass_s, pull_s):
     mass_s[...] = mass_ref[...]
     pull_s[...] = pull_ref[...]
-    plan_pass(left_ref.at[0 : out_ref.shape[1], :], b_ref, c_ref, w_ref, lse_ref, b_s, mass_s, pull_s, 2 * PLAN)
+    plan_pass(left_ref.at[0 : out_ref.shape[1], :], b_ref, c_ref, w_ref, lse_ref, b_s, mass_s, pull_s, 4 * PLAN)
     plan_finish(emb_ref, 0, mass_s, pull_s, out_ref)
 
 

time: 139 us -> 139 us (level)
  no operation moved by 1% of the time
where the time goes in v8:
time: 139 us; the launch traced here: 138 us
  blocking collectives  54.6 us (39%)
  starting transfers between devices  36.6 us (26%)
  Pallas kernels  29.5 us (21%)
  waiting for transfers between devices  14 us (10%)
  local copies, waits for them, and re-layouts  1.51 us (1%)
    all_to_all x4, blocking collectives, spread(): lax.all_to_all(block, 'src', 0, 0, axis_index_groups=groups, tiled=True)  54.6 us
    ppermute x17, starting transfers between devices, swapped(): lax.ppermute(value, axis, [(k, k ^ mask) for k in range(lax.axis_size(axi...  36.6 us
    pallas_call x18, Pallas kernels, call(): pl.pallas_call(kernel, out_shape=out_shape, scratch_shapes=[pltpu.VMEM(li...  29.5 us
    ppermute x17, waiting for transfers between devices, swapped(): lax.ppermute(value, axis, [(k, k ^ mask) for k in range(lax.axis_size(axi...  14 us
  transfers between devices with their start and end apart: 17, of which 8 were waited for; matrix products, arithmetic and copies ran while one was open for 0% of the time, Pallas kernels for 12%

profile of v8, /device:TPU:1, one launch (start us, length us, event | category | flops | bytes accessed | tf_op | source)
XLA Modules:
  0.0 138.4 jit_solution(6343921574030504151)
XLA Ops:
  0.6 0.7 fusion.6
  1.4 0.7 copy-done.3
  2.0 0.0 copy-done.4
  2.0 0.1 maximum_maximum_fusion
  2.2 0.0 copy-start
  2.2 0.0 copy-start.1
  2.2 18.4 %all_to_all.20.pack_ref = bf16[32,34,128]{2,1,0:T(8,128)(2,1)S(1)} all-to-all(bf16[32,34,128]{2,1,0:T(8,128)(2,1)S(1)} %broadcast_in_dim.19), channel_id=1, replica_groups={{0,8,16,24,32,40,48,56,64,72,80,88,96,104,112,120,128,136,144,152,160,1..., dimensions={0} | all-to-all | bytes 557056 | tf_op jit(solution)/shard_map/all_to_all | solution.py:393
  20.5 2.0 %collective-permute-start = (bf16[32,34,128]{2,1,0:T(8,128)(2,1)S(1)}, bf16[32,34,128]{2,1,0:T(8,128)(2,1)S(1)}, u32[]{:S(2)}, u32[]{:S(2)}) collective-permute-start(bf16[32,34,128]{2,1,0:T(8,128)(2,1)S(1)} %all_to_all.20.pack_ref), channel_id=1, source_target_pairs={{0,4},{4,0},{8,12},{12,8},{16,20},{20,16},{24,28},{28,24},{32,36},... | collective-permute-start | bytes 835592 | tf_op jit(solution)/shard_map/ppermute | solution.py:381
  22.5 2.3 %static_parts.1 = (bf16[1024,128]{1,0:T(8,128)(2,1)S(1)}, f32[8,128]{1,0:T(8,128)S(1)}, bf16[128,2048]{1,0:T(8,128)(2,1)S(1)}, f32[1,2048]{1,0:T(1,128)S(1)}, f3...) custom-call(bf16[64,1024]{1,0:T(8,128)(2,1)S(1)} %copy-done, ...), custom_call_target="tpu_custom_call" | custom-call | flops 536870912 | bytes 2000000 | tf_op jit(solution)/shard_map/static_parts/pallas_call | solution.py:365
  24.8 0.0 collective-permute-done.pack_ref
  24.8 1.8 %first_row_lse.1 = (f32[8,128]{1,0:T(8,128)S(1)}, bf16[128,2048]{1,0:T(8,128)(2,1)S(1)}, f32[1,2048]{1,0:T(1,128)S(1)}, f32[1,2048]{1,0:T(1,128)S(1)}) custom-call(bf16[1024,128]{1,0:T(8,128)(2,1)S(1)} %get-tuple-element.36.a_ref, f32[8,128]{1,0:T(8,128)S(1)} %get-tuple-element.37.r_ref, bf16[128,2048]{1,0:T(8,128)(2,1)S(1)} %get-tuple-element.38.near_b_ref.b_ref, ...), custom_call_target="tpu_custom_call" | custom-call | flops 536870912 | bytes 2000000 | tf_op jit(solution)/shard_map/first_row_lse/pallas_call | solution.py:365
  26.6 3.1 %collective-permute-start.1 = (f32[8,128]{1,0:T(8,128)S(1)}, f32[8,128]{1,0:T(8,128)S(1)}, u32[]{:S(2)}, u32[]{:S(2)}) collective-permute-start(f32[8,128]{1,0:T(8,128)S(1)} %get-tuple-element.44.lse_ref.guess_ref), channel_id=1, source_target_pairs={{0,1},{1,0},{2,3},{3,2},{4,5},{5,4},{6,7},{7,6},{8,9},{9,8},{10,11... | collective-permute-start | bytes 12296 | tf_op jit(solution)/shard_map/ppermute | solution.py:381
  29.7 1.0 collective-permute-done.1
  30.7 0.0 copy-start.2
  30.7 4.6 %collective-permute-start.2 = (f32[8,128]{1,0:T(8,128)S(1)}, f32[8,128]{1,0:T(8,128)S(1)}, u32[]{:S(2)}, u32[]{:S(2)}) collective-permute-start(f32[8,128]{1,0:T(8,128)S(1)} %log_add_fusion.8.one_ref), channel_id=1, source_target_pairs={{0,3},{1,2},{2,1},{3,0},{4,7},{5,6},{6,5},{7,4},{8,11},{9,10},{10,... | collective-permute-start | bytes 12296 | tf_op jit(solution)/shard_map/ppermute | solution.py:381
  35.3 2.1 %col_guess.1 = (bf16[128,2048]{1,0:T(8,128)(2,1)S(1)}, bf16[128,2048]{1,0:T(8,128)(2,1)S(1)}, bf16[1024,128]{1,0:T(8,128)(2,1)S(1)}, f32[1,2048]{1,0:T(1,128)S(1)}, f32[1,2048]{1,0:T(1,128)S(1)}) custom-call(bf16[1024,128]{1,0:T(8,128)(2,1)S(1)} %get-tuple-element.36.a_ref, f32[8,128]{1,0:T(8,128)S(1)} %get-tuple-element.37.r_ref, ...), custom_call_target="tpu_custom_call" | custom-call | flops 1073741824 | bytes 2000000 | tf_op jit(solution)/shard_map/col_guess/pallas_call | solution.py:365
  37.4 2.1 %far_col_lse.3 = (f32[1,2048]{1,0:T(1,128)S(1)}, f32[8,128]{1,0:T(8,128)}, bf16[1024,128]{1,0:T(8,128)(2,1)S(1)}) custom-call(bf16[1024,128]{1,0:T(8,128)(2,1)S(1)} %get-tuple-element.36.a_ref, f32[8,128]{1,0:T(8,128)S(1)} %get-tuple-element.37.r_ref, f32[8,128]{1,0:T(8,128)S(1)} %bitcast.20, f32[8,128]{1,0:T(8,128)S(1)} %log_add_fusion.8.one_ref, ...), custom_call_target="tpu_custom_call" | custom-call | flops 536870912 | bytes 2000000 | tf_op jit(solution)/shard_map/far_col_lse/pallas_call | solution.py:365
  39.5 1.4 %collective-permute-start.3 = (f32[1,2048]{1,0:T(1,128)S(1)}, f32[1,2048]{1,0:T(1,128)S(1)}, u32[]{:S(2)}, u32[]{:S(2)}) collective-permute-start(f32[1,2048]{1,0:T(1,128)S(1)} %get-tuple-element.52.far_guess_ref.guess_ref), channel_id=1, source_target_pairs={{0,4},{4,0},{8,12},{12,8},{16,20},{20,16},{24,28},{28,24},{32,36},... | collective-permute-start | bytes 24584 | tf_op jit(solution)/shard_map/ppermute | solution.py:381
  40.9 1.6 %near_col_lse.3.near_guess_ref.guess_ref = f32[1,2048]{1,0:T(1,128)S(1)} custom-call(bf16[1024,128]{1,0:T(8,128)(2,1)S(1)} %get-tuple-element.49.left_ref, bf16[128,2048]{1,0:T(8,128)(2,1)S(1)} %get-tuple-element.38.near_b_ref.b_ref, f32[1,2048]{1,0:T(1,128)S(1)} %get-tuple-element.39.near_c_ref.c_ref, bf16[128,2048]{1,0:T(8,128)(2,1)S(1)} %get-tuple-element.50.ready_ref, ...), custom_call_target="tpu_custom_call" | custom-call | flops 536870912 | bytes 2000000 | tf_op jit(solution)/shard_map/near_col_lse/pallas_call | solution.py:365
  42.6 12.0 %all_to_all.21 = f32[32,16,128]{2,1,0:T(8,128)S(1)} all-to-all(f32[32,16,128]{2,1,0:T(8,128)S(1)} %broadcast_in_dim.20), channel_id=1, replica_groups={{0,8,16,24,32,40,48,56,64,72,80,88,96,104,112,120,128,136,144,152,160,1..., dimensions={0} | all-to-all | bytes 524288 | tf_op jit(solution)/shard_map/all_to_all | solution.py:393
  54.7 0.1 exponential_reduce_fusion.2
  54.7 1.7 %collective-permute-start.4 = (f32[1,2048]{1,0:T(1,128)S(1)}, f32[1,2048]{1,0:T(1,128)S(1)}, u32[]{:S(2)}, u32[]{:S(2)}) collective-permute-start(f32[1,2048]{1,0:T(1,128)S(1)} %bitcast.10), channel_id=1, source_target_pairs={{0,4},{4,0},{8,12},{12,8},{16,20},{20,16},{24,28},{28,24},{32,36},... | collective-permute-start | bytes 24584 | tf_op jit(solution)/shard_map/ppermute | solution.py:381
  56.4 1.5 %near_row_lse.2.acc_ref = f32[1024,128]{1,0:T(8,128)S(1)} custom-call(bf16[128,2048]{1,0:T(8,128)(2,1)S(1)} %get-tuple-element.38.near_b_ref.b_ref, f32[1,2048]{1,0:T(1,128)S(1)} %get-tuple-element.39.near_c_ref.c_ref, f32[1,2048]{1,0:T(1,128)S(1)} %get-tuple-element.40.near_w_ref.w_ref, f32[1,2048]{1,0:T(1,128)S(1)} %bitcast.11, ...), custom_call_target="tpu_custom_call" | custom-call | flops 536870912 | bytes 2000000 | tf_op jit(solution)/shard_map/near_row_lse/pallas_call | solution.py:365
  57.9 0.0 collective-permute-done.4.lse_ref
  58.0 1.5 %row_lse.2.lse_ref.guess_ref = f32[8,128]{1,0:T(8,128)S(1)} custom-call(bf16[1024,128]{1,0:T(8,128)(2,1)S(1)} %get-tuple-element.36.a_ref, f32[8,128]{1,0:T(8,128)S(1)} %get-tuple-element.37.r_ref, bf16[128,2048]{1,0:T(8,128)(2,1)S(1)} %get-tuple-element.38.near_b_ref.b_ref, f32[1,2048]{1,0:T(1,128)S(1)} %get-tuple-element.39.near_c_ref.c_ref, ...), custom_call_target="tpu_custom_call" | custom-call | flops 536870912 | bytes 2000000 | tf_op jit(solution)/shard_map/row_lse/pallas_call | solution.py:365
  59.5 1.3 collective-permute-start.5
  60.7 2.2 %collective-permute-done.5 = f32[8,128]{1,0:T(8,128)S(1)} collective-permute-done((f32[8,128]{1,0:T(8,128)S(1)}, f32[8,128]{1,0:T(8,128)S(1)}, u32[]{:S(2)}, u32[]{:S(2)}) %collective-permute-start.5) | collective-permute-done | bytes 4128 | tf_op jit(solution)/shard_map/ppermute | solution.py:381
  62.9 3.4 %collective-permute-start.6 = (f32[8,128]{1,0:T(8,128)S(1)}, f32[8,128]{1,0:T(8,128)S(1)}, u32[]{:S(2)}, u32[]{:S(2)}) collective-permute-start(f32[8,128]{1,0:T(8,128)S(1)} %log_add_fusion.7.one_ref), channel_id=1, source_target_pairs={{0,3},{1,2},{2,1},{3,0},{4,7},{5,6},{6,5},{7,4},{8,11},{9,10},{10,... | collective-permute-start | bytes 12296 | tf_op jit(solution)/shard_map/ppermute | solution.py:381
  66.3 0.2 prepare.2
  66.5 1.1 collective-permute-done.6.two_ref
  67.6 2.1 %far_col_lse.4 = (f32[1,2048]{1,0:T(1,128)S(1)}, f32[8,128]{1,0:T(8,128)}, bf16[1024,128]{1,0:T(8,128)(2,1)S(1)}) custom-call(bf16[1024,128]{1,0:T(8,128)(2,1)S(1)} %get-tuple-element.36.a_ref, f32[8,128]{1,0:T(8,128)S(1)} %get-tuple-element.37.r_ref, f32[8,128]{1,0:T(8,128)S(1)} %bitcast.21, f32[8,128]{1,0:T(8,128)S(1)} %log_add_fusion.7.one_ref, ...), custom_call_target="tpu_custom_call" | custom-call | flops 536870912 | bytes 2000000 | tf_op jit(solution)/shard_map/far_col_lse/pallas_call | solution.py:365
  69.7 2.3 %collective-permute-start.7 = (f32[1,2048]{1,0:T(1,128)S(1)}, f32[1,2048]{1,0:T(1,128)S(1)}, u32[]{:S(2)}, u32[]{:S(2)}) collective-permute-start(f32[1,2048]{1,0:T(1,128)S(1)} %get-tuple-element.58.far_guess_ref.guess_ref), channel_id=1, source_target_pairs={{0,4},{4,0},{8,12},{12,8},{16,20},{20,16},{24,28},{28,24},{32,36},... | collective-permute-start | bytes 24584 | tf_op jit(solution)/shard_map/ppermute | solution.py:381
  72.0 1.6 %near_col_lse.4.near_guess_ref.guess_ref = f32[1,2048]{1,0:T(1,128)S(1)} custom-call(bf16[1024,128]{1,0:T(8,128)(2,1)S(1)} %get-tuple-element.56.left_ref, bf16[128,2048]{1,0:T(8,128)(2,1)S(1)} %get-tuple-element.38.near_b_ref.b_ref, f32[1,2048]{1,0:T(1,128)S(1)} %get-tuple-element.39.near_c_ref.c_ref, bf16[128,2048]{1,0:T(8,128)(2,1)S(1)} %get-tuple-element.57.ready_ref, ...), custom_call_target="tpu_custom_call" | custom-call | flops 536870912 | bytes 2000000 | tf_op jit(solution)/shard_map/near_col_lse/pallas_call | solution.py:365
  73.7 12.1 %all_to_all.22 = f32[32,16,128]{2,1,0:T(8,128)S(1)} all-to-all(f32[32,16,128]{2,1,0:T(8,128)S(1)} %broadcast_in_dim.21), channel_id=1, replica_groups={{0,8,16,24,32,40,48,56,64,72,80,88,96,104,112,120,128,136,144,152,160,1..., dimensions={0} | all-to-all | bytes 524288 | tf_op jit(solution)/shard_map/all_to_all | solution.py:393
  85.8 0.1 exponential_reduce_fusion.1
  85.9 1.5 %collective-permute-start.8 = (f32[1,2048]{1,0:T(1,128)S(1)}, f32[1,2048]{1,0:T(1,128)S(1)}, u32[]{:S(2)}, u32[]{:S(2)}) collective-permute-start(f32[1,2048]{1,0:T(1,128)S(1)} %bitcast.13), channel_id=1, source_target_pairs={{0,4},{4,0},{8,12},{12,8},{16,20},{20,16},{24,28},{28,24},{32,36},... | collective-permute-start | bytes 24584 | tf_op jit(solution)/shard_map/ppermute | solution.py:381
  87.4 1.5 %near_row_lse.3.acc_ref = f32[1024,128]{1,0:T(8,128)S(1)} custom-call(bf16[128,2048]{1,0:T(8,128)(2,1)S(1)} %get-tuple-element.38.near_b_ref.b_ref, f32[1,2048]{1,0:T(1,128)S(1)} %get-tuple-element.39.near_c_ref.c_ref, f32[1,2048]{1,0:T(1,128)S(1)} %get-tuple-element.40.near_w_ref.w_ref, f32[1,2048]{1,0:T(1,128)S(1)} %bitcast.14, ...), custom_call_target="tpu_custom_call" | custom-call | flops 536870912 | bytes 2000000 | tf_op jit(solution)/shard_map/near_row_lse/pallas_call | solution.py:365
  88.9 0.0 collective-permute-done.8.lse_ref
  88.9 1.5 %row_lse.3.lse_ref = f32[8,128]{1,0:T(8,128)S(1)} custom-call(bf16[1024,128]{1,0:T(8,128)(2,1)S(1)} %get-tuple-element.36.a_ref, f32[8,128]{1,0:T(8,128)S(1)} %get-tuple-element.37.r_ref, bf16[128,2048]{1,0:T(8,128)(2,1)S(1)} %get-tuple-element.38.near_b_ref.b_ref, f32[1,2048]{1,0:T(1,128)S(1)} %get-tuple-element.39.near_c_ref.c_ref, ...), custom_call_target="tpu_custom_call" | custom-call | flops 536870912 | bytes 2000000 | tf_op jit(solution)/shard_map/row_lse/pallas_call | solution.py:365
  90.4 1.3 collective-permute-start.9
  91.7 2.2 %collective-permute-done.9 = f32[8,128]{1,0:T(8,128)S(1)} collective-permute-done((f32[8,128]{1,0:T(8,128)S(1)}, f32[8,128]{1,0:T(8,128)S(1)}, u32[]{:S(2)}, u32[]{:S(2)}) %collective-permute-start.9) | collective-permute-done | bytes 4128 | tf_op jit(solution)/shard_map/ppermute | solution.py:381
  93.9 3.6 %collective-permute-start.10 = (f32[8,128]{1,0:T(8,128)S(1)}, f32[8,128]{1,0:T(8,128)S(1)}, u32[]{:S(2)}, u32[]{:S(2)}) collective-permute-start(f32[8,128]{1,0:T(8,128)S(1)} %log_add_fusion.6.one_ref), channel_id=1, source_target_pairs={{0,3},{1,2},{2,1},{3,0},{4,7},{5,6},{6,5},{7,4},{8,11},{9,10},{10,... | collective-permute-start | bytes 12296 | tf_op jit(solution)/shard_map/ppermute | solution.py:381
  97.4 0.1 prepare.3
  97.6 1.2 collective-permute-done.10.two_ref
  98.7 2.1 %far_col_lse.5 = (f32[1,2048]{1,0:T(1,128)S(1)}, f32[8,128]{1,0:T(8,128)}, bf16[1024,128]{1,0:T(8,128)(2,1)S(1)}) custom-call(bf16[1024,128]{1,0:T(8,128)(2,1)S(1)} %get-tuple-element.36.a_ref, f32[8,128]{1,0:T(8,128)S(1)} %get-tuple-element.37.r_ref, f32[8,128]{1,0:T(8,128)S(1)} %bitcast.22, f32[8,128]{1,0:T(8,128)S(1)} %log_add_fusion.6.one_ref, ...), custom_call_target="tpu_custom_call" | custom-call | flops 536870912 | bytes 2000000 | tf_op jit(solution)/shard_map/far_col_lse/pallas_call | solution.py:365
  100.8 2.3 %collective-permute-start.11 = (f32[1,2048]{1,0:T(1,128)S(1)}, f32[1,2048]{1,0:T(1,128)S(1)}, u32[]{:S(2)}, u32[]{:S(2)}) collective-permute-start(f32[1,2048]{1,0:T(1,128)S(1)} %get-tuple-element.64), channel_id=1, source_target_pairs={{0,4},{4,0},{8,12},{12,8},{16,20},{20,16},{24,28},{28,24},{32,36},... | collective-permute-start | bytes 24584 | tf_op jit(solution)/shard_map/ppermute | solution.py:381
  103.2 1.6 %near_col_lse.5 = f32[1,2048]{1,0:T(1,128)S(1)} custom-call(bf16[1024,128]{1,0:T(8,128)(2,1)S(1)} %get-tuple-element.62.left_ref, bf16[128,2048]{1,0:T(8,128)(2,1)S(1)} %get-tuple-element.38.near_b_ref.b_ref, f32[1,2048]{1,0:T(1,128)S(1)} %get-tuple-element.39.near_c_ref.c_ref, bf16[128,2048]{1,0:T(8,128)(2,1)S(1)} %get-tuple-element.63.ready_ref, ...), custom_call_target="tpu_custom_call" | custom-call | flops 536870912 | bytes 2000000 | tf_op jit(solution)/shard_map/near_col_lse/pallas_call | solution.py:365
  104.7 0.0 collective-permute-done.11
  104.8 12.1 %all_to_all.23 = f32[32,16,128]{2,1,0:T(8,128)S(1)} all-to-all(f32[32,16,128]{2,1,0:T(8,128)S(1)} %broadcast_in_dim.22), channel_id=1, replica_groups={{0,8,16,24,32,40,48,56,64,72,80,88,96,104,112,120,128,136,144,152,160,1..., dimensions={0} | all-to-all | bytes 524288 | tf_op jit(solution)/shard_map/all_to_all | solution.py:393
  116.9 0.1 exponential_reduce_fusion
  117.0 1.5 %collective-permute-start.12 = (f32[1,2048]{1,0:T(1,128)S(1)}, f32[1,2048]{1,0:T(1,128)S(1)}, u32[]{:S(2)}, u32[]{:S(2)}) collective-permute-start(f32[1,2048]{1,0:T(1,128)S(1)} %bitcast.16), channel_id=1, source_target_pairs={{0,4},{4,0},{8,12},{12,8},{16,20},{20,16},{24,28},{28,24},{32,36},... | collective-permute-start | bytes 24584 | tf_op jit(solution)/shard_map/ppermute | solution.py:381
  118.5 1.5 %near_plan.1 = (f32[512,128]{1,0:T(8,128)S(1)}, f32[512,64]{1,0:T(8,128)S(1)}) custom-call(bf16[1024,128]{1,0:T(8,128)(2,1)S(1)} %get-tuple-element.62.left_ref, bf16[128,2048]{1,0:T(8,128)(2,1)S(1)} %get-tuple-element.38.near_b_ref.b_ref, f32[1,2048]{1,0:T(1,128)S(1)} %get-tuple-element.39.near_c_ref.c_ref, ...), custom_call_target="tpu_custom_call" | custom-call | flops 536870912 | bytes 2000000 | tf_op jit(solution)/shard_map/near_plan/pallas_call | solution.py:365
  120.0 0.0 collective-permute-done.12.lse_ref
  120.0 1.4 first_plan.1
  121.4 1.3 collective-permute-start.13
  122.7 3.2 %last_plan.1 = (bf16[64,512]{1,0:T(8,128)(2,1)S(1)}, f32[1,64]{1,0:T(1,128)}) custom-call(bf16[64,1024]{1,0:T(8,128)(2,1)S(1)} %copy-done, bf16[1024,128]{1,0:T(8,128)(2,1)S(1)} %get-tuple-element.62.left_ref, bf16[128,2048]{1,0:T(8,128)(2,1)S(1)} %get-tuple-element.38.near_b_ref.b_ref, f32[1,2048]{1,0:T(1,128)S(1)} %get-tuple-element.39.near_c_ref.c_ref, ...), custom_call_target="tpu_custom_call" | custom-call | flops 1073741824 | bytes 2000000 | tf_op jit(solution)/shard_map/last_plan/pallas_call | solution.py:365
  125.9 1.3 collective-permute-start.14
  127.1 0.6 collective-permute-done.13
  127.8 2.7 %collective-permute-start.15 = (bf16[64,512]{1,0:T(8,128)(2,1)S(1)}, bf16[64,512]{1,0:T(8,128)(2,1)S(1)}, u32[]{:S(2)}, u32[]{:S(2)}) collective-permute-start(bf16[64,512]{1,0:T(8,128)(2,1)S(1)} %reduce-precision_convert_fusion.1), channel_id=1, source_target_pairs={{0,3},{1,2},{2,1},{3,0},{4,7},{5,6},{6,5},{7,4},{8,11},{9,10},{10,... | collective-permute-start | bytes 196616 | tf_op jit(solution)/shard_map/ppermute | solution.py:381
  130.5 1.7 %collective-permute-done.14 = bf16[64,512]{1,0:T(8,128)(2,1)S(1)} collective-permute-done((bf16[64,512]{1,0:T(8,128)(2,1)S(1)}, bf16[64,512]{1,0:T(8,128)(2,1)S(1)}, u32[]{:S(2)}, u32[]{:S(2)}) %collective-permute-start.14) | collective-permute-done | bytes 65568 | tf_op jit(solution)/shard_map/ppermute | solution.py:381
  132.3 1.5 %collective-permute-start.16 = (bf16[64,512]{1,0:T(8,128)(2,1)S(1)}, bf16[64,512]{1,0:T(8,128)(2,1)S(1)}, u32[]{:S(2)}, u32[]{:S(2)}) collective-permute-start(bf16[64,512]{1,0:T(8,128)(2,1)S(1)} %reduce-precision_convert_fusion), channel_id=1, source_target_pairs={{0,3},{1,2},{2,1},{3,0},{4,7},{5,6},{6,5},{7,4},{8,11},{9,10},{10,... | collective-permute-start | bytes 196616 | tf_op jit(solution)/shard_map/ppermute | solution.py:381
  133.7 0.0 collective-permute-done.15
  133.7 4.0 %collective-permute-done.16 = bf16[64,512]{1,0:T(8,128)(2,1)S(1)} collective-permute-done((bf16[64,512]{1,0:T(8,128)(2,1)S(1)}, bf16[64,512]{1,0:T(8,128)(2,1)S(1)}, u32[]{:S(2)}, u32[]{:S(2)}) %collective-permute-start.16) | collective-permute-done | bytes 65568 | tf_op jit(solution)/shard_map/ppermute | solution.py:381
  137.7 0.7 convert_add_fusion
  (26 shorter events, 0.5 us)
Async XLA Ops:
  1.3 0.7 copy-start.3
  1.3 0.7 copy-start.4
  2.2 20.3 %copy-start = (bf16[64,1024]{1,0:T(8,128)(2,1)S(1)}, bf16[64,1024]{1,0:T(8,128)(2,1)}, u32[]{:S(2)}) copy-start(bf16[64,1024]{1,0:T(8,128)(2,1)} %emb_ref.5) | copy-start | bytes 393220
  2.2 20.3 %copy-start.1 = (f32[2,1024]{1,0:T(2,128)S(1)}, f32[2,1024]{1,0:T(2,128)}, u32[]{:S(2)}) copy-start(f32[2,1024]{1,0:T(2,128)} %pos_ref.1) | copy-start | bytes 24580
  20.5 4.3 %collective-permute-start = (bf16[32,34,128]{2,1,0:T(8,128)(2,1)S(1)}, bf16[32,34,128]{2,1,0:T(8,128)(2,1)S(1)}, u32[]{:S(2)}, u32[]{:S(2)}) collective-permute-start(bf16[32,34,128]{2,1,0:T(8,128)(2,1)S(1)} %all_to_all.20.pack_ref), channel_id=1, source_target_pairs={{0,4},{4,0},{8,12},{12,8},{16,20},{20,16},{24,28},{28,24},{32,36},... | collective-permute-start | bytes 835592 | tf_op jit(solution)/shard_map/ppermute | solution.py:381
  26.6 4.1 %collective-permute-start.1 = (f32[8,128]{1,0:T(8,128)S(1)}, f32[8,128]{1,0:T(8,128)S(1)}, u32[]{:S(2)}, u32[]{:S(2)}) collective-permute-start(f32[8,128]{1,0:T(8,128)S(1)} %get-tuple-element.44.lse_ref.guess_ref), channel_id=1, source_target_pairs={{0,1},{1,0},{2,3},{3,2},{4,5},{5,4},{6,7},{7,6},{8,9},{9,8},{10,11... | collective-permute-start | bytes 12296 | tf_op jit(solution)/shard_map/ppermute | solution.py:381
  30.7 4.6 %copy-start.2 = (f32[1024]{0:T(1024)S(1)}, f32[1024]{0:T(1024)}, u32[]{:S(2)}) copy-start(f32[1024]{0:T(1024)} %param.8) | copy-start | bytes 12292
  30.7 6.7 %collective-permute-start.2 = (f32[8,128]{1,0:T(8,128)S(1)}, f32[8,128]{1,0:T(8,128)S(1)}, u32[]{:S(2)}, u32[]{:S(2)}) collective-permute-start(f32[8,128]{1,0:T(8,128)S(1)} %log_add_fusion.8.one_ref), channel_id=1, source_target_pairs={{0,3},{1,2},{2,1},{3,0},{4,7},{5,6},{6,5},{7,4},{8,11},{9,10},{10,... | collective-permute-start | bytes 12296 | tf_op jit(solution)/shard_map/ppermute | solution.py:381
  39.5 3.0 %collective-permute-start.3 = (f32[1,2048]{1,0:T(1,128)S(1)}, f32[1,2048]{1,0:T(1,128)S(1)}, u32[]{:S(2)}, u32[]{:S(2)}) collective-permute-start(f32[1,2048]{1,0:T(1,128)S(1)} %get-tuple-element.52.far_guess_ref.guess_ref), channel_id=1, source_target_pairs={{0,4},{4,0},{8,12},{12,8},{16,20},{20,16},{24,28},{28,24},{32,36},... | collective-permute-start | bytes 24584 | tf_op jit(solution)/shard_map/ppermute | solution.py:381
  54.7 3.2 %collective-permute-start.4 = (f32[1,2048]{1,0:T(1,128)S(1)}, f32[1,2048]{1,0:T(1,128)S(1)}, u32[]{:S(2)}, u32[]{:S(2)}) collective-permute-start(f32[1,2048]{1,0:T(1,128)S(1)} %bitcast.10), channel_id=1, source_target_pairs={{0,4},{4,0},{8,12},{12,8},{16,20},{20,16},{24,28},{28,24},{32,36},... | collective-permute-start | bytes 24584 | tf_op jit(solution)/shard_map/ppermute | solution.py:381
  59.5 3.5 %collective-permute-start.5 = (f32[8,128]{1,0:T(8,128)S(1)}, f32[8,128]{1,0:T(8,128)S(1)}, u32[]{:S(2)}, u32[]{:S(2)}) collective-permute-start(f32[8,128]{1,0:T(8,128)S(1)} %row_lse.2.lse_ref.guess_ref), channel_id=1, source_target_pairs={{0,1},{1,0},{2,3},{3,2},{4,5},{5,4},{6,7},{7,6},{8,9},{9,8},{10,11... | collective-permute-start | bytes 12296 | tf_op jit(solution)/shard_map/ppermute | solution.py:381
  62.9 4.7 %collective-permute-start.6 = (f32[8,128]{1,0:T(8,128)S(1)}, f32[8,128]{1,0:T(8,128)S(1)}, u32[]{:S(2)}, u32[]{:S(2)}) collective-permute-start(f32[8,128]{1,0:T(8,128)S(1)} %log_add_fusion.7.one_ref), channel_id=1, source_target_pairs={{0,3},{1,2},{2,1},{3,0},{4,7},{5,6},{6,5},{7,4},{8,11},{9,10},{10,... | collective-permute-start | bytes 12296 | tf_op jit(solution)/shard_map/ppermute | solution.py:381
  69.7 3.9 %collective-permute-start.7 = (f32[1,2048]{1,0:T(1,128)S(1)}, f32[1,2048]{1,0:T(1,128)S(1)}, u32[]{:S(2)}, u32[]{:S(2)}) collective-permute-start(f32[1,2048]{1,0:T(1,128)S(1)} %get-tuple-element.58.far_guess_ref.guess_ref), channel_id=1, source_target_pairs={{0,4},{4,0},{8,12},{12,8},{16,20},{20,16},{24,28},{28,24},{32,36},... | collective-permute-start | bytes 24584 | tf_op jit(solution)/shard_map/ppermute | solution.py:381
  85.9 3.0 %collective-permute-start.8 = (f32[1,2048]{1,0:T(1,128)S(1)}, f32[1,2048]{1,0:T(1,128)S(1)}, u32[]{:S(2)}, u32[]{:S(2)}) collective-permute-start(f32[1,2048]{1,0:T(1,128)S(1)} %bitcast.13), channel_id=1, source_target_pairs={{0,4},{4,0},{8,12},{12,8},{16,20},{20,16},{24,28},{28,24},{32,36},... | collective-permute-start | bytes 24584 | tf_op jit(solution)/shard_map/ppermute | solution.py:381
  90.4 3.5 %collective-permute-start.9 = (f32[8,128]{1,0:T(8,128)S(1)}, f32[8,128]{1,0:T(8,128)S(1)}, u32[]{:S(2)}, u32[]{:S(2)}) collective-permute-start(f32[8,128]{1,0:T(8,128)S(1)} %row_lse.3.lse_ref), channel_id=1, source_target_pairs={{0,1},{1,0},{2,3},{3,2},{4,5},{5,4},{6,7},{7,6},{8,9},{9,8},{10,11... | collective-permute-start | bytes 12296 | tf_op jit(solution)/shard_map/ppermute | solution.py:381
  93.9 4.9 %collective-permute-start.10 = (f32[8,128]{1,0:T(8,128)S(1)}, f32[8,128]{1,0:T(8,128)S(1)}, u32[]{:S(2)}, u32[]{:S(2)}) collective-permute-start(f32[8,128]{1,0:T(8,128)S(1)} %log_add_fusion.6.one_ref), channel_id=1, source_target_pairs={{0,3},{1,2},{2,1},{3,0},{4,7},{5,6},{6,5},{7,4},{8,11},{9,10},{10,... | collective-permute-start | bytes 12296 | tf_op jit(solution)/shard_map/ppermute | solution.py:381
  100.8 3.9 %collective-permute-start.11 = (f32[1,2048]{1,0:T(1,128)S(1)}, f32[1,2048]{1,0:T(1,128)S(1)}, u32[]{:S(2)}, u32[]{:S(2)}) collective-permute-start(f32[1,2048]{1,0:T(1,128)S(1)} %get-tuple-element.64), channel_id=1, source_target_pairs={{0,4},{4,0},{8,12},{12,8},{16,20},{20,16},{24,28},{28,24},{32,36},... | collective-permute-start | bytes 24584 | tf_op jit(solution)/shard_map/ppermute | solution.py:381
  117.0 3.0 %collective-permute-start.12 = (f32[1,2048]{1,0:T(1,128)S(1)}, f32[1,2048]{1,0:T(1,128)S(1)}, u32[]{:S(2)}, u32[]{:S(2)}) collective-permute-start(f32[1,2048]{1,0:T(1,128)S(1)} %bitcast.16), channel_id=1, source_target_pairs={{0,4},{4,0},{8,12},{12,8},{16,20},{20,16},{24,28},{28,24},{32,36},... | collective-permute-start | bytes 24584 | tf_op jit(solution)/shard_map/ppermute | solution.py:381
  121.4 6.4 %collective-permute-start.13 = (bf16[64,512]{1,0:T(8,128)(2,1)S(1)}, bf16[64,512]{1,0:T(8,128)(2,1)S(1)}, u32[]{:S(2)}, u32[]{:S(2)}) collective-permute-start(bf16[64,512]{1,0:T(8,128)(2,1)S(1)} %first_plan.1), channel_id=1, source_target_pairs={{0,1},{1,0},{2,3},{3,2},{4,5},{5,4},{6,7},{7,6},{8,9},{9,8},{10,11... | collective-permute-start | bytes 196616 | tf_op jit(solution)/shard_map/ppermute | solution.py:381
  125.9 6.4 %collective-permute-start.14 = (bf16[64,512]{1,0:T(8,128)(2,1)S(1)}, bf16[64,512]{1,0:T(8,128)(2,1)S(1)}, u32[]{:S(2)}, u32[]{:S(2)}) collective-permute-start(bf16[64,512]{1,0:T(8,128)(2,1)S(1)} %get-tuple-element.68), channel_id=1, source_target_pairs={{0,1},{1,0},{2,3},{3,2},{4,5},{5,4},{6,7},{7,6},{8,9},{9,8},{10,11... | collective-permute-start | bytes 196616 | tf_op jit(solution)/shard_map/ppermute | solution.py:381
  127.8 5.9 %collective-permute-start.15 = (bf16[64,512]{1,0:T(8,128)(2,1)S(1)}, bf16[64,512]{1,0:T(8,128)(2,1)S(1)}, u32[]{:S(2)}, u32[]{:S(2)}) collective-permute-start(bf16[64,512]{1,0:T(8,128)(2,1)S(1)} %reduce-precision_convert_fusion.1), channel_id=1, source_target_pairs={{0,3},{1,2},{2,1},{3,0},{4,7},{5,6},{6,5},{7,4},{8,11},{9,10},{10,... | collective-permute-start | bytes 196616 | tf_op jit(solution)/shard_map/ppermute | solution.py:381
  132.3 5.4 %collective-permute-start.16 = (bf16[64,512]{1,0:T(8,128)(2,1)S(1)}, bf16[64,512]{1,0:T(8,128)(2,1)S(1)}, u32[]{:S(2)}, u32[]{:S(2)}) collective-permute-start(bf16[64,512]{1,0:T(8,128)(2,1)S(1)} %reduce-precision_convert_fusion), channel_id=1, source_target_pairs={{0,3},{1,2},{2,1},{3,0},{4,7},{5,6},{6,5},{7,4},{8,11},{9,10},{10,... | collective-permute-start | bytes 196616 | tf_op jit(solution)/shard_map/ppermute | solution.py:381
